TPU v7x, 32 devices: a whole 2x2x4 slice. The times are simulated.
32 devices in a mesh: col: 8 (over z, y), row: 4 (over x, core).
Axes of the slice: x: 2, y: 2, z: 4, core: 2. Of those that a mesh axis runs over, the one named last changes fastest.
Arguments:
- latent: float32 [4096, 128], P('col'), may hold values from -6 to 6
- v_basis: float32 [8, 4, 16, 48, 256], P(None, 'row', 'col'), may hold values from -0.375 to 0.375
- u_basis: float32 [8, 4, 256, 768], P('col', 'row'), may hold values from -0.21875 to 0.21875
- ranks: int32 [8, 4, 16], P(None, 'row', 'col'), may hold values from 8 to 48, as said below
- slot_row: int32 [4, 8], P('row'), may hold values from 0 to 7, each once within a row
- wells: int32 [8, 4, 64], P('col', 'row'), may hold values from 0 to 255
- observed: float32 [8, 4, 64, 128], P('col', 'row'), may hold values from 0.3 to 2.5
Outputs:
- field: float32 [8, 4, 256, 128], P('col', 'row')
- gradient: float32 [4096, 128], P(('col', 'row'))
Inputs may be any that keep to these rules, and one draw needn't show every extreme that they name: Each row of slot_row is a permutation of 0 .. 7. For every tile row, class and pair of tile columns 2i, 2i + 1, the two ranks sum to at most 72; in every class some pair reaches 72. `wells`: cells may repeat within a slot.
All inputs are finite; a program needn't handle non-finite values.
Results may differ from a plain program's by a relative error of at most 0.0003.
Values sent between devices are 32-bit elements; how exact they have to be, the bound alone decides.
No kernel may reach another device: no remote copies, remote signals or barrier semaphores. Data moves between devices by JAX's collectives and lax.ppermute only.
A program may use at most 128 MiB of HBM per device.

v0:
```python
import jax
import jax.numpy as jnp
from jax import lax
from jax.sharding import PartitionSpec as P


def owner_pass(received, u_owned, onehot, observed_here):
    highest = lax.Precision.HIGHEST
    width = received.shape[-1]
    stacked = received.reshape(-1, width)
    field_block = jnp.dot(u_owned, stacked, precision=highest, preferred_element_type=jnp.float32)
    at_wells = jnp.dot(onehot, field_block, precision=highest, preferred_element_type=jnp.float32)
    expo_wells = jnp.exp(at_wells)
    weighted = (expo_wells - observed_here) * expo_wells / 0.25
    contract = (((0,), (0,)), ((), ()))
    well_rows = jnp.dot(onehot, u_owned, precision=highest, preferred_element_type=jnp.float32)
    adjoint = lax.dot_general(
        well_rows, weighted, contract, precision=highest, preferred_element_type=jnp.float32
    )
    return (field_block, adjoint.reshape(received.shape))


def on_device(latent, v_basis, u_basis, ranks, slot_row, wells, observed):
    highest = lax.Precision.HIGHEST
    class_rows = v_basis.shape[0]
    local_cols = v_basis.shape[2]
    rank_pad = v_basis.shape[3]
    tile_order = v_basis.shape[4]
    realizations = latent.shape[1]
    latent_tiles = latent.reshape(local_cols, tile_order, realizations)
    v_rows = v_basis[:, 0]
    live_mask = (lax.iota(jnp.int32, rank_pad)[None, None, :] < ranks[:, 0, :, None]).astype(
        jnp.float32
    )
    blocks = (
        jnp.einsum(
            "qjkb,jbs->qjks",
            v_rows,
            latent_tiles,
            precision=highest,
            preferred_element_type=jnp.float32,
        )
        * live_mask[:, :, :, None]
    )
    owner_order = slot_row[0]
    inverse = (
        jnp.zeros((class_rows,), jnp.int32)
        .at[owner_order]
        .set(jnp.arange(class_rows, dtype=jnp.int32))
    )
    sent_blocks = jnp.take(blocks, owner_order, axis=0)
    u_owned = u_basis[0, 0]
    onehot = (wells[0, 0][:, None] == lax.iota(jnp.int32, tile_order)[None, :]).astype(jnp.float32)
    observed_here = observed[0, 0]
    received = lax.all_to_all(sent_blocks, "col", split_axis=0, concat_axis=1, tiled=True)
    field_block, adjoint = owner_pass(received, u_owned, onehot, observed_here)
    returned = lax.all_to_all(adjoint, "col", split_axis=1, concat_axis=0, tiled=True)
    ordered = jnp.take(returned, inverse, axis=0) * live_mask[:, :, :, None]
    partial_value = jnp.einsum(
        "qjkb,qjks->jbs", v_rows, ordered, precision=highest, preferred_element_type=jnp.float32
    ).reshape(local_cols * tile_order, realizations)
    summed = lax.psum_scatter(partial_value, "row", scatter_dimension=0, tiled=True)
    out_rows = summed.shape[0]
    row_start = lax.axis_index("row") * out_rows
    gradient = lax.dynamic_slice_in_dim(latent, row_start, out_rows, 0) + summed
    return (field_block[None, None], gradient)


def solution(mesh):
    placed = (
        P("col", None),
        P(None, "row", "col", None, None),
        P("col", "row", None, None),
        P(None, "row", "col"),
        P("row", None),
        P("col", "row", None),
        P("col", "row", None, None),
    )
    return jax.shard_map(
        on_device,
        mesh=mesh,
        in_specs=placed,
        out_specs=(P("col", "row", None, None), P(("col", "row"), None)),
        check_vma=False,
    )
```

profile of v0, /device:TPU:0, one launch (start us, length us, event | category | flops | bytes accessed | tf_op | source)
XLA Modules:
  0.0 78.7 jit_solution(10162481754329847960)
XLA Ops:
  7.2 0.0 copy-start
  7.2 0.0 copy-start.5
  7.2 0.7 compare_select_fusion.1
  7.9 0.0 copy-done.5
  7.9 0.0 copy-start.4
  7.9 0.7 copy-done.4
  8.6 0.1 fusion.15
  8.7 0.0 copy-done
  8.7 1.8 %fusion = f32[8,2,48,128]{3,2,0,1:T(8,128)S(1)} fusion(f32[2,256,128,1]{2,1,3,0:T(8,128)} %bitcast.56, f32[8,2,48]{2,0,1:T(8,128)S(1)} %fusion.15, f32[8,1,2,48,256]{4,3,2,1,0:T(8,128)S(1)} %copy-done), kind=kOutput, calls=%fused_computation.4 | convolution fusion | flops 302088192 | bytes 1444864 | tf_op jit(solution)/shard_map/qjkb,jbs->qjks/dot_general | solution.py:36
  10.5 0.6 gather_fusion
  11.1 0.0 copy-start.1
  11.1 0.8 %broadcast_select_fusion = f32[8,2,48,128]{3,2,1,0:T(8,128)} fusion(f32[8,2,48,128]{3,2,1,0:T(8,128)S(1)} %gather_fusion, pred[8]{0:T(512)(128)(4,1)S(1)} %compare_and_fusion.1), kind=kLoop, calls=%fused_computation.16 | loop fusion | flops 98304 | bytes 786440 | tf_op jit(solution)/shard_map/jit(_take)/select_n | solution.py:51
  11.9 7.3 %all-to-all-start = ((f32[8,2,48,128]{3,2,1,0:T(8,128)}), f32[8,2,48,128]{3,2,1,0:T(8,128)S(1)}, u32[]{:S(2)}, u32[]{:S(2)}) async-start(f32[8,2,48,128]{3,2,1,0:T(8,128)} %broadcast_select_fusion), calls=%async_computation | async-start | bytes 786432 | tf_op jit(solution)/shard_map/all_to_all | solution.py:55
  19.2 0.0 copy-done.1
  19.2 0.6 copy-done.3
  19.9 0.4 fusion.1
  20.3 10.6 %all-to-all-done = f32[8,2,48,128]{3,2,1,0:T(8,128)S(1)} async-done(((f32[8,2,48,128]{3,2,1,0:T(8,128)}), f32[8,2,48,128]{3,2,1,0:T(8,128)S(1)}, u32[]{:S(2)}, u32[]{:S(2)}) %all-to-all-start) | async-done | bytes 393248 | tf_op jit(solution)/shard_map/all_to_all | solution.py:55
  30.9 0.8 %fusion.3 = f32[128,256]{1,0:T(8,128)S(1)} fusion(f32[768,128]{1,0:T(8,128)S(1)} %bitcast.53, f32[1,1,256,768]{3,2,1,0:T(8,128)S(1)} %copy-done.1), kind=kOutput, calls=%fused_computation.9 | convolution fusion | flops 301989888 | bytes 1310720 | tf_op jit(solution)/shard_map/dot_general | solution.py:11
  31.7 0.0 copy-done.2
  31.7 0.3 fusion.12
  32.0 1.5 %fusion.20 = f32[768,128]{1,0:T(8,128)} fusion(f32[64,768]{1,0:T(8,128)S(1)} %fusion.1, f32[64,128]{1,0:T(8,128)S(1)} %fusion.12), kind=kOutput, calls=%fused_computation.38 | convolution fusion | flops 75497472 | bytes 622592 | tf_op jit(solution)/shard_map/dot_general | solution.py:17
  33.5 3.6 %all-to-all-start.1 = ((f32[1,16,48,128]{3,2,0,1:T(8,128)}), f32[1,16,48,128]{3,2,0,1:T(8,128)S(1)}, u32[]{:S(2)}, u32[]{:S(2)}) async-start(f32[1,16,48,128]{3,2,0,1:T(8,128)} %bitcast.16), calls=%async_computation.1 | async-start | bytes 786432 | tf_op jit(solution)/shard_map/all_to_all | solution.py:57
  37.1 0.0 reduce-scatter.2.cloned.1.call-start
  37.2 0.6 scatter_custom_fusion
  37.8 10.9 %all-to-all-done.1 = f32[1,16,48,128]{3,2,0,1:T(8,128)S(1)} async-done(((f32[1,16,48,128]{3,2,0,1:T(8,128)}), f32[1,16,48,128]{3,2,0,1:T(8,128)S(1)}, u32[]{:S(2)}, u32[]{:S(2)}) %all-to-all-start.1) | async-done | bytes 393248 | tf_op jit(solution)/shard_map/all_to_all | solution.py:57
  48.7 0.6 gather_fusion.1
  49.3 1.0 %convolution_bitcast_fusion.1 = f32[2,256,128]{1,2,0:T(8,128)S(1)} fusion(f32[8,2,48,128]{3,2,1,0:T(8,128)S(1)} %gather_fusion.1, f32[8,2,48]{2,0,1:T(8,128)S(1)} %fusion.15, pred[8]{0:T(512)(128)(4,1)S(1)} %compare_and_fusion, f32[8,1,2,48,256]{4,3,2,1,0:T(8,128)S(1)} %copy-done), kind=kOutput, calls=%fused_computation.5 | convolution fusion | flops 302186496 | bytes 1444872 | tf_op jit(solution)/shard_map/qjkb,qjks->jbs/dot_general | solution.py:59
  50.3 0.8 %copy.21 = f32[2,256,128]{2,1,0:T(8,128)} copy(f32[2,256,128]{1,2,0:T(8,128)S(1)} %convolution_bitcast_fusion.1) | data formatting | bytes 524288 | tf_op jit(solution)/shard_map/qjkb,qjks->jbs/dot_general | solution.py:59
  51.1 0.0 reduce-scatter.2.cloned.1.call-update
  51.1 0.8 copy.22
  51.9 18.5 %reduce-scatter.2.cloned.1.call-done = f32[128,128]{1,0:T(8,128)} async-done(((f32[512,128]{1,0:T(8,128)}), f32[128,128]{1,0:T(8,128)}) %reduce-scatter.2.cloned.1.call-update) | async-done | bytes 65552 | tf_op jit(solution)/shard_map/reduce_scatter | solution.py:62
  70.4 1.5 %dynamic-slice_add_fusion = f32[128,128]{1,0:T(8,128)} fusion(f32[128,128]{1,0:T(8,128)} %reduce-scatter.2.cloned.1.call-done, f32[512,128]{1,0:T(8,128)} %param.9, s32[]{:T(128)S(6)} %select_n.20), kind=kLoop, calls=%fused_computation.20 | loop fusion | flops 16384 | bytes 196612 | tf_op jit(solution)/shard_map/add | solution.py:65
  (9 shorter events, 0.0 us)
Async XLA Ops:
  7.2 1.5 %copy-start = (f32[8,1,2,48,256]{4,3,2,1,0:T(8,128)S(1)}, f32[8,1,2,48,256]{4,3,2,1,0:T(8,128)}, u32[]{:S(2)}) copy-start(f32[8,1,2,48,256]{4,3,2,1,0:T(8,128)} %param.10) | copy-start | bytes 2359300
  7.2 0.7 copy-start.5
  7.9 0.7 copy-start.4
  11.1 8.1 %copy-start.1 = (f32[1,1,256,768]{3,2,1,0:T(8,128)S(1)}, f32[1,1,256,768]{3,2,1,0:T(8,128)}, u32[]{:S(2)}) copy-start(f32[1,1,256,768]{3,2,1,0:T(8,128)} %param.11) | copy-start | bytes 2359300
  11.9 19.0 %all-to-all-start = ((f32[8,2,48,128]{3,2,1,0:T(8,128)}), f32[8,2,48,128]{3,2,1,0:T(8,128)S(1)}, u32[]{:S(2)}, u32[]{:S(2)}) async-start(f32[8,2,48,128]{3,2,1,0:T(8,128)} %broadcast_select_fusion), calls=%async_computation | async-start | bytes 786432 | tf_op jit(solution)/shard_map/all_to_all | solution.py:55
  19.2 0.7 copy-start.3
  30.9 0.8 %copy-start.2 = (f32[1,1,64,128]{3,2,1,0:T(8,128)S(1)}, f32[1,1,64,128]{3,2,1,0:T(8,128)}, u32[]{:S(2)}) copy-start(f32[1,1,64,128]{3,2,1,0:T(8,128)} %param.15) | copy-start | bytes 98308
  33.5 15.2 %all-to-all-start.1 = ((f32[1,16,48,128]{3,2,0,1:T(8,128)}), f32[1,16,48,128]{3,2,0,1:T(8,128)S(1)}, u32[]{:S(2)}, u32[]{:S(2)}) async-start(f32[1,16,48,128]{3,2,0,1:T(8,128)} %bitcast.16), calls=%async_computation.1 | async-start | bytes 786432 | tf_op jit(solution)/shard_map/all_to_all | solution.py:57
  37.1 33.2 %reduce-scatter.2.cloned.1.call-start = ((), (), s32[]{:S(2)}) async-start(), calls=%async_computation.3 | async-start | bytes 327680 | tf_op jit(solution)/shard_map/reduce_scatter | solution.py:62
Sparse Core Ops, SparseCore 0:
  51.2 19.0 reduce-scatter.1
where the time goes:
time: 79.1 us; the launch traced here: 78.7 us
  waiting for transfers between devices  40 us (51%)
  between operations  14.2 us (18%)
  starting transfers between devices  10.9 us (14%)
  matrix products  5.77 us (7%)
  local copies, waits for them, and re-layouts  4.67 us (6%)
  other arithmetic  3.19 us (4%)
    reduce_scatter x1, waiting for transfers between devices, on_device(): lax.psum_scatter(partial_value, 'row', scatter_dimension=0, tiled=True)  18.5 us
    all_to_all x1, waiting for transfers between devices, on_device(): lax.all_to_all(adjoint, 'col', split_axis=1, concat_axis=0, tiled=True)  10.9 us
    all_to_all x1, waiting for transfers between devices, on_device(): lax.all_to_all(sent_blocks, 'col', split_axis=0, concat_axis=1, tiled=True)  10.6 us
    all_to_all x1, starting transfers between devices, on_device(): lax.all_to_all(sent_blocks, 'col', split_axis=0, concat_axis=1, tiled=True)  7.28 us
    all_to_all x1, starting transfers between devices, on_device(): lax.all_to_all(adjoint, 'col', split_axis=1, concat_axis=0, tiled=True)  3.62 us
    unnamed x13, local copies, waits for them, and re-layouts  2.1 us
    dot_general x1, matrix products, on_device(): jnp.einsum('qjkb,jbs->qjks', v_rows, latent_tiles, precision=highest, pre...  1.77 us
  transfers between devices with their start and end apart: 3, of which 3 were waited for; matrix products, arithmetic and copies ran while one was open for 2% of the time, Pallas kernels for 0%

commit v1 on v0

v1 whole, which is shorter than its diff:
```python
import functools

import jax
import jax.numpy as jnp
from jax import lax
from jax.experimental import pallas as pl
from jax.experimental.pallas import tpu as pltpu
from jax.sharding import PartitionSpec as P

F32 = jnp.float32
BF16 = jnp.bfloat16
VMEM = pl.BlockSpec(memory_space=pltpu.VMEM)
SMEM = pl.BlockSpec(memory_space=pltpu.SMEM)


def split(x):
    high = x.astype(BF16)
    low = (x - high.astype(F32)).astype(BF16)
    return high, low


def product(a, b, contract=(1, 0)):
    dims = (((contract[0],), (contract[1],)), ((), ()))
    a_high, a_low = split(a)
    b_high, b_low = split(b)
    both = lax.dot_general(a_high, jnp.concatenate([b_high, b_low], axis=1), dims, preferred_element_type=F32)
    width = b.shape[1]
    return both[:, :width] + both[:, width:] + lax.dot_general(a_low, b_high, dims, preferred_element_type=F32)


def repeat(count, body):
    if count == 1:
        body(0)
    else:
        pl.loop(0, count)(body)


def params(arrays):
    held = sum(a.size * a.dtype.itemsize for a in arrays)
    return pltpu.CompilerParams(vmem_limit_bytes=min(4 * held + (4 << 20), 56 << 20))


def blocks_kernel(group, order_ref, ranks_ref, latent_ref, v_ref, out_ref, held_ref):
    rows, local, rank_pad, cells = v_ref.shape
    width = latent_ref.shape[1]

    def some(g):
        for j in range(local):
            v_rows = v_ref[pl.ds(g * group, group), j].reshape(group * rank_pad, cells)
            made = product(v_rows, latent_ref[j * cells : (j + 1) * cells, :])
            held_ref[pl.ds(g * group, group), j] = made.reshape(group, rank_pad, width)

    repeat(rows // group, some)
    rank_index = lax.broadcasted_iota(jnp.int32, (rank_pad, width), 0)

    def place(g):
        for i in range(group):
            c = g * group + i
            q = order_ref[0, c]
            for j in range(local):
                live = rank_index < ranks_ref[q, j]
                out_ref[c, j * rank_pad : (j + 1) * rank_pad, :] = jnp.where(live, held_ref[q, j], 0.0)

    repeat(rows // group, place)


def owner_kernel(chunk, wells_ref, received_ref, u_ref, observed_ref, field_ref, adjoint_ref, at_wells_ref, rows_ref):
    depth = received_ref.shape[0]
    wells = observed_ref.shape[0]

    def first(k):
        part = product(u_ref[:, pl.ds(k * chunk, chunk)], received_ref[pl.ds(k * chunk, chunk), :])
        if depth == chunk:
            field_ref[...] = part
        else:

            @pl.when(k == 0)
            def _():
                field_ref[...] = part

            @pl.when(k > 0)
            def _():
                field_ref[...] += part

    repeat(depth // chunk, first)
    for w in range(wells):
        cell = wells_ref[0, 0, w]
        at_wells_ref[w : w + 1, :] = field_ref[pl.ds(cell, 1), :]
        rows_ref[w : w + 1, :] = u_ref[pl.ds(cell, 1), :]
    expo = jnp.exp(at_wells_ref[...])
    weighted = (expo - observed_ref[...]) * expo / 0.25

    def back(k):
        adjoint_ref[pl.ds(k * chunk, chunk), :] = product(rows_ref[:, pl.ds(k * chunk, chunk)], weighted, (0, 0))

    repeat(depth // chunk, back)


def gradient_kernel(
    group, axis, turn, order_ref, ranks_ref, returned_ref, v_ref, latent_ref, *refs
):
    out_refs, (ordered_ref, total_ref) = refs[:-2], refs[-2:]
    rows, local, rank_pad, cells = v_ref.shape
    width = latent_ref.shape[1]
    rank_index = lax.broadcasted_iota(jnp.int32, (rank_pad, width), 0)

    def place(g):
        for i in range(group):
            c = g * group + i
            q = order_ref[0, c]
            for j in range(local):
                live = rank_index < ranks_ref[q, j]
                ordered_ref[j, q] = jnp.where(live, returned_ref[c, j * rank_pad : (j + 1) * rank_pad, :], 0.0)

    repeat(rows // group, place)

    def some(g):
        for j in range(local):
            v_rows = v_ref[pl.ds(g * group, group), j].reshape(group * rank_pad, cells)
            part = product(v_rows, ordered_ref[j, pl.ds(g * group, group)].reshape(group * rank_pad, width), (0, 0))
            here = slice(j * cells, (j + 1) * cells)
            if rows == group:
                total_ref[here, :] = part
            else:

                @pl.when(g == 0)
                def _():
                    total_ref[here, :] = part

                @pl.when(g > 0)
                def _():
                    total_ref[here, :] += part

    repeat(rows // group, some)
    me = lax.axis_index(axis)
    size = out_refs[0].shape[0]
    for step, out_ref in enumerate(out_refs):
        there = pl.ds(pl.multiple_of(turn(me, step) * size, size), size)
        if step == 0:
            out_ref[...] = total_ref[there, :] + latent_ref[there, :]
        else:
            out_ref[...] = total_ref[there, :]


def on_device(n_row, latent, v_basis, u_basis, ranks, slot_row, wells, observed):
    rows, _, local, rank_pad, cells = v_basis.shape
    width = latent.shape[1]
    v_rows = v_basis[:, 0]
    ranks_here = ranks[:, 0]
    u_owned = u_basis[0, 0]
    observed_here = observed[0, 0]
    well_count = observed_here.shape[0]
    depth = u_owned.shape[1]
    group = 8 if rows % 8 == 0 else 1
    chunk = 768 if depth % 768 == 0 else depth
    sent = pl.pallas_call(
        functools.partial(blocks_kernel, group),
        out_shape=jax.ShapeDtypeStruct((rows, local * rank_pad, width), F32),
        in_specs=[SMEM, SMEM, VMEM, VMEM],
        out_specs=VMEM,
        scratch_shapes=[pltpu.VMEM((rows, local, rank_pad, width), F32)],
        compiler_params=params([latent, v_rows]),
        name="blocks",
    )(slot_row, ranks_here, latent, v_rows)
    received = lax.all_to_all(sent, "col", split_axis=0, concat_axis=0, tiled=True).reshape(depth, width)
    field, adjoint = pl.pallas_call(
        functools.partial(owner_kernel, chunk),
        out_shape=(jax.ShapeDtypeStruct((cells, width), F32), jax.ShapeDtypeStruct((depth, width), F32)),
        in_specs=[SMEM, VMEM, VMEM, VMEM],
        out_specs=(VMEM, VMEM),
        scratch_shapes=[pltpu.VMEM((well_count, width), F32), pltpu.VMEM((well_count, depth), F32)],
        compiler_params=params([received, u_owned, observed_here]),
        name="owner",
    )(wells, received, u_owned, observed_here)
    returned = lax.all_to_all(
        adjoint.reshape(rows, local * rank_pad, width), "col", split_axis=0, concat_axis=0, tiled=True
    )
    paired = n_row & (n_row - 1) == 0

    def turn(index, step):
        return index ^ step if paired else lax.rem(index + step, n_row)

    size = local * cells // n_row
    parts = pl.pallas_call(
        functools.partial(gradient_kernel, group, "row", turn),
        out_shape=[jax.ShapeDtypeStruct((size, width), F32)] * n_row,
        in_specs=[SMEM, SMEM, VMEM, VMEM, VMEM],
        out_specs=[VMEM] * n_row,
        scratch_shapes=[pltpu.VMEM((local, rows, rank_pad, width), F32), pltpu.VMEM((local * cells, width), F32)],
        compiler_params=params([returned, v_rows, latent]),
        name="gradient",
    )(slot_row, ranks_here, returned, v_rows, latent)
    gradient = parts[0]
    for step in range(1, n_row):
        pairs = [(i, i ^ step if paired else (i + step) % n_row) for i in range(n_row)]
        gradient = gradient + lax.ppermute(parts[step], "row", pairs)
    return field[None, None], gradient


def solution(mesh):
    placed = (
        P("col", None),
        P(None, "row", "col", None, None),
        P("col", "row", None, None),
        P(None, "row", "col"),
        P("row", None),
        P("col", "row", None),
        P("col", "row", None, None),
    )
    return jax.shard_map(
        functools.partial(on_device, mesh.shape["row"]),
        mesh=mesh,
        in_specs=placed,
        out_specs=(P("col", "row", None, None), P(("col", "row"), None)),
        check_vma=False,
    )
```

time: 79.1 us -> 49.5 us (0.63)
  waiting for transfers between devices: 40 us -> 3.75 us
  blocking collectives: 0 us -> 34.2 us
  between operations: 14.2 us -> 0.68 us
  starting transfers between devices: 10.9 us -> 1.93 us
  matrix products: 5.77 us -> 0 us
  Pallas kernels: 0 us -> 3.76 us
  other arithmetic: 3.19 us -> 0.64 us
    all_to_all x0 -> x2, blocking collectives: none -> 34.2 us  [the longest x1 19.2 us: on_device(): lax.all_to_all(sent, 'col', split_axis=0, concat_axis=0, tiled=True)]
    all_to_all x2 -> x0, waiting for transfers between devices: 21.5 us -> none  [the longest x1 10.9 us: on_device(): lax.all_to_all(adjoint, 'col', split_axis=1, concat_axis=0, tiled=True)]
    reduce_scatter x1 -> x0, waiting for transfers between devices: 18.5 us -> none  [on_device(): lax.psum_scatter(partial_value, 'row', scatter_dimension=0, tiled=True)]
    all_to_all x2 -> x0, starting transfers between devices: 10.9 us -> none  [the longest x1 7.28 us: on_device(): lax.all_to_all(sent_blocks, 'col', split_axis=0, concat_axis=1, tiled=True)]
    dot_general x6 -> x0, matrix products: 5.77 us -> none  [the longest x1 1.77 us: on_device(): jnp.einsum('qjkb,jbs->qjks', v_rows, latent_tiles, precision=highest, pre...]
    pallas_call x0 -> x3, Pallas kernels: none -> 3.76 us  [the longest x1 1.67 us: on_device(): pl.pallas_call(functools.partial(owner_kernel, chunk), out_shape=(jax.Sha...]
    ppermute x0 -> x3, waiting for transfers between devices: none -> 3.75 us  [on_device(): gradient = gradient + lax.ppermute(parts[step], 'row', pairs)]
    unnamed x13 -> x18, local copies, waits for them, and re-layouts: 2.1 us -> 4.08 us
  transfers between devices with their start and end apart: 3 -> 3, of which waited for: 3 -> 2; matrix products, arithmetic and copies ran while one was open for 2% -> 0% of each run, Pallas kernels for 0% -> 0%
where the time goes in v1:
time: 49.5 us; the launch traced here: 49.2 us
  blocking collectives  34.2 us (69%)
  local copies, waits for them, and re-layouts  4.16 us (8%)
  Pallas kernels  3.76 us (8%)
  waiting for transfers between devices  3.75 us (8%)
  starting transfers between devices  1.93 us (4%)
  between operations  0.68 us (1%)
  other arithmetic  0.64 us (1%)
    all_to_all x1, blocking collectives, on_device(): lax.all_to_all(sent, 'col', split_axis=0, concat_axis=0, tiled=True)  19.2 us
    all_to_all x1, blocking collectives, on_device(): lax.all_to_all(adjoint.reshape(rows, local * rank_pad, width), 'col', spl...  15.1 us
    unnamed x18, local copies, waits for them, and re-layouts  4.08 us
    ppermute x3, waiting for transfers between devices, on_device(): gradient = gradient + lax.ppermute(parts[step], 'row', pairs)  3.75 us
    ppermute x3, starting transfers between devices, on_device(): gradient = gradient + lax.ppermute(parts[step], 'row', pairs)  1.93 us
    pallas_call x1, Pallas kernels, on_device(): pl.pallas_call(functools.partial(owner_kernel, chunk), out_shape=(jax.Sha...  1.67 us
    pallas_call x1, Pallas kernels, on_device(): pl.pallas_call(functools.partial(gradient_kernel, group, 'row', turn), ou...  1.08 us
    pallas_call x1, Pallas kernels, on_device(): pl.pallas_call(functools.partial(blocks_kernel, group), out_shape=jax.Sha...  1.01 us
  transfers between devices with their start and end apart: 3, of which 2 were waited for; matrix products, arithmetic and copies ran while one was open for 0% of the time, Pallas kernels for 0%

profile of v1, /device:TPU:0, one launch (start us, length us, event | category | flops | bytes accessed | tf_op | source)
XLA Modules:
  0.0 49.2 jit_solution(15496311678409188687)
XLA Ops:
  0.6 0.0 copy-start.8
  0.6 0.7 %copy-done.8 = s32[8,1,2]{0,2,1:T(2,128)S(1)} copy-done((s32[8,1,2]{0,2,1:T(2,128)S(1)}, s32[8,1,2]{0,2,1:T(2,128)}, u32[]{:S(2)}) %copy-start.8) | copy-done | bytes 88
  1.3 0.1 copy.9.ranks_ref
  1.4 0.0 copy-start.6
  1.4 0.7 %copy-done.6 = s32[1,8]{1,0:T(1,128)S(1)} copy-done((s32[1,8]{1,0:T(1,128)S(1)}, s32[1,8]{1,0:T(1,128)}, u32[]{:S(2)}) %copy-start.6) | copy-done | bytes 56
  2.0 0.0 copy-start
  2.0 1.1 %copy-done = f32[8,1,2,48,256]{4,3,2,1,0:T(8,128)S(1)} copy-done((f32[8,1,2,48,256]{4,3,2,1,0:T(8,128)S(1)}, f32[8,1,2,48,256]{4,3,2,1,0:T(8,128)}, u32[]{:S(2)}) %copy-start) | copy-done | bytes 786456
  3.2 0.0 copy-start.2
  3.2 0.9 %copy-done.2 = f32[512,128]{1,0:T(8,128)S(1)} copy-done((f32[512,128]{1,0:T(8,128)S(1)}, f32[512,128]{1,0:T(8,128)}, u32[]{:S(2)}) %copy-start.2) | copy-done | bytes 262168
  4.1 0.0 copy-start.4
  4.1 1.0 %blocks.1 = f32[8,96,128]{2,1,0:T(8,128)S(1)} custom-call(s32[1,8]{1,0:T(1,128)S(1)} %copy-done.6, s32[8,2]{1,0:T(8,128)S(1)} %copy.9.ranks_ref, f32[512,128]{1,0:T(8,128)S(1)} %copy-done.2, f32[8,2,48,256]{3,2,1,0:T(8,128)S(1)} %bitcast.7), custom_call_target="tpu_custom_call" | custom-call | tf_op jit(solution)/shard_map/blocks/pallas_call | solution.py:156
  5.2 0.0 copy-start.5
  5.2 19.2 %all_to_all.10 = f32[8,96,128]{2,1,0:T(8,128)S(1)} all-to-all(f32[8,96,128]{2,1,0:T(8,128)S(1)} %blocks.1), channel_id=1, replica_groups=mesh['col'=8,'row'=4] {'col'}, dimensions={0} | all-to-all | bytes 786432 | tf_op jit(solution)/shard_map/all_to_all | solution.py:165
  24.3 0.0 copy-start.7
  24.3 0.0 copy-done.4
  24.3 0.0 copy-done.5
  24.3 0.6 %copy-done.7 = s32[1,1,64]{2,1,0:T(1,128)S(1)} copy-done((s32[1,1,64]{2,1,0:T(1,128)S(1)}, s32[1,1,64]{2,1,0:T(1,128)}, u32[]{:S(2)}) %copy-start.7) | copy-done | bytes 280
  25.0 0.0 copy-start.1
  25.0 1.7 %owner.1 = (f32[256,128]{1,0:T(8,128)}, f32[768,128]{1,0:T(8,128)S(1)}) custom-call(s32[1,1,64]{2,1,0:T(1,128)S(1)} %copy-done.7, f32[768,128]{1,0:T(8,128)S(1)} %bitcast.9, f32[256,768]{1,0:T(8,128)S(1)} %bitcast.10, f32[64,128]{1,0:T(8,128)S(1)} %bitcast.12), custom_call_target="tpu_custom_call" | custom-call | tf_op jit(solution)/shard_map/owner/pallas_call | solution.py:166
  26.7 0.0 copy-start.3
  26.7 15.1 %all_to_all.11.returned_ref = f32[8,96,128]{2,1,0:T(8,128)S(1)} all-to-all(f32[8,96,128]{2,1,0:T(8,128)S(1)} %bitcast.11), channel_id=1, replica_groups=mesh['col'=8,'row'=4] {'col'}, dimensions={0} | all-to-all | bytes 786432 | tf_op jit(solution)/shard_map/all_to_all | solution.py:175
  41.7 0.0 copy-done.1
  41.7 0.0 copy-done.3
  41.7 1.1 %gradient.1 = (f32[128,128]{1,0:T(8,128)S(1)}, f32[128,128]{1,0:T(8,128)S(1)}, f32[128,128]{1,0:T(8,128)S(1)}, f32[128,128]{1,0:T(8,128)S(1)}) custom-call(s32[1,8]{1,0:T(1,128)S(1)} %copy-done.6, s32[8,2]{1,0:T(8,128)S(1)} %copy.9.ranks_ref, f32[8,96,128]{2,1,0:T(8,128)S(1)} %all_to_all.11.returned_ref, f32[8,2,48,256]{3,2,1,0:T(8,128)S(1)} %bitcast.8, ...), custom_call_target="tpu_custom_call" | custom-call | tf_op jit(solution)/shard_map/gradient/pallas_call | solution.py:184
  42.8 0.1 collective-permute-start
  42.9 1.6 %collective-permute-start.1 = (f32[128,128]{1,0:T(8,128)S(1)}, f32[128,128]{1,0:T(8,128)S(1)}, u32[]{:S(2)}, u32[]{:S(2)}) collective-permute-start(f32[128,128]{1,0:T(8,128)S(1)} %get-tuple-element.12), channel_id=1, source_target_pairs={{0,2},{1,3},{2,0},{3,1},{4,6},{5,7},{6,4},{7,5},{8,10},{9,11},{10,... | collective-permute-start | bytes 196616 | tf_op jit(solution)/shard_map/ppermute | solution.py:196
  44.5 0.3 collective-permute-start.2
  44.8 0.0 collective-permute-done
  44.8 2.6 %collective-permute-done.1 = f32[128,128]{1,0:T(8,128)S(1)} collective-permute-done((f32[128,128]{1,0:T(8,128)S(1)}, f32[128,128]{1,0:T(8,128)S(1)}, u32[]{:S(2)}, u32[]{:S(2)}) %collective-permute-start.1) | collective-permute-done | bytes 65568 | tf_op jit(solution)/shard_map/ppermute | solution.py:196
  47.4 1.1 %collective-permute-done.2 = f32[128,128]{1,0:T(8,128)S(1)} collective-permute-done((f32[128,128]{1,0:T(8,128)S(1)}, f32[128,128]{1,0:T(8,128)S(1)}, u32[]{:S(2)}, u32[]{:S(2)}) %collective-permute-start.2) | collective-permute-done | bytes 65568 | tf_op jit(solution)/shard_map/ppermute | solution.py:196
  48.5 0.6 %add_add_fusion = f32[128,128]{1,0:T(8,128)} fusion(f32[128,128]{1,0:T(8,128)S(1)} %collective-permute-done.2, f32[128,128]{1,0:T(8,128)S(1)} %collective-permute-done.1, f32[128,128]{1,0:T(8,128)S(1)} %get-tuple-element.10, f32[128,128]{1,0:T(8,128)S(1)} %collective-permute-done), kind=kLoop, calls=%fused_computation | loop fusion | flops 49152 | bytes 327680 | tf_op jit(solution)/shard_map/add | solution.py:196
Async XLA Ops:
  0.6 0.7 %copy-start.8 = (s32[8,1,2]{0,2,1:T(2,128)S(1)}, s32[8,1,2]{0,2,1:T(2,128)}, u32[]{:S(2)}) copy-start(s32[8,1,2]{0,2,1:T(2,128)} %param.10) | copy-start | bytes 196
  1.4 0.7 %copy-start.6 = (s32[1,8]{1,0:T(1,128)S(1)}, s32[1,8]{1,0:T(1,128)}, u32[]{:S(2)}) copy-start(s32[1,8]{1,0:T(1,128)} %order_ref.3) | copy-start | bytes 100
  2.0 1.1 %copy-start = (f32[8,1,2,48,256]{4,3,2,1,0:T(8,128)S(1)}, f32[8,1,2,48,256]{4,3,2,1,0:T(8,128)}, u32[]{:S(2)}) copy-start(f32[8,1,2,48,256]{4,3,2,1,0:T(8,128)} %param.8) | copy-start | bytes 2359300
  3.2 0.9 %copy-start.2 = (f32[512,128]{1,0:T(8,128)S(1)}, f32[512,128]{1,0:T(8,128)}, u32[]{:S(2)}) copy-start(f32[512,128]{1,0:T(8,128)} %latent_ref.3) | copy-start | bytes 786436
  4.1 20.2 %copy-start.4 = (f32[1,1,256,768]{3,2,1,0:T(8,128)S(1)}, f32[1,1,256,768]{3,2,1,0:T(8,128)}, u32[]{:S(2)}) copy-start(f32[1,1,256,768]{3,2,1,0:T(8,128)} %param.9) | copy-start | bytes 2359300
  5.2 19.2 %copy-start.5 = (f32[1,1,64,128]{3,2,1,0:T(8,128)S(1)}, f32[1,1,64,128]{3,2,1,0:T(8,128)}, u32[]{:S(2)}) copy-start(f32[1,1,64,128]{3,2,1,0:T(8,128)} %param.13) | copy-start | bytes 98308
  24.3 0.7 %copy-start.7 = (s32[1,1,64]{2,1,0:T(1,128)S(1)}, s32[1,1,64]{2,1,0:T(1,128)}, u32[]{:S(2)}) copy-start(s32[1,1,64]{2,1,0:T(1,128)} %wells_ref.1) | copy-start | bytes 772
  25.0 16.7 %copy-start.1 = (f32[8,1,2,48,256]{4,3,2,1,0:T(8,128)S(1)}, f32[8,1,2,48,256]{4,3,2,1,0:T(8,128)}, u32[]{:S(2)}) copy-start(f32[8,1,2,48,256]{4,3,2,1,0:T(8,128)} %param.8) | copy-start | bytes 2359300
  26.7 15.1 %copy-start.3 = (f32[512,128]{1,0:T(8,128)S(1)}, f32[512,128]{1,0:T(8,128)}, u32[]{:S(2)}) copy-start(f32[512,128]{1,0:T(8,128)} %latent_ref.3) | copy-start | bytes 786436
  42.8 1.9 %collective-permute-start = (f32[128,128]{1,0:T(8,128)S(1)}, f32[128,128]{1,0:T(8,128)S(1)}, u32[]{:S(2)}, u32[]{:S(2)}) collective-permute-start(f32[128,128]{1,0:T(8,128)S(1)} %get-tuple-element.11), channel_id=1, source_target_pairs={{0,1},{1,0},{2,3},{3,2},{4,5},{5,4},{6,7},{7,6},{8,9},{9,8},{10,11... | collective-permute-start | bytes 196616 | tf_op jit(solution)/shard_map/ppermute | solution.py:196
  42.9 4.5 %collective-permute-start.1 = (f32[128,128]{1,0:T(8,128)S(1)}, f32[128,128]{1,0:T(8,128)S(1)}, u32[]{:S(2)}, u32[]{:S(2)}) collective-permute-start(f32[128,128]{1,0:T(8,128)S(1)} %get-tuple-element.12), channel_id=1, source_target_pairs={{0,2},{1,3},{2,0},{3,1},{4,6},{5,7},{6,4},{7,5},{8,10},{9,11},{10,... | collective-permute-start | bytes 196616 | tf_op jit(solution)/shard_map/ppermute | solution.py:196
  44.5 4.0 %collective-permute-start.2 = (f32[128,128]{1,0:T(8,128)S(1)}, f32[128,128]{1,0:T(8,128)S(1)}, u32[]{:S(2)}, u32[]{:S(2)}) collective-permute-start(f32[128,128]{1,0:T(8,128)S(1)} %get-tuple-element.13), channel_id=1, source_target_pairs={{0,3},{1,2},{2,1},{3,0},{4,7},{5,6},{6,5},{7,4},{8,11},{9,10},{10,... | collective-permute-start | bytes 196616 | tf_op jit(solution)/shard_map/ppermute | solution.py:196

commit v2 on v1

--- a/solution.py
+++ b/solution.py
@@ -11,6 +11,7 @@
 BF16 = jnp.bfloat16
 VMEM = pl.BlockSpec(memory_space=pltpu.VMEM)
 SMEM = pl.BlockSpec(memory_space=pltpu.SMEM)
+HBM = pl.BlockSpec(memory_space=pltpu.HBM)
 
 
 def split(x):
@@ -40,17 +41,45 @@
     return pltpu.CompilerParams(vmem_limit_bytes=min(4 * held + (4 << 20), 56 << 20))
 
 
-def blocks_kernel(group, order_ref, ranks_ref, latent_ref, v_ref, out_ref, held_ref):
-    rows, local, rank_pad, cells = v_ref.shape
+def stay(x):
+    return pltpu.with_memory_space_constraint(x, pltpu.HBM)
+
+
+def blocks_kernel(
+    group, order_hbm, ranks_hbm, latent_hbm, v_hbm, out_ref, held_ref, order_ref, ranks_ref, latent_ref, v_ref, sems
+):
+    local, rows, rank_pad, cells = v_ref.shape
     width = latent_ref.shape[1]
-
-    def some(g):
-        for j in range(local):
-            v_rows = v_ref[pl.ds(g * group, group), j].reshape(group * rank_pad, cells)
+    small = [
+        pltpu.make_async_copy(order_hbm, order_ref, sems.at[2 * local]),
+        pltpu.make_async_copy(ranks_hbm, ranks_ref, sems.at[2 * local + 1]),
+    ]
+    tiles = []
+    for j in range(local):
+        here = pl.ds(j * cells, cells)
+        tiles.append(
+            (
+                pltpu.make_async_copy(v_hbm.at[:, j], v_ref.at[j], sems.at[2 * j]),
+                pltpu.make_async_copy(latent_hbm.at[here], latent_ref.at[here], sems.at[2 * j + 1]),
+            )
+        )
+    for copies in tiles:
+        for copy in copies:
+            copy.start()
+    for copy in small:
+        copy.start()
+    for j in range(local):
+        for copy in tiles[j]:
+            copy.wait()
+
+        def some(g):
+            v_rows = v_ref[j, pl.ds(g * group, group)].reshape(group * rank_pad, cells)
             made = product(v_rows, latent_ref[j * cells : (j + 1) * cells, :])
-            held_ref[pl.ds(g * group, group), j] = made.reshape(group, rank_pad, width)
-
-    repeat(rows // group, some)
+            held_ref[j, pl.ds(g * group, group)] = made.reshape(group, rank_pad, width)
+
+        repeat(rows // group, some)
+    for copy in small:
+        copy.wait()
     rank_index = lax.broadcasted_iota(jnp.int32, (rank_pad, width), 0)
 
     def place(g):
@@ -58,14 +87,18 @@
             c = g * group + i
             q = order_ref[0, c]
             for j in range(local):
-                live = rank_index < ranks_ref[q, j]
-                out_ref[c, j * rank_pad : (j + 1) * rank_pad, :] = jnp.where(live, held_ref[q, j], 0.0)
+                live = rank_index < ranks_ref[j, q]
+                out_ref[c, j * rank_pad : (j + 1) * rank_pad, :] = jnp.where(live, held_ref[j, q], 0.0)
 
     repeat(rows // group, place)
 
 
-def owner_kernel(chunk, wells_ref, received_ref, u_ref, observed_ref, field_ref, adjoint_ref, at_wells_ref, rows_ref):
+def owner_kernel(
+    chunk, wells_hbm, received_ref, u_ref, observed_ref, field_ref, adjoint_ref, at_wells_ref, rows_ref, wells_ref, sem
+):
     depth = received_ref.shape[0]
+    copy = pltpu.make_async_copy(wells_hbm, wells_ref, sem)
+    copy.start()
     wells = observed_ref.shape[0]
 
     def first(k):
@@ -83,8 +116,9 @@
                 field_ref[...] += part
 
     repeat(depth // chunk, first)
+    copy.wait()
     for w in range(wells):
-        cell = wells_ref[0, 0, w]
+        cell = wells_ref[0, w]
         at_wells_ref[w : w + 1, :] = field_ref[pl.ds(cell, 1), :]
         rows_ref[w : w + 1, :] = u_ref[pl.ds(cell, 1), :]
     expo = jnp.exp(at_wells_ref[...])
@@ -109,7 +143,7 @@
             c = g * group + i
             q = order_ref[0, c]
             for j in range(local):
-                live = rank_index < ranks_ref[q, j]
+                live = rank_index < ranks_ref[j, q]
                 ordered_ref[j, q] = jnp.where(live, returned_ref[c, j * rank_pad : (j + 1) * rank_pad, :], 0.0)
 
     repeat(rows // group, place)
@@ -146,7 +180,7 @@
     rows, _, local, rank_pad, cells = v_basis.shape
     width = latent.shape[1]
     v_rows = v_basis[:, 0]
-    ranks_here = ranks[:, 0]
+    ranks_here = ranks[:, 0].T
     u_owned = u_basis[0, 0]
     observed_here = observed[0, 0]
     well_count = observed_here.shape[0]
@@ -156,22 +190,34 @@
     sent = pl.pallas_call(
         functools.partial(blocks_kernel, group),
         out_shape=jax.ShapeDtypeStruct((rows, local * rank_pad, width), F32),
-        in_specs=[SMEM, SMEM, VMEM, VMEM],
+        in_specs=[HBM, HBM, HBM, HBM],
         out_specs=VMEM,
-        scratch_shapes=[pltpu.VMEM((rows, local, rank_pad, width), F32)],
+        scratch_shapes=[
+            pltpu.VMEM((local, rows, rank_pad, width), F32),
+            pltpu.SMEM(slot_row.shape, jnp.int32),
+            pltpu.SMEM(ranks_here.shape, jnp.int32),
+            pltpu.VMEM(latent.shape, F32),
+            pltpu.VMEM((local, rows, rank_pad, cells), F32),
+            pltpu.SemaphoreType.DMA((2 * local + 2,)),
+        ],
         compiler_params=params([latent, v_rows]),
         name="blocks",
-    )(slot_row, ranks_here, latent, v_rows)
+    )(stay(slot_row), stay(ranks_here), stay(latent), stay(v_rows))
     received = lax.all_to_all(sent, "col", split_axis=0, concat_axis=0, tiled=True).reshape(depth, width)
     field, adjoint = pl.pallas_call(
         functools.partial(owner_kernel, chunk),
         out_shape=(jax.ShapeDtypeStruct((cells, width), F32), jax.ShapeDtypeStruct((depth, width), F32)),
-        in_specs=[SMEM, VMEM, VMEM, VMEM],
+        in_specs=[HBM, VMEM, VMEM, VMEM],
         out_specs=(VMEM, VMEM),
-        scratch_shapes=[pltpu.VMEM((well_count, width), F32), pltpu.VMEM((well_count, depth), F32)],
+        scratch_shapes=[
+            pltpu.VMEM((well_count, width), F32),
+            pltpu.VMEM((well_count, depth), F32),
+            pltpu.SMEM((1, well_count), jnp.int32),
+            pltpu.SemaphoreType.DMA,
+        ],
         compiler_params=params([received, u_owned, observed_here]),
         name="owner",
-    )(wells, received, u_owned, observed_here)
+    )(stay(wells[0]), received, u_owned, observed_here)
     returned = lax.all_to_all(
         adjoint.reshape(rows, local * rank_pad, width), "col", split_axis=0, concat_axis=0, tiled=True
     )

time: 49.5 us -> 46.1 us (0.931)
  local copies, waits for them, and re-layouts: 4.16 us -> 0.03 us
  Pallas kernels: 3.76 us -> 4.46 us
    unnamed x18 -> x12, local copies, waits for them, and re-layouts: 4.08 us -> 0.03 us
    pallas_call x1, Pallas kernels: 1.01 us -> 1.76 us  [on_device(): pl.pallas_call(functools.partial(blocks_kernel, group), out_shape=jax.Sha...]
where the time goes in v2:
time: 46.1 us; the launch traced here: 45.8 us
  blocking collectives  34.2 us (74%)
  Pallas kernels  4.46 us (10%)
  waiting for transfers between devices  3.74 us (8%)
  starting transfers between devices  1.93 us (4%)
  between operations  0.72 us (2%)
  other arithmetic  0.64 us (1%)
    all_to_all x1, blocking collectives, on_device(): lax.all_to_all(sent, 'col', split_axis=0, concat_axis=0, tiled=True)  19.2 us
    all_to_all x1, blocking collectives, on_device(): lax.all_to_all(adjoint.reshape(rows, local * rank_pad, width), 'col', spl...  15.1 us
    ppermute x3, waiting for transfers between devices, on_device(): gradient = gradient + lax.ppermute(parts[step], 'row', pairs)  3.74 us
    ppermute x3, starting transfers between devices, on_device(): gradient = gradient + lax.ppermute(parts[step], 'row', pairs)  1.93 us
    pallas_call x1, Pallas kernels, on_device(): pl.pallas_call(functools.partial(blocks_kernel, group), out_shape=jax.Sha...  1.76 us
    pallas_call x1, Pallas kernels, on_device(): pl.pallas_call(functools.partial(owner_kernel, chunk), out_shape=(jax.Sha...  1.67 us
    pallas_call x1, Pallas kernels, on_device(): pl.pallas_call(functools.partial(gradient_kernel, group, 'row', turn), ou...  1.03 us
  transfers between devices with their start and end apart: 3, of which 2 were waited for; matrix products, arithmetic and copies ran while one was open for 0% of the time, Pallas kernels for 0%

profile of v2, /device:TPU:0, one launch (start us, length us, event | category | flops | bytes accessed | tf_op | source)
XLA Modules:
  0.0 45.8 jit_solution(2695515688953844191)
XLA Ops:
  0.6 0.0 copy-start.2
  0.6 1.8 %blocks.1 = f32[8,96,128]{2,1,0:T(8,128)S(1)} custom-call(s32[1,8]{1,0:T(1,128)} %order_ref.1, s32[2,8]{1,0:T(2,128)} %bitcast.16, f32[512,128]{1,0:T(8,128)} %latent_ref.1, f32[8,2,48,256]{3,2,1,0:T(8,128)} %bitcast.10), custom_call_target="tpu_custom_call" | custom-call | tf_op jit(solution)/shard_map/blocks/pallas_call | solution.py:190
  2.4 0.0 copy-start.3
  2.4 19.2 %all_to_all.10 = f32[8,96,128]{2,1,0:T(8,128)S(1)} all-to-all(f32[8,96,128]{2,1,0:T(8,128)S(1)} %blocks.1), channel_id=1, replica_groups=mesh['col'=8,'row'=4] {'col'}, dimensions={0} | all-to-all | bytes 786432 | tf_op jit(solution)/shard_map/all_to_all | solution.py:206
  21.6 0.0 copy-done.2
  21.6 0.0 copy-done.3
  21.6 0.0 copy-start
  21.6 1.7 %owner.1 = (f32[256,128]{1,0:T(8,128)}, f32[768,128]{1,0:T(8,128)S(1)}) custom-call(s32[1,64]{1,0:T(1,128)} %bitcast.18, f32[768,128]{1,0:T(8,128)S(1)} %bitcast.12, f32[256,768]{1,0:T(8,128)S(1)} %bitcast.13, f32[64,128]{1,0:T(8,128)S(1)} %bitcast.15), custom_call_target="tpu_custom_call" | custom-call | tf_op jit(solution)/shard_map/owner/pallas_call | solution.py:207
  23.3 0.0 copy-start.1
  23.3 0.0 copy-start.4
  23.3 0.0 copy-start.5
  23.3 15.1 %all_to_all.11.returned_ref = f32[8,96,128]{2,1,0:T(8,128)S(1)} all-to-all(f32[8,96,128]{2,1,0:T(8,128)S(1)} %bitcast.14), channel_id=1, replica_groups=mesh['col'=8,'row'=4] {'col'}, dimensions={0} | all-to-all | bytes 786432 | tf_op jit(solution)/shard_map/all_to_all | solution.py:221
  38.4 0.0 copy-done
  38.4 0.0 copy-done.1
  38.4 0.0 copy-done.4
  38.4 0.0 copy-done.5
  38.4 1.0 %gradient.1 = (f32[128,128]{1,0:T(8,128)S(1)}, f32[128,128]{1,0:T(8,128)S(1)}, f32[128,128]{1,0:T(8,128)S(1)}, f32[128,128]{1,0:T(8,128)S(1)}) custom-call(s32[1,8]{1,0:T(1,128)S(1)} %copy-done.5, s32[2,8]{1,0:T(2,128)S(1)} %bitcast.17, f32[8,96,128]{2,1,0:T(8,128)S(1)} %all_to_all.11.returned_ref, f32[8,2,48,256]{3,2,1,0:T(8,128)S(1)} %bitcast.11, ...), custom_call_target="tpu_custom_call" | custom-call | tf_op jit(solution)/shard_map/gradient/pallas_call | solution.py:230
  39.4 0.1 collective-permute-start
  39.5 1.6 %collective-permute-start.1 = (f32[128,128]{1,0:T(8,128)S(1)}, f32[128,128]{1,0:T(8,128)S(1)}, u32[]{:S(2)}, u32[]{:S(2)}) collective-permute-start(f32[128,128]{1,0:T(8,128)S(1)} %get-tuple-element.12), channel_id=1, source_target_pairs={{0,2},{1,3},{2,0},{3,1},{4,6},{5,7},{6,4},{7,5},{8,10},{9,11},{10,... | collective-permute-start | bytes 196616 | tf_op jit(solution)/shard_map/ppermute | solution.py:242
  41.1 0.3 collective-permute-start.2
  41.4 0.0 collective-permute-done
  41.4 2.6 %collective-permute-done.1 = f32[128,128]{1,0:T(8,128)S(1)} collective-permute-done((f32[128,128]{1,0:T(8,128)S(1)}, f32[128,128]{1,0:T(8,128)S(1)}, u32[]{:S(2)}, u32[]{:S(2)}) %collective-permute-start.1) | collective-permute-done | bytes 65568 | tf_op jit(solution)/shard_map/ppermute | solution.py:242
  44.0 1.1 %collective-permute-done.2 = f32[128,128]{1,0:T(8,128)S(1)} collective-permute-done((f32[128,128]{1,0:T(8,128)S(1)}, f32[128,128]{1,0:T(8,128)S(1)}, u32[]{:S(2)}, u32[]{:S(2)}) %collective-permute-start.2) | collective-permute-done | bytes 65568 | tf_op jit(solution)/shard_map/ppermute | solution.py:242
  45.1 0.6 %add_add_fusion = f32[128,128]{1,0:T(8,128)} fusion(f32[128,128]{1,0:T(8,128)S(1)} %collective-permute-done.2, f32[128,128]{1,0:T(8,128)S(1)} %collective-permute-done.1, f32[128,128]{1,0:T(8,128)S(1)} %get-tuple-element.10, f32[128,128]{1,0:T(8,128)S(1)} %collective-permute-done), kind=kLoop, calls=%fused_computation | loop fusion | flops 49152 | bytes 327680 | tf_op jit(solution)/shard_map/add | solution.py:242
Async XLA Ops:
  0.6 21.0 %copy-start.2 = (f32[1,1,256,768]{3,2,1,0:T(8,128)S(1)}, f32[1,1,256,768]{3,2,1,0:T(8,128)}, u32[]{:S(2)}) copy-start(f32[1,1,256,768]{3,2,1,0:T(8,128)} %param.9) | copy-start | bytes 2359300
  2.4 19.2 %copy-start.3 = (f32[1,1,64,128]{3,2,1,0:T(8,128)S(1)}, f32[1,1,64,128]{3,2,1,0:T(8,128)}, u32[]{:S(2)}) copy-start(f32[1,1,64,128]{3,2,1,0:T(8,128)} %param.13) | copy-start | bytes 98308
  21.6 16.8 %copy-start = (f32[8,1,2,48,256]{4,3,2,1,0:T(8,128)S(1)}, f32[8,1,2,48,256]{4,3,2,1,0:T(8,128)}, u32[]{:S(2)}) copy-start(f32[8,1,2,48,256]{4,3,2,1,0:T(8,128)} %param.8) | copy-start | bytes 2359300
  23.3 15.1 %copy-start.1 = (f32[512,128]{1,0:T(8,128)S(1)}, f32[512,128]{1,0:T(8,128)}, u32[]{:S(2)}) copy-start(f32[512,128]{1,0:T(8,128)} %latent_ref.1) | copy-start | bytes 786436
  23.3 15.1 %copy-start.4 = (s32[8,1,2]{0,2,1:T(2,128)S(1)}, s32[8,1,2]{0,2,1:T(2,128)}, u32[]{:S(2)}) copy-start(s32[8,1,2]{0,2,1:T(2,128)} %param.10) | copy-start | bytes 196
  23.3 15.1 %copy-start.5 = (s32[1,8]{1,0:T(1,128)S(1)}, s32[1,8]{1,0:T(1,128)}, u32[]{:S(2)}) copy-start(s32[1,8]{1,0:T(1,128)} %order_ref.1) | copy-start | bytes 100
  39.4 1.9 %collective-permute-start = (f32[128,128]{1,0:T(8,128)S(1)}, f32[128,128]{1,0:T(8,128)S(1)}, u32[]{:S(2)}, u32[]{:S(2)}) collective-permute-start(f32[128,128]{1,0:T(8,128)S(1)} %get-tuple-element.11), channel_id=1, source_target_pairs={{0,1},{1,0},{2,3},{3,2},{4,5},{5,4},{6,7},{7,6},{8,9},{9,8},{10,11... | collective-permute-start | bytes 196616 | tf_op jit(solution)/shard_map/ppermute | solution.py:242
  39.5 4.5 %collective-permute-start.1 = (f32[128,128]{1,0:T(8,128)S(1)}, f32[128,128]{1,0:T(8,128)S(1)}, u32[]{:S(2)}, u32[]{:S(2)}) collective-permute-start(f32[128,128]{1,0:T(8,128)S(1)} %get-tuple-element.12), channel_id=1, source_target_pairs={{0,2},{1,3},{2,0},{3,1},{4,6},{5,7},{6,4},{7,5},{8,10},{9,11},{10,... | collective-permute-start | bytes 196616 | tf_op jit(solution)/shard_map/ppermute | solution.py:242
  41.1 4.0 %collective-permute-start.2 = (f32[128,128]{1,0:T(8,128)S(1)}, f32[128,128]{1,0:T(8,128)S(1)}, u32[]{:S(2)}, u32[]{:S(2)}) collective-permute-start(f32[128,128]{1,0:T(8,128)S(1)} %get-tuple-element.13), channel_id=1, source_target_pairs={{0,3},{1,2},{2,1},{3,0},{4,7},{5,6},{6,5},{7,4},{8,11},{9,10},{10,... | collective-permute-start | bytes 196616 | tf_op jit(solution)/shard_map/ppermute | solution.py:242

commit v3 on v2

--- a/solution.py
+++ b/solution.py
@@ -12,6 +12,7 @@
 VMEM = pl.BlockSpec(memory_space=pltpu.VMEM)
 SMEM = pl.BlockSpec(memory_space=pltpu.SMEM)
 HBM = pl.BlockSpec(memory_space=pltpu.HBM)
+MARK = 8
 
 
 def split(x):
@@ -36,9 +37,25 @@
         pl.loop(0, count)(body)
 
 
+def each(count, body):
+    if count <= 16:
+        for i in range(count):
+            body(i)
+    else:
+        pl.loop(0, count)(body)
+
+
 def params(arrays):
     held = sum(a.size * a.dtype.itemsize for a in arrays)
     return pltpu.CompilerParams(vmem_limit_bytes=min(4 * held + (4 << 20), 56 << 20))
+
+
+def packed_rows(rank_pad):
+    return rank_pad + rank_pad // 2
+
+
+def lengthen(x, size):
+    return jnp.concatenate([x, jnp.zeros((size - x.shape[0], x.shape[1]), x.dtype)], axis=0)
 
 
 def stay(x):
@@ -81,28 +98,76 @@
     for copy in small:
         copy.wait()
     rank_index = lax.broadcasted_iota(jnp.int32, (rank_pad, width), 0)
+    size = packed_rows(rank_pad)
 
     def place(g):
         for i in range(group):
             c = g * group + i
             q = order_ref[0, c]
-            for j in range(local):
-                live = rank_index < ranks_ref[j, q]
-                out_ref[c, j * rank_pad : (j + 1) * rank_pad, :] = jnp.where(live, held_ref[j, q], 0.0)
+            for pair in range(local // 2):
+                left, right = 2 * pair, 2 * pair + 1
+                cut = ranks_ref[left, q]
+                first = jnp.where(rank_index < cut, held_ref[left, q], 0.0)
+                second = jnp.where(rank_index < ranks_ref[right, q], held_ref[right, q], 0.0)
+                base = pair * (size + MARK)
+                out_ref[c, base : base + size, :] = lengthen(first, size) + pltpu.roll(lengthen(second, size), cut, 0)
+                out_ref[c, base + size : base + size + MARK, :] = jnp.full((MARK, width), cut.astype(F32))
 
     repeat(rows // group, place)
 
 
 def owner_kernel(
-    chunk, wells_hbm, received_ref, u_ref, observed_ref, field_ref, adjoint_ref, at_wells_ref, rows_ref, wells_ref, sem
+    chunk,
+    rank_pad,
+    wells_hbm,
+    received_ref,
+    u_ref,
+    observed_ref,
+    field_ref,
+    packed_ref,
+    stacked_ref,
+    at_wells_ref,
+    rows_ref,
+    wells_ref,
+    sem,
 ):
-    depth = received_ref.shape[0]
+    sources = received_ref.shape[0]
+    depth, width = stacked_ref.shape
+    wells = observed_ref.shape[0]
+    size = packed_rows(rank_pad)
+    pairs = received_ref.shape[1] // (size + MARK)
     copy = pltpu.make_async_copy(wells_hbm, wells_ref, sem)
     copy.start()
-    wells = observed_ref.shape[0]
+    rank_index = lax.broadcasted_iota(jnp.int32, (rank_pad, width), 0)
+    packed_index = lax.broadcasted_iota(jnp.int32, (size, width), 0)
+
+    def first_rank(c, pair):
+        at = pair * (size + MARK) + size
+        return received_ref[c, at : at + 1, :][0, 0].astype(jnp.int32)
+
+    def unpack(c):
+        for pair in range(pairs):
+            cut = first_rank(c, pair)
+            both = received_ref[c, pair * (size + MARK) : pair * (size + MARK) + size, :]
+            left = pl.multiple_of((c * pairs + pair) * 2 * rank_pad, 8)
+            stacked_ref[pl.ds(left, rank_pad), :] = jnp.where(rank_index < cut, both[:rank_pad], 0.0)
+            second = pltpu.roll(both, size - cut, 0)[:rank_pad]
+            right = pl.multiple_of(left + rank_pad, 8)
+            stacked_ref[pl.ds(right, rank_pad), :] = jnp.where(rank_index < size - cut, second, 0.0)
+
+    def pack(c):
+        for pair in range(pairs):
+            cut = first_rank(c, pair)
+            left = pl.multiple_of((c * pairs + pair) * 2 * rank_pad, 8)
+            first = lengthen(stacked_ref[pl.ds(left, rank_pad), :], size)
+            right = pl.multiple_of(left + rank_pad, 8)
+            second = pltpu.roll(lengthen(stacked_ref[pl.ds(right, rank_pad), :], size), cut, 0)
+            packed_ref[c, pair * size : (pair + 1) * size, :] = jnp.where(packed_index < cut, first, second)
+
+    each(sources, unpack)
 
     def first(k):
-        part = product(u_ref[:, pl.ds(k * chunk, chunk)], received_ref[pl.ds(k * chunk, chunk), :])
+        part = product(u_ref[:, pl.ds(k * chunk, chunk)], stacked_ref[pl.ds(k * chunk, chunk), :])
         if depth == chunk:
             field_ref[...] = part
         else:
@@ -125,9 +190,10 @@
     weighted = (expo - observed_ref[...]) * expo / 0.25
 
     def back(k):
-        adjoint_ref[pl.ds(k * chunk, chunk), :] = product(rows_ref[:, pl.ds(k * chunk, chunk)], weighted, (0, 0))
+        stacked_ref[pl.ds(k * chunk, chunk), :] = product(rows_ref[:, pl.ds(k * chunk, chunk)], weighted, (0, 0))
 
     repeat(depth // chunk, back)
+    each(sources, pack)
 
 
 def gradient_kernel(
@@ -138,13 +204,19 @@
     width = latent_ref.shape[1]
     rank_index = lax.broadcasted_iota(jnp.int32, (rank_pad, width), 0)
 
+    packed = packed_rows(rank_pad)
+
     def place(g):
         for i in range(group):
             c = g * group + i
             q = order_ref[0, c]
-            for j in range(local):
-                live = rank_index < ranks_ref[j, q]
-                ordered_ref[j, q] = jnp.where(live, returned_ref[c, j * rank_pad : (j + 1) * rank_pad, :], 0.0)
+            for pair in range(local // 2):
+                left, right = 2 * pair, 2 * pair + 1
+                cut = ranks_ref[left, q]
+                both = returned_ref[c, pair * packed : (pair + 1) * packed, :]
+                ordered_ref[left, q] = jnp.where(rank_index < cut, both[:rank_pad], 0.0)
+                second = pltpu.roll(both, packed - cut, 0)[:rank_pad]
+                ordered_ref[right, q] = jnp.where(rank_index < ranks_ref[right, q], second, 0.0)
 
     repeat(rows // group, place)
 
@@ -184,12 +256,13 @@
     u_owned = u_basis[0, 0]
     observed_here = observed[0, 0]
     well_count = observed_here.shape[0]
+    pairs, packed = local // 2, packed_rows(rank_pad)
     depth = u_owned.shape[1]
     group = 8 if rows % 8 == 0 else 1
     chunk = 768 if depth % 768 == 0 else depth
     sent = pl.pallas_call(
         functools.partial(blocks_kernel, group),
-        out_shape=jax.ShapeDtypeStruct((rows, local * rank_pad, width), F32),
+        out_shape=jax.ShapeDtypeStruct((rows, pairs * (packed + MARK), width), F32),
         in_specs=[HBM, HBM, HBM, HBM],
         out_specs=VMEM,
         scratch_shapes=[
@@ -203,13 +276,17 @@
         compiler_params=params([latent, v_rows]),
         name="blocks",
     )(stay(slot_row), stay(ranks_here), stay(latent), stay(v_rows))
-    received = lax.all_to_all(sent, "col", split_axis=0, concat_axis=0, tiled=True).reshape(depth, width)
+    received = lax.all_to_all(sent, "col", split_axis=0, concat_axis=0, tiled=True)
     field, adjoint = pl.pallas_call(
-        functools.partial(owner_kernel, chunk),
-        out_shape=(jax.ShapeDtypeStruct((cells, width), F32), jax.ShapeDtypeStruct((depth, width), F32)),
+        functools.partial(owner_kernel, chunk, rank_pad),
+        out_shape=(
+            jax.ShapeDtypeStruct((cells, width), F32),
+            jax.ShapeDtypeStruct((rows, pairs * packed, width), F32),
+        ),
         in_specs=[HBM, VMEM, VMEM, VMEM],
         out_specs=(VMEM, VMEM),
         scratch_shapes=[
+            pltpu.VMEM((depth, width), F32),
             pltpu.VMEM((well_count, width), F32),
             pltpu.VMEM((well_count, depth), F32),
             pltpu.SMEM((1, well_count), jnp.int32),
@@ -218,9 +295,7 @@
         compiler_params=params([received, u_owned, observed_here]),
         name="owner",
     )(stay(wells[0]), received, u_owned, observed_here)
-    returned = lax.all_to_all(
-        adjoint.reshape(rows, local * rank_pad, width), "col", split_axis=0, concat_axis=0, tiled=True
-    )
+    returned = lax.all_to_all(adjoint, "col", split_axis=0, concat_axis=0, tiled=True)
     paired = n_row & (n_row - 1) == 0
 
     def turn(index, step):

time: 46.1 us -> 43.4 us (0.941)
  blocking collectives: 34.2 us -> 31.1 us
    all_to_all x1, blocking collectives: 15.1 us -> 13.1 us  [on_device(): lax.all_to_all(adjoint, 'col', split_axis=0, concat_axis=0, tiled=True)]
    all_to_all x1, blocking collectives: 19.2 us -> 18 us  [on_device(): lax.all_to_all(sent, 'col', split_axis=0, concat_axis=0, tiled=True)]
where the time goes in v3:
time: 43.4 us; the launch traced here: 43.1 us
  blocking collectives  31.1 us (72%)
  Pallas kernels  4.91 us (11%)
  waiting for transfers between devices  3.74 us (9%)
  starting transfers between devices  1.93 us (4%)
  between operations  0.72 us (2%)
  other arithmetic  0.64 us (1%)
    all_to_all x1, blocking collectives, on_device(): lax.all_to_all(sent, 'col', split_axis=0, concat_axis=0, tiled=True)  18 us
    all_to_all x1, blocking collectives, on_device(): lax.all_to_all(adjoint, 'col', split_axis=0, concat_axis=0, tiled=True)  13.1 us
    ppermute x3, waiting for transfers between devices, on_device(): gradient = gradient + lax.ppermute(parts[step], 'row', pairs)  3.74 us
    pallas_call x1, Pallas kernels, on_device(): pl.pallas_call(functools.partial(owner_kernel, chunk, rank_pad), out_shap...  1.99 us
    ppermute x3, starting transfers between devices, on_device(): gradient = gradient + lax.ppermute(parts[step], 'row', pairs)  1.93 us
    pallas_call x1, Pallas kernels, on_device(): pl.pallas_call(functools.partial(blocks_kernel, group), out_shape=jax.Sha...  1.83 us
    pallas_call x1, Pallas kernels, on_device(): pl.pallas_call(functools.partial(gradient_kernel, group, 'row', turn), ou...  1.09 us
  transfers between devices with their start and end apart: 3, of which 2 were waited for; matrix products, arithmetic and copies ran while one was open for 0% of the time, Pallas kernels for 0%

profile of v3, /device:TPU:0, one launch (start us, length us, event | category | flops | bytes accessed | tf_op | source)
XLA Modules:
  0.0 43.1 jit_solution(6898480663865657968)
XLA Ops:
  0.6 0.0 copy-start.2
  0.6 1.8 %blocks.1 = f32[8,80,128]{2,1,0:T(8,128)S(1)} custom-call(s32[1,8]{1,0:T(1,128)} %order_ref.1, s32[2,8]{1,0:T(2,128)} %bitcast.12, f32[512,128]{1,0:T(8,128)} %latent_ref.1, f32[8,2,48,256]{3,2,1,0:T(8,128)} %bitcast.8), custom_call_target="tpu_custom_call" | custom-call | tf_op jit(solution)/shard_map/blocks/pallas_call | solution.py:263
  2.5 0.0 copy-start.3
  2.5 18.0 %all_to_all.10.received_ref = f32[8,80,128]{2,1,0:T(8,128)S(1)} all-to-all(f32[8,80,128]{2,1,0:T(8,128)S(1)} %blocks.1), channel_id=1, replica_groups=mesh['col'=8,'row'=4] {'col'}, dimensions={0} | all-to-all | bytes 655360 | tf_op jit(solution)/shard_map/all_to_all | solution.py:279
  20.5 0.0 copy-done.2
  20.5 0.0 copy-done.3
  20.5 0.0 copy-start
  20.5 2.0 %owner.1 = (f32[256,128]{1,0:T(8,128)}, f32[8,72,128]{2,1,0:T(8,128)S(1)}) custom-call(s32[1,64]{1,0:T(1,128)} %bitcast.14, f32[8,80,128]{2,1,0:T(8,128)S(1)} %all_to_all.10.received_ref, f32[256,768]{1,0:T(8,128)S(1)} %bitcast.10, f32[64,128]{1,0:T(8,128)S(1)} %bitcast.11), custom_call_target="tpu_custom_call" | custom-call | tf_op jit(solution)/shard_map/owner/pallas_call | solution.py:280
  22.5 0.0 copy-start.1
  22.5 0.0 copy-start.4
  22.5 0.0 copy-start.5
  22.5 13.1 %all_to_all.11.returned_ref = f32[8,72,128]{2,1,0:T(8,128)S(1)} all-to-all(f32[8,72,128]{2,1,0:T(8,128)S(1)} %get-tuple-element.9), channel_id=1, replica_groups=mesh['col'=8,'row'=4] {'col'}, dimensions={0} | all-to-all | bytes 589824 | tf_op jit(solution)/shard_map/all_to_all | solution.py:298
  35.6 0.0 copy-done
  35.6 0.0 copy-done.1
  35.6 0.0 copy-done.4
  35.6 0.0 copy-done.5
  35.6 1.1 %gradient.1 = (f32[128,128]{1,0:T(8,128)S(1)}, f32[128,128]{1,0:T(8,128)S(1)}, f32[128,128]{1,0:T(8,128)S(1)}, f32[128,128]{1,0:T(8,128)S(1)}) custom-call(s32[1,8]{1,0:T(1,128)S(1)} %copy-done.5, s32[2,8]{1,0:T(2,128)S(1)} %bitcast.13, f32[8,72,128]{2,1,0:T(8,128)S(1)} %all_to_all.11.returned_ref, f32[8,2,48,256]{3,2,1,0:T(8,128)S(1)} %bitcast.9, ...), custom_call_target="tpu_custom_call" | custom-call | tf_op jit(solution)/shard_map/gradient/pallas_call | solution.py:305
  36.7 0.1 collective-permute-start
  36.8 1.6 %collective-permute-start.1 = (f32[128,128]{1,0:T(8,128)S(1)}, f32[128,128]{1,0:T(8,128)S(1)}, u32[]{:S(2)}, u32[]{:S(2)}) collective-permute-start(f32[128,128]{1,0:T(8,128)S(1)} %get-tuple-element.12), channel_id=1, source_target_pairs={{0,2},{1,3},{2,0},{3,1},{4,6},{5,7},{6,4},{7,5},{8,10},{9,11},{10,... | collective-permute-start | bytes 196616 | tf_op jit(solution)/shard_map/ppermute | solution.py:317
  38.4 0.3 collective-permute-start.2
  38.7 0.0 collective-permute-done
  38.7 2.6 %collective-permute-done.1 = f32[128,128]{1,0:T(8,128)S(1)} collective-permute-done((f32[128,128]{1,0:T(8,128)S(1)}, f32[128,128]{1,0:T(8,128)S(1)}, u32[]{:S(2)}, u32[]{:S(2)}) %collective-permute-start.1) | collective-permute-done | bytes 65568 | tf_op jit(solution)/shard_map/ppermute | solution.py:317
  41.3 1.1 %collective-permute-done.2 = f32[128,128]{1,0:T(8,128)S(1)} collective-permute-done((f32[128,128]{1,0:T(8,128)S(1)}, f32[128,128]{1,0:T(8,128)S(1)}, u32[]{:S(2)}, u32[]{:S(2)}) %collective-permute-start.2) | collective-permute-done | bytes 65568 | tf_op jit(solution)/shard_map/ppermute | solution.py:317
  42.4 0.6 %add_add_fusion = f32[128,128]{1,0:T(8,128)} fusion(f32[128,128]{1,0:T(8,128)S(1)} %collective-permute-done.2, f32[128,128]{1,0:T(8,128)S(1)} %collective-permute-done.1, f32[128,128]{1,0:T(8,128)S(1)} %get-tuple-element.10, f32[128,128]{1,0:T(8,128)S(1)} %collective-permute-done), kind=kLoop, calls=%fused_computation | loop fusion | flops 49152 | bytes 327680 | tf_op jit(solution)/shard_map/add | solution.py:317
Async XLA Ops:
  0.6 19.8 %copy-start.2 = (f32[1,1,256,768]{3,2,1,0:T(8,128)S(1)}, f32[1,1,256,768]{3,2,1,0:T(8,128)}, u32[]{:S(2)}) copy-start(f32[1,1,256,768]{3,2,1,0:T(8,128)} %param.9) | copy-start | bytes 2359300
  2.5 18.0 %copy-start.3 = (f32[1,1,64,128]{3,2,1,0:T(8,128)S(1)}, f32[1,1,64,128]{3,2,1,0:T(8,128)}, u32[]{:S(2)}) copy-start(f32[1,1,64,128]{3,2,1,0:T(8,128)} %param.13) | copy-start | bytes 98308
  20.5 15.1 %copy-start = (f32[8,1,2,48,256]{4,3,2,1,0:T(8,128)S(1)}, f32[8,1,2,48,256]{4,3,2,1,0:T(8,128)}, u32[]{:S(2)}) copy-start(f32[8,1,2,48,256]{4,3,2,1,0:T(8,128)} %param.8) | copy-start | bytes 2359300
  22.5 13.1 %copy-start.1 = (f32[512,128]{1,0:T(8,128)S(1)}, f32[512,128]{1,0:T(8,128)}, u32[]{:S(2)}) copy-start(f32[512,128]{1,0:T(8,128)} %latent_ref.1) | copy-start | bytes 786436
  22.5 13.1 %copy-start.4 = (s32[8,1,2]{0,2,1:T(2,128)S(1)}, s32[8,1,2]{0,2,1:T(2,128)}, u32[]{:S(2)}) copy-start(s32[8,1,2]{0,2,1:T(2,128)} %param.10) | copy-start | bytes 196
  22.5 13.1 %copy-start.5 = (s32[1,8]{1,0:T(1,128)S(1)}, s32[1,8]{1,0:T(1,128)}, u32[]{:S(2)}) copy-start(s32[1,8]{1,0:T(1,128)} %order_ref.1) | copy-start | bytes 100
  36.7 1.9 %collective-permute-start = (f32[128,128]{1,0:T(8,128)S(1)}, f32[128,128]{1,0:T(8,128)S(1)}, u32[]{:S(2)}, u32[]{:S(2)}) collective-permute-start(f32[128,128]{1,0:T(8,128)S(1)} %get-tuple-element.11), channel_id=1, source_target_pairs={{0,1},{1,0},{2,3},{3,2},{4,5},{5,4},{6,7},{7,6},{8,9},{9,8},{10,11... | collective-permute-start | bytes 196616 | tf_op jit(solution)/shard_map/ppermute | solution.py:317
  36.8 4.5 %collective-permute-start.1 = (f32[128,128]{1,0:T(8,128)S(1)}, f32[128,128]{1,0:T(8,128)S(1)}, u32[]{:S(2)}, u32[]{:S(2)}) collective-permute-start(f32[128,128]{1,0:T(8,128)S(1)} %get-tuple-element.12), channel_id=1, source_target_pairs={{0,2},{1,3},{2,0},{3,1},{4,6},{5,7},{6,4},{7,5},{8,10},{9,11},{10,... | collective-permute-start | bytes 196616 | tf_op jit(solution)/shard_map/ppermute | solution.py:317
  38.4 4.0 %collective-permute-start.2 = (f32[128,128]{1,0:T(8,128)S(1)}, f32[128,128]{1,0:T(8,128)S(1)}, u32[]{:S(2)}, u32[]{:S(2)}) collective-permute-start(f32[128,128]{1,0:T(8,128)S(1)} %get-tuple-element.13), channel_id=1, source_target_pairs={{0,3},{1,2},{2,1},{3,0},{4,7},{5,6},{6,5},{7,4},{8,11},{9,10},{10,... | collective-permute-start | bytes 196616 | tf_op jit(solution)/shard_map/ppermute | solution.py:317

commit v4 on v3

--- a/solution.py
+++ b/solution.py
@@ -10,7 +10,6 @@
 F32 = jnp.float32
 BF16 = jnp.bfloat16
 VMEM = pl.BlockSpec(memory_space=pltpu.VMEM)
-SMEM = pl.BlockSpec(memory_space=pltpu.SMEM)
 HBM = pl.BlockSpec(memory_space=pltpu.HBM)
 MARK = 8
 
@@ -58,18 +57,39 @@
     return jnp.concatenate([x, jnp.zeros((size - x.shape[0], x.shape[1]), x.dtype)], axis=0)
 
 
+def scalar(ref, row, column):
+    return ref[row : row + 1, column : column + 1][0, 0]
+
+
 def stay(x):
     return pltpu.with_memory_space_constraint(x, pltpu.HBM)
 
 
 def blocks_kernel(
-    group, order_hbm, ranks_hbm, latent_hbm, v_hbm, out_ref, held_ref, order_ref, ranks_ref, latent_ref, v_ref, sems
+    group,
+    order_hbm,
+    ranks_hbm,
+    latent_hbm,
+    v_hbm,
+    out_ref,
+    order_out,
+    ranks_out,
+    held_ref,
+    order_ref,
+    ranks_ref,
+    latent_ref,
+    v_ref,
+    sems,
 ):
     local, rows, rank_pad, cells = v_ref.shape
     width = latent_ref.shape[1]
     small = [
         pltpu.make_async_copy(order_hbm, order_ref, sems.at[2 * local]),
         pltpu.make_async_copy(ranks_hbm, ranks_ref, sems.at[2 * local + 1]),
+    ]
+    later = [
+        pltpu.make_async_copy(order_hbm, order_out, sems.at[2 * local + 2]),
+        pltpu.make_async_copy(ranks_hbm, ranks_out, sems.at[2 * local + 3]),
     ]
     tiles = []
     for j in range(local):
@@ -83,7 +103,7 @@
     for copies in tiles:
         for copy in copies:
             copy.start()
-    for copy in small:
+    for copy in small + later:
         copy.start()
     for j in range(local):
         for copy in tiles[j]:
@@ -114,6 +134,8 @@
                 out_ref[c, base + size : base + size + MARK, :] = jnp.full((MARK, width), cut.astype(F32))
 
     repeat(rows // group, place)
+    for copy in later:
+        copy.wait()
 
 
 def owner_kernel(
@@ -123,13 +145,15 @@
     received_ref,
     u_ref,
     observed_ref,
-    field_ref,
+    field_hbm,
     packed_ref,
     stacked_ref,
+    field_ref,
     at_wells_ref,
     rows_ref,
     wells_ref,
     sem,
+    field_sem,
 ):
     sources = received_ref.shape[0]
     depth, width = stacked_ref.shape
@@ -143,7 +167,7 @@
 
     def first_rank(c, pair):
         at = pair * (size + MARK) + size
-        return received_ref[c, at : at + 1, :][0, 0].astype(jnp.int32)
+        return scalar(received_ref.at[c], at, 0).astype(jnp.int32)
 
     def unpack(c):
         for pair in range(pairs):
@@ -181,6 +205,8 @@
                 field_ref[...] += part
 
     repeat(depth // chunk, first)
+    away = pltpu.make_async_copy(field_ref, field_hbm, field_sem)
+    away.start()
     copy.wait()
     for w in range(wells):
         cell = wells_ref[0, w]
@@ -194,6 +220,7 @@
 
     repeat(depth // chunk, back)
     each(sources, pack)
+    away.wait()
 
 
 def gradient_kernel(
@@ -206,19 +233,22 @@
 
     packed = packed_rows(rank_pad)
 
-    def place(g):
-        for i in range(group):
-            c = g * group + i
-            q = order_ref[0, c]
+    square = (rows, rows)
+    is_owner = order_ref[...] == lax.broadcasted_iota(jnp.int32, square, 0)
+    owners = jnp.sum(jnp.where(is_owner, lax.broadcasted_iota(jnp.int32, square, 1), 0), axis=1, keepdims=True)
+
+    def place():
+        for q in range(rows):
+            c = owners[q : q + 1, :][0, 0]
             for pair in range(local // 2):
                 left, right = 2 * pair, 2 * pair + 1
-                cut = ranks_ref[left, q]
+                cut = scalar(ranks_ref, left, q)
                 both = returned_ref[c, pair * packed : (pair + 1) * packed, :]
                 ordered_ref[left, q] = jnp.where(rank_index < cut, both[:rank_pad], 0.0)
                 second = pltpu.roll(both, packed - cut, 0)[:rank_pad]
-                ordered_ref[right, q] = jnp.where(rank_index < ranks_ref[right, q], second, 0.0)
-
-    repeat(rows // group, place)
+                ordered_ref[right, q] = jnp.where(rank_index < scalar(ranks_ref, right, q), second, 0.0)
+
+    place()
 
     def some(g):
         for j in range(local):
@@ -252,7 +282,6 @@
     rows, _, local, rank_pad, cells = v_basis.shape
     width = latent.shape[1]
     v_rows = v_basis[:, 0]
-    ranks_here = ranks[:, 0].T
     u_owned = u_basis[0, 0]
     observed_here = observed[0, 0]
     well_count = observed_here.shape[0]
@@ -260,22 +289,26 @@
     depth = u_owned.shape[1]
     group = 8 if rows % 8 == 0 else 1
     chunk = 768 if depth % 768 == 0 else depth
-    sent = pl.pallas_call(
+    sent, order_here, ranks_here = pl.pallas_call(
         functools.partial(blocks_kernel, group),
-        out_shape=jax.ShapeDtypeStruct((rows, pairs * (packed + MARK), width), F32),
-        in_specs=[HBM, HBM, HBM, HBM],
-        out_specs=VMEM,
+        out_shape=(
+            jax.ShapeDtypeStruct((rows, pairs * (packed + MARK), width), F32),
+            jax.ShapeDtypeStruct((1, rows), jnp.int32),
+            jax.ShapeDtypeStruct((local, rows), jnp.int32),
+        ),
+        in_specs=[HBM] * 4,
+        out_specs=(VMEM,) * 3,
         scratch_shapes=[
             pltpu.VMEM((local, rows, rank_pad, width), F32),
             pltpu.SMEM(slot_row.shape, jnp.int32),
-            pltpu.SMEM(ranks_here.shape, jnp.int32),
+            pltpu.SMEM((local, rows), jnp.int32),
             pltpu.VMEM(latent.shape, F32),
             pltpu.VMEM((local, rows, rank_pad, cells), F32),
-            pltpu.SemaphoreType.DMA((2 * local + 2,)),
+            pltpu.SemaphoreType.DMA((2 * local + 4,)),
         ],
         compiler_params=params([latent, v_rows]),
         name="blocks",
-    )(stay(slot_row), stay(ranks_here), stay(latent), stay(v_rows))
+    )(stay(slot_row), stay(ranks[:, 0].T), stay(latent), stay(v_rows))
     received = lax.all_to_all(sent, "col", split_axis=0, concat_axis=0, tiled=True)
     field, adjoint = pl.pallas_call(
         functools.partial(owner_kernel, chunk, rank_pad),
@@ -284,12 +317,14 @@
             jax.ShapeDtypeStruct((rows, pairs * packed, width), F32),
         ),
         in_specs=[HBM, VMEM, VMEM, VMEM],
-        out_specs=(VMEM, VMEM),
+        out_specs=(HBM, VMEM),
         scratch_shapes=[
             pltpu.VMEM((depth, width), F32),
+            pltpu.VMEM((cells, width), F32),
             pltpu.VMEM((well_count, width), F32),
             pltpu.VMEM((well_count, depth), F32),
             pltpu.SMEM((1, well_count), jnp.int32),
+            pltpu.SemaphoreType.DMA,
             pltpu.SemaphoreType.DMA,
         ],
         compiler_params=params([received, u_owned, observed_here]),
@@ -305,12 +340,12 @@
     parts = pl.pallas_call(
         functools.partial(gradient_kernel, group, "row", turn),
         out_shape=[jax.ShapeDtypeStruct((size, width), F32)] * n_row,
-        in_specs=[SMEM, SMEM, VMEM, VMEM, VMEM],
+        in_specs=[VMEM] * 5,
         out_specs=[VMEM] * n_row,
         scratch_shapes=[pltpu.VMEM((local, rows, rank_pad, width), F32), pltpu.VMEM((local * cells, width), F32)],
         compiler_params=params([returned, v_rows, latent]),
         name="gradient",
-    )(slot_row, ranks_here, returned, v_rows, latent)
+    )(order_here, ranks_here, returned, v_rows, latent)
     gradient = parts[0]
     for step in range(1, n_row):
         pairs = [(i, i ^ step if paired else (i + step) % n_row) for i in range(n_row)]

time: 43.4 us -> 42.3 us (0.975)
  Pallas kernels: 4.91 us -> 3.93 us
    pallas_call x1, Pallas kernels: 1.99 us -> 1.45 us  [on_device(): pl.pallas_call(functools.partial(owner_kernel, chunk, rank_pad), out_shap...]
    pallas_call x1, Pallas kernels: 1.09 us -> 0.64 us  [on_device(): pl.pallas_call(functools.partial(gradient_kernel, group, 'row', turn), ou...]
where the time goes in v4:
time: 42.3 us; the launch traced here: 42.1 us
  blocking collectives  31.1 us (74%)
  Pallas kernels  3.93 us (9%)
  waiting for transfers between devices  3.74 us (9%)
  starting transfers between devices  1.93 us (5%)
  between operations  0.69 us (2%)
  other arithmetic  0.64 us (2%)
    all_to_all x1, blocking collectives, on_device(): lax.all_to_all(sent, 'col', split_axis=0, concat_axis=0, tiled=True)  18 us
    all_to_all x1, blocking collectives, on_device(): lax.all_to_all(adjoint, 'col', split_axis=0, concat_axis=0, tiled=True)  13.1 us
    ppermute x3, waiting for transfers between devices, on_device(): gradient = gradient + lax.ppermute(parts[step], 'row', pairs)  3.74 us
    ppermute x3, starting transfers between devices, on_device(): gradient = gradient + lax.ppermute(parts[step], 'row', pairs)  1.93 us
    pallas_call x1, Pallas kernels, on_device(): pl.pallas_call(functools.partial(blocks_kernel, group), out_shape=(jax.Sh...  1.85 us
    pallas_call x1, Pallas kernels, on_device(): pl.pallas_call(functools.partial(owner_kernel, chunk, rank_pad), out_shap...  1.45 us
  transfers between devices with their start and end apart: 3, of which 2 were waited for; matrix products, arithmetic and copies ran while one was open for 0% of the time, Pallas kernels for 0%

profile of v4, /device:TPU:0, one launch (start us, length us, event | category | flops | bytes accessed | tf_op | source)
XLA Modules:
  0.0 42.1 jit_solution(16372025901000657750)
XLA Ops:
  0.6 0.0 copy-start.2
  0.6 1.9 %blocks.1 = (f32[8,80,128]{2,1,0:T(8,128)S(1)}, s32[1,8]{1,0:T(1,128)S(1)}, s32[2,8]{1,0:T(2,128)S(1)}) custom-call(s32[1,8]{1,0:T(1,128)} %order_hbm.1, s32[2,8]{1,0:T(2,128)} %bitcast.12, f32[512,128]{1,0:T(8,128)} %latent_ref.1, f32[8,2,48,256]{3,2,1,0:T(8,128)} %bitcast.8), custom_call_target="tpu_custom_call" | custom-call | tf_op jit(solution)/shard_map/blocks/pallas_call | solution.py:292
  2.5 0.0 copy-start.3
  2.5 18.0 %all_to_all.10.received_ref = f32[8,80,128]{2,1,0:T(8,128)S(1)} all-to-all(f32[8,80,128]{2,1,0:T(8,128)S(1)} %get-tuple-element.11), channel_id=1, replica_groups=mesh['col'=8,'row'=4] {'col'}, dimensions={0} | all-to-all | bytes 655360 | tf_op jit(solution)/shard_map/all_to_all | solution.py:312
  20.5 0.0 copy-done.2
  20.5 0.0 copy-done.3
  20.5 0.0 copy-start
  20.5 1.4 %owner.1 = (f32[256,128]{1,0:T(8,128)}, f32[8,72,128]{2,1,0:T(8,128)S(1)}) custom-call(s32[1,64]{1,0:T(1,128)} %bitcast.13, f32[8,80,128]{2,1,0:T(8,128)S(1)} %all_to_all.10.received_ref, f32[256,768]{1,0:T(8,128)S(1)} %bitcast.10, f32[64,128]{1,0:T(8,128)S(1)} %bitcast.11), custom_call_target="tpu_custom_call" | custom-call | tf_op jit(solution)/shard_map/owner/pallas_call | solution.py:313
  22.0 0.0 copy-start.1
  22.0 13.1 %all_to_all.11.returned_ref = f32[8,72,128]{2,1,0:T(8,128)S(1)} all-to-all(f32[8,72,128]{2,1,0:T(8,128)S(1)} %get-tuple-element.15), channel_id=1, replica_groups=mesh['col'=8,'row'=4] {'col'}, dimensions={0} | all-to-all | bytes 589824 | tf_op jit(solution)/shard_map/all_to_all | solution.py:333
  35.1 0.0 copy-done
  35.1 0.0 copy-done.1
  35.1 0.6 %gradient.1 = (f32[128,128]{1,0:T(8,128)S(1)}, f32[128,128]{1,0:T(8,128)S(1)}, f32[128,128]{1,0:T(8,128)S(1)}, f32[128,128]{1,0:T(8,128)S(1)}) custom-call(s32[1,8]{1,0:T(1,128)S(1)} %get-tuple-element.13.order_ref, s32[2,8]{1,0:T(2,128)S(1)} %get-tuple-element.14.ranks_ref, f32[8,72,128]{2,1,0:T(8,128)S(1)} %all_to_all.11.returned_ref, ...), custom_call_target="tpu_custom_call" | custom-call | tf_op jit(solution)/shard_map/gradient/pallas_call | solution.py:340
  35.7 0.1 collective-permute-start
  35.8 1.6 %collective-permute-start.1 = (f32[128,128]{1,0:T(8,128)S(1)}, f32[128,128]{1,0:T(8,128)S(1)}, u32[]{:S(2)}, u32[]{:S(2)}) collective-permute-start(f32[128,128]{1,0:T(8,128)S(1)} %get-tuple-element.18), channel_id=1, source_target_pairs={{0,2},{1,3},{2,0},{3,1},{4,6},{5,7},{6,4},{7,5},{8,10},{9,11},{10,... | collective-permute-start | bytes 196616 | tf_op jit(solution)/shard_map/ppermute | solution.py:352
  37.4 0.3 collective-permute-start.2
  37.7 0.0 collective-permute-done
  37.7 2.6 %collective-permute-done.1 = f32[128,128]{1,0:T(8,128)S(1)} collective-permute-done((f32[128,128]{1,0:T(8,128)S(1)}, f32[128,128]{1,0:T(8,128)S(1)}, u32[]{:S(2)}, u32[]{:S(2)}) %collective-permute-start.1) | collective-permute-done | bytes 65568 | tf_op jit(solution)/shard_map/ppermute | solution.py:352
  40.3 1.1 %collective-permute-done.2 = f32[128,128]{1,0:T(8,128)S(1)} collective-permute-done((f32[128,128]{1,0:T(8,128)S(1)}, f32[128,128]{1,0:T(8,128)S(1)}, u32[]{:S(2)}, u32[]{:S(2)}) %collective-permute-start.2) | collective-permute-done | bytes 65568 | tf_op jit(solution)/shard_map/ppermute | solution.py:352
  41.4 0.6 %add_add_fusion = f32[128,128]{1,0:T(8,128)} fusion(f32[128,128]{1,0:T(8,128)S(1)} %collective-permute-done.2, f32[128,128]{1,0:T(8,128)S(1)} %collective-permute-done.1, f32[128,128]{1,0:T(8,128)S(1)} %get-tuple-element.16, f32[128,128]{1,0:T(8,128)S(1)} %collective-permute-done), kind=kLoop, calls=%fused_computation | loop fusion | flops 49152 | bytes 327680 | tf_op jit(solution)/shard_map/add | solution.py:352
Async XLA Ops:
  0.6 19.9 %copy-start.2 = (f32[1,1,256,768]{3,2,1,0:T(8,128)S(1)}, f32[1,1,256,768]{3,2,1,0:T(8,128)}, u32[]{:S(2)}) copy-start(f32[1,1,256,768]{3,2,1,0:T(8,128)} %param.9) | copy-start | bytes 2359300
  2.5 18.0 %copy-start.3 = (f32[1,1,64,128]{3,2,1,0:T(8,128)S(1)}, f32[1,1,64,128]{3,2,1,0:T(8,128)}, u32[]{:S(2)}) copy-start(f32[1,1,64,128]{3,2,1,0:T(8,128)} %param.13) | copy-start | bytes 98308
  20.5 14.6 %copy-start = (f32[8,1,2,48,256]{4,3,2,1,0:T(8,128)S(1)}, f32[8,1,2,48,256]{4,3,2,1,0:T(8,128)}, u32[]{:S(2)}) copy-start(f32[8,1,2,48,256]{4,3,2,1,0:T(8,128)} %param.8) | copy-start | bytes 2359300
  22.0 13.1 %copy-start.1 = (f32[512,128]{1,0:T(8,128)S(1)}, f32[512,128]{1,0:T(8,128)}, u32[]{:S(2)}) copy-start(f32[512,128]{1,0:T(8,128)} %latent_ref.1) | copy-start | bytes 786436
  35.7 1.9 %collective-permute-start = (f32[128,128]{1,0:T(8,128)S(1)}, f32[128,128]{1,0:T(8,128)S(1)}, u32[]{:S(2)}, u32[]{:S(2)}) collective-permute-start(f32[128,128]{1,0:T(8,128)S(1)} %get-tuple-element.17), channel_id=1, source_target_pairs={{0,1},{1,0},{2,3},{3,2},{4,5},{5,4},{6,7},{7,6},{8,9},{9,8},{10,11... | collective-permute-start | bytes 196616 | tf_op jit(solution)/shard_map/ppermute | solution.py:352
  35.8 4.5 %collective-permute-start.1 = (f32[128,128]{1,0:T(8,128)S(1)}, f32[128,128]{1,0:T(8,128)S(1)}, u32[]{:S(2)}, u32[]{:S(2)}) collective-permute-start(f32[128,128]{1,0:T(8,128)S(1)} %get-tuple-element.18), channel_id=1, source_target_pairs={{0,2},{1,3},{2,0},{3,1},{4,6},{5,7},{6,4},{7,5},{8,10},{9,11},{10,... | collective-permute-start | bytes 196616 | tf_op jit(solution)/shard_map/ppermute | solution.py:352
  37.4 4.0 %collective-permute-start.2 = (f32[128,128]{1,0:T(8,128)S(1)}, f32[128,128]{1,0:T(8,128)S(1)}, u32[]{:S(2)}, u32[]{:S(2)}) collective-permute-start(f32[128,128]{1,0:T(8,128)S(1)} %get-tuple-element.19), channel_id=1, source_target_pairs={{0,3},{1,2},{2,1},{3,0},{4,7},{5,6},{6,5},{7,4},{8,11},{9,10},{10,... | collective-permute-start | bytes 196616 | tf_op jit(solution)/shard_map/ppermute | solution.py:352

commit v5 on v4

--- a/solution.py
+++ b/solution.py
@@ -14,15 +14,22 @@
 MARK = 8
 
 
+def split_rest(x):
+    high = x.astype(BF16)
+    return high, x - high.astype(F32)
+
+
 def split(x):
-    high = x.astype(BF16)
-    low = (x - high.astype(F32)).astype(BF16)
-    return high, low
+    high, rest = split_rest(x)
+    return high, rest.astype(BF16)
 
 
 def product(a, b, contract=(1, 0)):
+    return product_of(*split(a), b, contract)
+
+
+def product_of(a_high, a_low, b, contract=(1, 0)):
     dims = (((contract[0],), (contract[1],)), ((), ()))
-    a_high, a_low = split(a)
     b_high, b_low = split(b)
     both = lax.dot_general(a_high, jnp.concatenate([b_high, b_low], axis=1), dims, preferred_element_type=F32)
     width = b.shape[1]
@@ -69,11 +76,13 @@
     group,
     order_hbm,
     ranks_hbm,
+    wells_hbm,
     latent_hbm,
     v_hbm,
     out_ref,
     order_out,
     ranks_out,
+    wells_out,
     held_ref,
     order_ref,
     ranks_ref,
@@ -90,6 +99,7 @@
     later = [
         pltpu.make_async_copy(order_hbm, order_out, sems.at[2 * local + 2]),
         pltpu.make_async_copy(ranks_hbm, ranks_out, sems.at[2 * local + 3]),
+        pltpu.make_async_copy(wells_hbm, wells_out, sems.at[2 * local + 4]),
     ]
     tiles = []
     for j in range(local):
@@ -141,27 +151,21 @@
 def owner_kernel(
     chunk,
     rank_pad,
-    wells_hbm,
+    wells_ref,
     received_ref,
     u_ref,
     observed_ref,
-    field_hbm,
+    field_ref,
     packed_ref,
     stacked_ref,
-    field_ref,
-    at_wells_ref,
     rows_ref,
-    wells_ref,
-    sem,
-    field_sem,
 ):
     sources = received_ref.shape[0]
     depth, width = stacked_ref.shape
     wells = observed_ref.shape[0]
+    cells = u_ref.shape[0]
     size = packed_rows(rank_pad)
     pairs = received_ref.shape[1] // (size + MARK)
-    copy = pltpu.make_async_copy(wells_hbm, wells_ref, sem)
-    copy.start()
     rank_index = lax.broadcasted_iota(jnp.int32, (rank_pad, width), 0)
     packed_index = lax.broadcasted_iota(jnp.int32, (size, width), 0)
 
@@ -189,9 +193,17 @@
             packed_ref[c, pair * size : (pair + 1) * size, :] = jnp.where(packed_index < cut, first, second)
 
     each(sources, unpack)
+    picked = jnp.where(lax.broadcasted_iota(jnp.int32, (cells, wells), 0) == wells_ref[...], 1.0, 0.0).astype(BF16)
+    turned = (((0,), (0,)), ((), ()))
 
     def first(k):
-        part = product(u_ref[:, pl.ds(k * chunk, chunk)], stacked_ref[pl.ds(k * chunk, chunk), :])
+        here = pl.ds(k * chunk, chunk)
+        high, low = split(u_ref[:, here])
+        part = product_of(high, low, stacked_ref[here, :])
+        own = lax.dot_general(picked, high, turned, preferred_element_type=F32).astype(BF16)
+        rows_ref[0:wells, here] = own
+        rows_ref[wells : 2 * wells, here] = own
+        rows_ref[2 * wells :, here] = lax.dot_general(picked, low, turned, preferred_element_type=F32).astype(BF16)
         if depth == chunk:
             field_ref[...] = part
         else:
@@ -205,22 +217,21 @@
                 field_ref[...] += part
 
     repeat(depth // chunk, first)
-    away = pltpu.make_async_copy(field_ref, field_hbm, field_sem)
-    away.start()
-    copy.wait()
-    for w in range(wells):
-        cell = wells_ref[0, w]
-        at_wells_ref[w : w + 1, :] = field_ref[pl.ds(cell, 1), :]
-        rows_ref[w : w + 1, :] = u_ref[pl.ds(cell, 1), :]
-    expo = jnp.exp(at_wells_ref[...])
+    high, rest = split_rest(field_ref[...])
+    middle, rest = split_rest(rest)
+    parts = jnp.concatenate([high, middle, rest.astype(BF16)], axis=1)
+    parts = lax.dot_general(picked, parts, turned, preferred_element_type=F32)
+    expo = jnp.exp(parts[:, :width] + parts[:, width : 2 * width] + parts[:, 2 * width :])
     weighted = (expo - observed_ref[...]) * expo / 0.25
+    high, low = split(weighted)
+    below = jnp.concatenate([high, low, high], axis=0)
 
     def back(k):
-        stacked_ref[pl.ds(k * chunk, chunk), :] = product(rows_ref[:, pl.ds(k * chunk, chunk)], weighted, (0, 0))
+        here = pl.ds(k * chunk, chunk)
+        stacked_ref[here, :] = lax.dot_general(rows_ref[:, here], below, turned, preferred_element_type=F32)
 
     repeat(depth // chunk, back)
     each(sources, pack)
-    away.wait()
 
 
 def gradient_kernel(
@@ -289,47 +300,43 @@
     depth = u_owned.shape[1]
     group = 8 if rows % 8 == 0 else 1
     chunk = 768 if depth % 768 == 0 else depth
-    sent, order_here, ranks_here = pl.pallas_call(
+    sent, order_here, ranks_here, wells_here = pl.pallas_call(
         functools.partial(blocks_kernel, group),
         out_shape=(
             jax.ShapeDtypeStruct((rows, pairs * (packed + MARK), width), F32),
             jax.ShapeDtypeStruct((1, rows), jnp.int32),
             jax.ShapeDtypeStruct((local, rows), jnp.int32),
+            jax.ShapeDtypeStruct((1, well_count), jnp.int32),
         ),
-        in_specs=[HBM] * 4,
-        out_specs=(VMEM,) * 3,
+        in_specs=[HBM] * 5,
+        out_specs=(VMEM,) * 4,
         scratch_shapes=[
             pltpu.VMEM((local, rows, rank_pad, width), F32),
             pltpu.SMEM(slot_row.shape, jnp.int32),
             pltpu.SMEM((local, rows), jnp.int32),
             pltpu.VMEM(latent.shape, F32),
             pltpu.VMEM((local, rows, rank_pad, cells), F32),
-            pltpu.SemaphoreType.DMA((2 * local + 4,)),
+            pltpu.SemaphoreType.DMA((2 * local + 5,)),
         ],
         compiler_params=params([latent, v_rows]),
         name="blocks",
-    )(stay(slot_row), stay(ranks[:, 0].T), stay(latent), stay(v_rows))
+    )(stay(slot_row), stay(ranks[:, 0].T), stay(wells[0]), stay(latent), stay(v_rows))
     received = lax.all_to_all(sent, "col", split_axis=0, concat_axis=0, tiled=True)
     field, adjoint = pl.pallas_call(
         functools.partial(owner_kernel, chunk, rank_pad),
         out_shape=(
-            jax.ShapeDtypeStruct((cells, width), F32),
+            pltpu.VMEM((cells, width), F32),
             jax.ShapeDtypeStruct((rows, pairs * packed, width), F32),
         ),
-        in_specs=[HBM, VMEM, VMEM, VMEM],
-        out_specs=(HBM, VMEM),
+        in_specs=[VMEM, VMEM, VMEM, VMEM],
+        out_specs=(VMEM, VMEM),
         scratch_shapes=[
             pltpu.VMEM((depth, width), F32),
-            pltpu.VMEM((cells, width), F32),
-            pltpu.VMEM((well_count, width), F32),
-            pltpu.VMEM((well_count, depth), F32),
-            pltpu.SMEM((1, well_count), jnp.int32),
-            pltpu.SemaphoreType.DMA,
-            pltpu.SemaphoreType.DMA,
+            pltpu.VMEM((3 * well_count, depth), BF16),
         ],
         compiler_params=params([received, u_owned, observed_here]),
         name="owner",
-    )(stay(wells[0]), received, u_owned, observed_here)
+    )(wells_here, received, u_owned, observed_here)
     returned = lax.all_to_all(adjoint, "col", split_axis=0, concat_axis=0, tiled=True)
     paired = n_row & (n_row - 1) == 0
 

time: 42.3 us -> 41.8 us (0.988)
  waiting for transfers between devices: 3.74 us -> 3.08 us
  local copies, waits for them, and re-layouts: 0.02 us -> 0.68 us
  Pallas kernels: 3.93 us -> 3.45 us
    unnamed x8 -> x9, local copies, waits for them, and re-layouts: 0.02 us -> 0.68 us
    ppermute x3, waiting for transfers between devices: 3.74 us -> 3.08 us  [on_device(): gradient = gradient + lax.ppermute(parts[step], 'row', pairs)]
    pallas_call x1, Pallas kernels: 1.45 us -> 0.95 us  [on_device(): pl.pallas_call(functools.partial(owner_kernel, chunk, rank_pad), out_shap...]
  transfers between devices with their start and end apart: 3 -> 3, of which waited for: 2 -> 2; matrix products, arithmetic and copies ran while one was open for 0% -> 2% of each run, Pallas kernels for 0% -> 0%
where the time goes in v5:
time: 41.8 us; the launch traced here: 41.6 us
  blocking collectives  31.1 us (74%)
  Pallas kernels  3.45 us (8%)
  waiting for transfers between devices  3.08 us (7%)
  starting transfers between devices  1.93 us (5%)
  between operations  0.69 us (2%)
  local copies, waits for them, and re-layouts  0.68 us (2%)
  other arithmetic  0.64 us (2%)
    all_to_all x1, blocking collectives, on_device(): lax.all_to_all(sent, 'col', split_axis=0, concat_axis=0, tiled=True)  18 us
    all_to_all x1, blocking collectives, on_device(): lax.all_to_all(adjoint, 'col', split_axis=0, concat_axis=0, tiled=True)  13.1 us
    ppermute x3, waiting for transfers between devices, on_device(): gradient = gradient + lax.ppermute(parts[step], 'row', pairs)  3.08 us
    ppermute x3, starting transfers between devices, on_device(): gradient = gradient + lax.ppermute(parts[step], 'row', pairs)  1.93 us
    pallas_call x1, Pallas kernels, on_device(): pl.pallas_call(functools.partial(blocks_kernel, group), out_shape=(jax.Sh...  1.86 us
    pallas_call x1, Pallas kernels, on_device(): pl.pallas_call(functools.partial(owner_kernel, chunk, rank_pad), out_shap...  0.95 us
  transfers between devices with their start and end apart: 3, of which 2 were waited for; matrix products, arithmetic and copies ran while one was open for 2% of the time, Pallas kernels for 0%

profile of v5, /device:TPU:0, one launch (start us, length us, event | category | flops | bytes accessed | tf_op | source)
XLA Modules:
  0.0 41.6 jit_solution(9529134072306180584)
XLA Ops:
  0.6 0.0 copy-start.2
  0.6 1.9 %blocks.1 = (f32[8,80,128]{2,1,0:T(8,128)S(1)}, s32[1,8]{1,0:T(1,128)S(1)}, s32[2,8]{1,0:T(2,128)S(1)}, s32[1,64]{1,0:T(1,128)S(1)}) custom-call(s32[1,8]{1,0:T(1,128)} %order_hbm.1, s32[2,8]{1,0:T(2,128)} %bitcast.13, s32[1,64]{1,0:T(1,128)} %bitcast.14, f32[512,128]{1,0:T(8,128)} %latent_ref.1, f32[8,2,48,256]{3,2,1,0:T(8,128)} %bitcast.9), custom_call_target="tpu_custom_call" | custom-call | tf_op jit(solution)/shard_map/blocks/pallas_call | solution.py:303
  2.5 0.0 copy-start.3
  2.5 18.0 %all_to_all.10.received_ref = f32[8,80,128]{2,1,0:T(8,128)S(1)} all-to-all(f32[8,80,128]{2,1,0:T(8,128)S(1)} %get-tuple-element.13), channel_id=1, replica_groups=mesh['col'=8,'row'=4] {'col'}, dimensions={0} | all-to-all | bytes 655360 | tf_op jit(solution)/shard_map/all_to_all | solution.py:324
  20.5 0.0 copy-done.2
  20.5 0.0 copy-done.3
  20.5 0.0 copy-start
  20.5 1.0 %owner.1 = (f32[256,128]{1,0:T(8,128)S(1)}, f32[8,72,128]{2,1,0:T(8,128)S(1)}) custom-call(s32[1,64]{1,0:T(1,128)S(1)} %get-tuple-element.12.wells_ref, f32[8,80,128]{2,1,0:T(8,128)S(1)} %all_to_all.10.received_ref, f32[256,768]{1,0:T(8,128)S(1)} %bitcast.11, f32[64,128]{1,0:T(8,128)S(1)} %bitcast.12), custom_call_target="tpu_custom_call" | custom-call | tf_op jit(solution)/shard_map/owner/pallas_call | solution.py:325
  21.5 0.0 copy-start.1
  21.5 13.1 %all_to_all.11.returned_ref = f32[8,72,128]{2,1,0:T(8,128)S(1)} all-to-all(f32[8,72,128]{2,1,0:T(8,128)S(1)} %get-tuple-element.17), channel_id=1, replica_groups=mesh['col'=8,'row'=4] {'col'}, dimensions={0} | all-to-all | bytes 589824 | tf_op jit(solution)/shard_map/all_to_all | solution.py:340
  34.6 0.0 copy-done
  34.6 0.0 copy-done.1
  34.6 0.6 %gradient.1 = (f32[128,128]{1,0:T(8,128)S(1)}, f32[128,128]{1,0:T(8,128)S(1)}, f32[128,128]{1,0:T(8,128)S(1)}, f32[128,128]{1,0:T(8,128)S(1)}) custom-call(s32[1,8]{1,0:T(1,128)S(1)} %get-tuple-element.15.order_ref, s32[2,8]{1,0:T(2,128)S(1)} %get-tuple-element.16.ranks_ref, f32[8,72,128]{2,1,0:T(8,128)S(1)} %all_to_all.11.returned_ref, ...), custom_call_target="tpu_custom_call" | custom-call | tf_op jit(solution)/shard_map/gradient/pallas_call | solution.py:347
  35.2 0.1 collective-permute-start
  35.3 1.6 %collective-permute-start.1 = (f32[128,128]{1,0:T(8,128)S(1)}, f32[128,128]{1,0:T(8,128)S(1)}, u32[]{:S(2)}, u32[]{:S(2)}) collective-permute-start(f32[128,128]{1,0:T(8,128)S(1)} %get-tuple-element.20), channel_id=1, source_target_pairs={{0,2},{1,3},{2,0},{3,1},{4,6},{5,7},{6,4},{7,5},{8,10},{9,11},{10,... | collective-permute-start | bytes 196616 | tf_op jit(solution)/shard_map/ppermute | solution.py:359
  36.9 0.3 collective-permute-start.2
  37.2 0.7 %copy.9 = f32[1,1,256,128]{3,2,1,0:T(8,128)} copy(f32[1,1,256,128]{3,2,1,0:T(8,128)S(1)} %bitcast.8) | data formatting | bytes 262144
  37.8 0.0 collective-permute-done
  37.8 2.0 %collective-permute-done.1 = f32[128,128]{1,0:T(8,128)S(1)} collective-permute-done((f32[128,128]{1,0:T(8,128)S(1)}, f32[128,128]{1,0:T(8,128)S(1)}, u32[]{:S(2)}, u32[]{:S(2)}) %collective-permute-start.1) | collective-permute-done | bytes 65568 | tf_op jit(solution)/shard_map/ppermute | solution.py:359
  39.8 1.1 %collective-permute-done.2 = f32[128,128]{1,0:T(8,128)S(1)} collective-permute-done((f32[128,128]{1,0:T(8,128)S(1)}, f32[128,128]{1,0:T(8,128)S(1)}, u32[]{:S(2)}, u32[]{:S(2)}) %collective-permute-start.2) | collective-permute-done | bytes 65568 | tf_op jit(solution)/shard_map/ppermute | solution.py:359
  40.9 0.6 %add_add_fusion = f32[128,128]{1,0:T(8,128)} fusion(f32[128,128]{1,0:T(8,128)S(1)} %collective-permute-done.2, f32[128,128]{1,0:T(8,128)S(1)} %collective-permute-done.1, f32[128,128]{1,0:T(8,128)S(1)} %get-tuple-element.18, f32[128,128]{1,0:T(8,128)S(1)} %collective-permute-done), kind=kLoop, calls=%fused_computation | loop fusion | flops 49152 | bytes 327680 | tf_op jit(solution)/shard_map/add | solution.py:359
Async XLA Ops:
  0.6 19.9 %copy-start.2 = (f32[1,1,256,768]{3,2,1,0:T(8,128)S(1)}, f32[1,1,256,768]{3,2,1,0:T(8,128)}, u32[]{:S(2)}) copy-start(f32[1,1,256,768]{3,2,1,0:T(8,128)} %param.9) | copy-start | bytes 2359300
  2.5 18.0 %copy-start.3 = (f32[1,1,64,128]{3,2,1,0:T(8,128)S(1)}, f32[1,1,64,128]{3,2,1,0:T(8,128)}, u32[]{:S(2)}) copy-start(f32[1,1,64,128]{3,2,1,0:T(8,128)} %param.13) | copy-start | bytes 98308
  20.5 14.1 %copy-start = (f32[8,1,2,48,256]{4,3,2,1,0:T(8,128)S(1)}, f32[8,1,2,48,256]{4,3,2,1,0:T(8,128)}, u32[]{:S(2)}) copy-start(f32[8,1,2,48,256]{4,3,2,1,0:T(8,128)} %param.8) | copy-start | bytes 2359300
  21.5 13.1 %copy-start.1 = (f32[512,128]{1,0:T(8,128)S(1)}, f32[512,128]{1,0:T(8,128)}, u32[]{:S(2)}) copy-start(f32[512,128]{1,0:T(8,128)} %latent_ref.1) | copy-start | bytes 786436
  35.2 2.6 %collective-permute-start = (f32[128,128]{1,0:T(8,128)S(1)}, f32[128,128]{1,0:T(8,128)S(1)}, u32[]{:S(2)}, u32[]{:S(2)}) collective-permute-start(f32[128,128]{1,0:T(8,128)S(1)} %get-tuple-element.19), channel_id=1, source_target_pairs={{0,1},{1,0},{2,3},{3,2},{4,5},{5,4},{6,7},{7,6},{8,9},{9,8},{10,11... | collective-permute-start | bytes 196616 | tf_op jit(solution)/shard_map/ppermute | solution.py:359
  35.3 4.5 %collective-permute-start.1 = (f32[128,128]{1,0:T(8,128)S(1)}, f32[128,128]{1,0:T(8,128)S(1)}, u32[]{:S(2)}, u32[]{:S(2)}) collective-permute-start(f32[128,128]{1,0:T(8,128)S(1)} %get-tuple-element.20), channel_id=1, source_target_pairs={{0,2},{1,3},{2,0},{3,1},{4,6},{5,7},{6,4},{7,5},{8,10},{9,11},{10,... | collective-permute-start | bytes 196616 | tf_op jit(solution)/shard_map/ppermute | solution.py:359
  36.9 4.0 %collective-permute-start.2 = (f32[128,128]{1,0:T(8,128)S(1)}, f32[128,128]{1,0:T(8,128)S(1)}, u32[]{:S(2)}, u32[]{:S(2)}) collective-permute-start(f32[128,128]{1,0:T(8,128)S(1)} %get-tuple-element.21), channel_id=1, source_target_pairs={{0,3},{1,2},{2,1},{3,0},{4,7},{5,6},{6,5},{7,4},{8,11},{9,10},{10,... | collective-permute-start | bytes 196616 | tf_op jit(solution)/shard_map/ppermute | solution.py:359

commit v6 on v5

v6 whole, which is shorter than its diff:
```python
import functools

import jax
import jax.numpy as jnp
from jax import lax
from jax.experimental import pallas as pl
from jax.experimental.pallas import tpu as pltpu
from jax.sharding import PartitionSpec as P

F32 = jnp.float32
BF16 = jnp.bfloat16
VMEM = pl.BlockSpec(memory_space=pltpu.VMEM)
HBM = pl.BlockSpec(memory_space=pltpu.HBM)
MARK = 8


def split_rest(x):
    high = x.astype(BF16)
    return high, x - high.astype(F32)


def split(x):
    high, rest = split_rest(x)
    return high, rest.astype(BF16)


def product(a, b, contract=(1, 0)):
    return product_of(*split(a), b, contract)


def product_of(a_high, a_low, b, contract=(1, 0)):
    dims = (((contract[0],), (contract[1],)), ((), ()))
    b_high, b_low = split(b)
    both = lax.dot_general(a_high, jnp.concatenate([b_high, b_low], axis=1), dims, preferred_element_type=F32)
    width = b.shape[1]
    return both[:, :width] + both[:, width:] + lax.dot_general(a_low, b_high, dims, preferred_element_type=F32)


def repeat(count, body):
    if count == 1:
        body(0)
    else:
        pl.loop(0, count)(body)


def each(count, body):
    if count <= 16:
        for i in range(count):
            body(i)
    else:
        pl.loop(0, count)(body)


def params(arrays):
    held = sum(a.size * a.dtype.itemsize for a in arrays)
    return pltpu.CompilerParams(vmem_limit_bytes=min(4 * held + (4 << 20), 56 << 20))


def packed_rows(rank_pad):
    return rank_pad + rank_pad // 2


def lengthen(x, size):
    return jnp.concatenate([x, jnp.zeros((size - x.shape[0], x.shape[1]), x.dtype)], axis=0)


def scalar(ref, row, column):
    return ref[pl.ds(row, 1), column : column + 1][0, 0]


def block(refs, k):
    return refs[k] if len(refs) > 1 else refs[0].at[k]


def partner(refs, k):
    return lax.axis_index("col") ^ k if len(refs) > 1 else k


def stay(x):
    return pltpu.with_memory_space_constraint(x, pltpu.HBM)


def blocks_kernel(group, order_hbm, ranks_hbm, wells_hbm, latent_hbm, v_hbm, *refs):
    out_refs, (plan_ref, wells_out, held_ref, order_ref, ranks_ref, latent_ref, v_ref, sems) = refs[:-8], refs[-8:]
    local, rows, rank_pad, cells = v_ref.shape
    width = latent_ref.shape[1]
    small = [
        pltpu.make_async_copy(order_hbm, order_ref, sems.at[2 * local]),
        pltpu.make_async_copy(ranks_hbm, ranks_ref, sems.at[2 * local + 1]),
    ]
    later = [pltpu.make_async_copy(wells_hbm, wells_out, sems.at[2 * local + 2])]
    tiles = []
    for j in range(local):
        here = pl.ds(j * cells, cells)
        tiles.append(
            (
                pltpu.make_async_copy(v_hbm.at[:, j], v_ref.at[j], sems.at[2 * j]),
                pltpu.make_async_copy(latent_hbm.at[here], latent_ref.at[here], sems.at[2 * j + 1]),
            )
        )
    for copies in tiles:
        for copy in copies:
            copy.start()
    for copy in small + later:
        copy.start()
    for j in range(local):
        for copy in tiles[j]:
            copy.wait()

        def some(g):
            v_rows = v_ref[j, pl.ds(g * group, group)].reshape(group * rank_pad, cells)
            made = product(v_rows, latent_ref[j * cells : (j + 1) * cells, :])
            held_ref[j, pl.ds(g * group, group)] = made.reshape(group, rank_pad, width)

        repeat(rows // group, some)
    for copy in small:
        copy.wait()
    rank_index = lax.broadcasted_iota(jnp.int32, (rank_pad, width), 0)
    size = packed_rows(rank_pad)

    lane = lax.broadcasted_iota(jnp.int32, (1, plan_ref.shape[1]), 1)

    def place(k):
        q = order_ref[0, partner(out_refs, k)]
        plan = jnp.where(lane == 0, q, 0)
        for j in range(local):
            plan = jnp.where(lane == 1 + j, ranks_ref[j, q], plan)
        plan_ref[pl.ds(k, 1), :] = plan
        out_ref = block(out_refs, k)
        for pair in range(local // 2):
            left, right = 2 * pair, 2 * pair + 1
            cut = ranks_ref[left, q]
            first = jnp.where(rank_index < cut, held_ref[left, q], 0.0)
            second = jnp.where(rank_index < ranks_ref[right, q], held_ref[right, q], 0.0)
            base = pair * (size + MARK)
            out_ref[base : base + size, :] = lengthen(first, size) + pltpu.roll(lengthen(second, size), cut, 0)
            out_ref[base + size : base + size + MARK, :] = jnp.full((MARK, width), cut.astype(F32))

    each(rows, place)
    for copy in later:
        copy.wait()


def owner_kernel(chunk, rank_pad, count, wells_ref, u_ref, observed_ref, *refs):
    received_refs, field_ref, packed_refs, (stacked_ref, rows_ref) = (
        refs[:count],
        refs[count],
        refs[count + 1 : 2 * count + 1],
        refs[2 * count + 1 :],
    )
    depth, width = stacked_ref.shape
    wells = observed_ref.shape[0]
    cells = u_ref.shape[0]
    size = packed_rows(rank_pad)
    sources = depth // (received_refs[0].shape[-2] // (size + MARK) * 2 * rank_pad)
    pairs = depth // (sources * 2 * rank_pad)
    rank_index = lax.broadcasted_iota(jnp.int32, (rank_pad, width), 0)
    packed_index = lax.broadcasted_iota(jnp.int32, (size, width), 0)

    def first_rank(k, pair):
        return scalar(block(received_refs, k), pair * (size + MARK) + size, 0).astype(jnp.int32)

    def places(k, pair):
        left = pl.multiple_of((partner(received_refs, k) * pairs + pair) * 2 * rank_pad, 8)
        return pl.ds(left, rank_pad), pl.ds(pl.multiple_of(left + rank_pad, 8), rank_pad)

    def unpack(k):
        for pair in range(pairs):
            cut = first_rank(k, pair)
            both = block(received_refs, k)[pair * (size + MARK) : pair * (size + MARK) + size, :]
            left, right = places(k, pair)
            stacked_ref[left, :] = jnp.where(rank_index < cut, both[:rank_pad], 0.0)
            second = pltpu.roll(both, size - cut, 0)[:rank_pad]
            stacked_ref[right, :] = jnp.where(rank_index < size - cut, second, 0.0)

    def pack(k):
        for pair in range(pairs):
            cut = first_rank(k, pair)
            left, right = places(k, pair)
            first = lengthen(stacked_ref[left, :], size)
            second = pltpu.roll(lengthen(stacked_ref[right, :], size), cut, 0)
            here = slice(pair * size, (pair + 1) * size)
            block(packed_refs, k)[here, :] = jnp.where(packed_index < cut, first, second)

    each(sources, unpack)
    picked = jnp.where(lax.broadcasted_iota(jnp.int32, (cells, wells), 0) == wells_ref[...], 1.0, 0.0).astype(BF16)
    turned = (((0,), (0,)), ((), ()))

    def first(k):
        here = pl.ds(k * chunk, chunk)
        high, low = split(u_ref[:, here])
        part = product_of(high, low, stacked_ref[here, :])
        own = lax.dot_general(picked, high, turned, preferred_element_type=F32).astype(BF16)
        rows_ref[0:wells, here] = own
        rows_ref[wells : 2 * wells, here] = own
        rows_ref[2 * wells :, here] = lax.dot_general(picked, low, turned, preferred_element_type=F32).astype(BF16)
        if depth == chunk:
            field_ref[...] = part
        else:

            @pl.when(k == 0)
            def _():
                field_ref[...] = part

            @pl.when(k > 0)
            def _():
                field_ref[...] += part

    repeat(depth // chunk, first)
    high, rest = split_rest(field_ref[...])
    middle, rest = split_rest(rest)
    parts = jnp.concatenate([high, middle, rest.astype(BF16)], axis=1)
    parts = lax.dot_general(picked, parts, turned, preferred_element_type=F32)
    expo = jnp.exp(parts[:, :width] + parts[:, width : 2 * width] + parts[:, 2 * width :])
    weighted = (expo - observed_ref[...]) * expo / 0.25
    high, low = split(weighted)
    below = jnp.concatenate([high, low, high], axis=0)

    def back(k):
        here = pl.ds(k * chunk, chunk)
        stacked_ref[here, :] = lax.dot_general(rows_ref[:, here], below, turned, preferred_element_type=F32)

    repeat(depth // chunk, back)
    each(sources, pack)


def gradient_kernel(group, axis, turn, count, plan_ref, v_ref, latent_ref, *refs):
    returned_refs, out_refs, (ordered_ref, total_ref) = refs[:count], refs[count:-2], refs[-2:]
    rows, local, rank_pad, cells = v_ref.shape
    width = latent_ref.shape[1]
    rank_index = lax.broadcasted_iota(jnp.int32, (rank_pad, width), 0)

    packed = packed_rows(rank_pad)

    def place(k):
        q = scalar(plan_ref, k, 0)
        for pair in range(local // 2):
            left, right = 2 * pair, 2 * pair + 1
            cut = scalar(plan_ref, k, 1 + left)
            both = block(returned_refs, k)[pair * packed : (pair + 1) * packed, :]
            ordered_ref[left, q] = jnp.where(rank_index < cut, both[:rank_pad], 0.0)
            second = pltpu.roll(both, packed - cut, 0)[:rank_pad]
            ordered_ref[right, q] = jnp.where(rank_index < scalar(plan_ref, k, 1 + right), second, 0.0)

    each(rows, place)

    def some(g):
        for j in range(local):
            v_rows = v_ref[pl.ds(g * group, group), j].reshape(group * rank_pad, cells)
            part = product(v_rows, ordered_ref[j, pl.ds(g * group, group)].reshape(group * rank_pad, width), (0, 0))
            here = slice(j * cells, (j + 1) * cells)
            if rows == group:
                total_ref[here, :] = part
            else:

                @pl.when(g == 0)
                def _():
                    total_ref[here, :] = part

                @pl.when(g > 0)
                def _():
                    total_ref[here, :] += part

    repeat(rows // group, some)
    me = lax.axis_index(axis)
    size = out_refs[0].shape[0]
    for step, out_ref in enumerate(out_refs):
        there = pl.ds(pl.multiple_of(turn(me, step) * size, size), size)
        if step == 0:
            out_ref[...] = total_ref[there, :] + latent_ref[there, :]
        else:
            out_ref[...] = total_ref[there, :]


def exchange(arrays):
    if len(arrays) == 1:
        return [lax.all_to_all(arrays[0], "col", split_axis=0, concat_axis=0, tiled=True)]
    count = len(arrays)
    return [arrays[0]] + [lax.ppermute(arrays[k], "col", [(i, i ^ k) for i in range(count)]) for k in range(1, count)]


def on_device(n_row, latent, v_basis, u_basis, ranks, slot_row, wells, observed):
    rows, _, local, rank_pad, cells = v_basis.shape
    width = latent.shape[1]
    v_rows = v_basis[:, 0]
    u_owned = u_basis[0, 0]
    observed_here = observed[0, 0]
    well_count = observed_here.shape[0]
    pairs, packed = local // 2, packed_rows(rank_pad)
    depth = u_owned.shape[1]
    group = 8 if rows % 8 == 0 else 1
    chunk = 768 if depth % 768 == 0 else depth
    direct = rows <= 8 and rows & (rows - 1) == 0 and rows > 1
    count = rows if direct else 1
    far = [0] + sorted(range(1, count), key=lambda k: (-k.bit_length(), -(k & 1), -k))

    def carried(size):
        shape = (size, width) if direct else (rows, size, width)
        return [jax.ShapeDtypeStruct(shape, F32)] * count

    def sorted_refs(kernel, before, lists):
        def run(*refs):
            refs = list(refs)
            for start in (before + at for at in lists):
                moved = refs[start : start + count]
                refs[start : start + count] = [moved[far.index(k)] for k in range(count)]
            kernel(*refs)

        return run

    outs = pl.pallas_call(
        functools.partial(blocks_kernel, group),
        out_shape=(
            *carried(pairs * (packed + MARK)),
            jax.ShapeDtypeStruct((rows, 128), jnp.int32),
            jax.ShapeDtypeStruct((1, well_count), jnp.int32),
        ),
        in_specs=[HBM] * 5,
        out_specs=(VMEM,) * (count + 2),
        scratch_shapes=[
            pltpu.VMEM((local, rows, rank_pad, width), F32),
            pltpu.SMEM(slot_row.shape, jnp.int32),
            pltpu.SMEM((local, rows), jnp.int32),
            pltpu.VMEM(latent.shape, F32),
            pltpu.VMEM((local, rows, rank_pad, cells), F32),
            pltpu.SemaphoreType.DMA((2 * local + 3,)),
        ],
        compiler_params=params([latent, v_rows]),
        name="blocks",
    )(stay(slot_row), stay(ranks[:, 0].T), stay(wells[0]), stay(latent), stay(v_rows))
    sent, (plan, wells_here) = outs[:count], outs[count:]
    received = exchange(sent)
    field, *adjoint = pl.pallas_call(
        sorted_refs(functools.partial(owner_kernel, chunk, rank_pad, count), 3, [0]),
        out_shape=(pltpu.VMEM((cells, width), F32), *carried(pairs * packed)),
        in_specs=[VMEM] * (3 + count),
        out_specs=(VMEM,) * (1 + count),
        scratch_shapes=[pltpu.VMEM((depth, width), F32), pltpu.VMEM((3 * well_count, depth), BF16)],
        compiler_params=params([u_owned, u_owned, observed_here]),
        name="owner",
    )(wells_here, u_owned, observed_here, *[received[k] for k in far])
    returned = exchange(adjoint)
    paired = n_row & (n_row - 1) == 0

    def turn(index, step):
        return index ^ step if paired else lax.rem(index + step, n_row)

    size = local * cells // n_row
    parts = pl.pallas_call(
        sorted_refs(functools.partial(gradient_kernel, group, "row", turn, count), 3, [0]),
        out_shape=[jax.ShapeDtypeStruct((size, width), F32)] * n_row,
        in_specs=[VMEM] * (3 + count),
        out_specs=[VMEM] * n_row,
        scratch_shapes=[pltpu.VMEM((local, rows, rank_pad, width), F32), pltpu.VMEM((local * cells, width), F32)],
        compiler_params=params([u_owned, v_rows, latent]),
        name="gradient",
    )(plan, v_rows, latent, *[returned[k] for k in far])
    gradient = parts[0]
    for step in range(1, n_row):
        pairs_of = [(i, i ^ step if paired else (i + step) % n_row) for i in range(n_row)]
        gradient = gradient + lax.ppermute(parts[step], "row", pairs_of)
    return field[None, None], gradient


def solution(mesh):
    placed = (
        P("col", None),
        P(None, "row", "col", None, None),
        P("col", "row", None, None),
        P(None, "row", "col"),
        P("row", None),
        P("col", "row", None),
        P("col", "row", None, None),
    )
    return jax.shard_map(
        functools.partial(on_device, mesh.shape["row"]),
        mesh=mesh,
        in_specs=placed,
        out_specs=(P("col", "row", None, None), P(("col", "row"), None)),
        check_vma=False,
    )
```

time: 41.8 us -> 40.2 us (0.962)
  blocking collectives: 31.1 us -> 0 us
  starting transfers between devices: 1.93 us -> 24 us
  waiting for transfers between devices: 3.08 us -> 10.6 us
    all_to_all x2 -> x0, blocking collectives: 31.1 us -> none  [the longest x1 18 us: on_device(): lax.all_to_all(sent, 'col', split_axis=0, concat_axis=0, tiled=True)]
    ppermute x3 -> x17, starting transfers between devices: 1.93 us -> 24 us  [the longest x14 22 us: exchange(): lax.ppermute(arrays[k], 'col', [(i, i ^ k) for i in range(count)])]
    ppermute x3 -> x17, waiting for transfers between devices: 3.08 us -> 10.6 us  [the longest x14 7.48 us: exchange(): lax.ppermute(arrays[k], 'col', [(i, i ^ k) for i in range(count)])]
  transfers between devices with their start and end apart: 3 -> 17, of which waited for: 2 -> 10; matrix products, arithmetic and copies ran while one was open for 2% -> 2% of each run, Pallas kernels for 0% -> 0%
where the time goes in v6:
time: 40.2 us; the launch traced here: 40 us
  starting transfers between devices  24 us (60%)
  waiting for transfers between devices  10.6 us (26%)
  Pallas kernels  3.5 us (9%)
  between operations  0.71 us (2%)
  local copies, waits for them, and re-layouts  0.67 us (2%)
  other arithmetic  0.64 us (2%)
    ppermute x14, starting transfers between devices, exchange(): lax.ppermute(arrays[k], 'col', [(i, i ^ k) for i in range(count)])  22 us
    ppermute x14, waiting for transfers between devices, exchange(): lax.ppermute(arrays[k], 'col', [(i, i ^ k) for i in range(count)])  7.48 us
    ppermute x3, waiting for transfers between devices, on_device(): gradient = gradient + lax.ppermute(parts[step], 'row', pairs_of)  3.08 us
    ppermute x3, starting transfers between devices, on_device(): gradient = gradient + lax.ppermute(parts[step], 'row', pairs_of)  1.93 us
    pallas_call x1, Pallas kernels, on_device(): pl.pallas_call(functools.partial(blocks_kernel, group), out_shape=(*carri...  1.86 us
    pallas_call x1, Pallas kernels, on_device(): pl.pallas_call(sorted_refs(functools.partial(owner_kernel, chunk, rank_pa...  1.02 us
  transfers between devices with their start and end apart: 17, of which 10 were waited for; matrix products, arithmetic and copies ran while one was open for 2% of the time, Pallas kernels for 0%

profile of v6, /device:TPU:0, one launch (start us, length us, event | category | flops | bytes accessed | tf_op | source)
XLA Modules:
  0.0 40.0 jit_solution(11958296874623343965)
XLA Ops:
  0.7 1.9 %blocks.1 = (f32[80,128]{1,0:T(8,128)S(1)}, f32[80,128]{1,0:T(8,128)S(1)}, f32[80,128]{1,0:T(8,128)S(1)}, f32[80,128]{1,0:T(8,128)S(1)}, f32[80,128]{1,0:T(8,128...) custom-call(s32[1,8]{1,0:T(1,128)} %order_hbm.1, ...), custom_call_target="tpu_custom_call" | custom-call | tf_op jit(solution)/shard_map/blocks/pallas_call | solution.py:311
  2.5 0.0 copy-start
  2.5 6.1 %collective-permute-start = (f32[80,128]{1,0:T(8,128)S(1)}, f32[80,128]{1,0:T(8,128)S(1)}, u32[]{:S(2)}, u32[]{:S(2)}) collective-permute-start(f32[80,128]{1,0:T(8,128)S(1)} %get-tuple-element.27), channel_id=1, source_target_pairs={{0,28},{4,24},{8,20},{12,16},{16,12},{20,8},{24,4},{28,0},{1,29},{... | collective-permute-start | bytes 122888 | tf_op jit(solution)/shard_map/ppermute | solution.py:279
  8.6 0.0 collective-permute-start.1
  8.6 1.9 %collective-permute-start.2 = (f32[80,128]{1,0:T(8,128)S(1)}, f32[80,128]{1,0:T(8,128)S(1)}, u32[]{:S(2)}, u32[]{:S(2)}) collective-permute-start(f32[80,128]{1,0:T(8,128)S(1)} %get-tuple-element.29), channel_id=1, source_target_pairs={{0,24},{4,28},{8,16},{12,20},{16,8},{20,12},{24,0},{28,4},{1,25},{... | collective-permute-start | bytes 122888 | tf_op jit(solution)/shard_map/ppermute | solution.py:279
  10.5 1.0 %collective-permute-start.3 = (f32[80,128]{1,0:T(8,128)S(1)}, f32[80,128]{1,0:T(8,128)S(1)}, u32[]{:S(2)}, u32[]{:S(2)}) collective-permute-start(f32[80,128]{1,0:T(8,128)S(1)} %get-tuple-element.30), channel_id=1, source_target_pairs={{0,16},{4,20},{8,24},{12,28},{16,0},{20,4},{24,8},{28,12},{1,17},{... | collective-permute-start | bytes 122888 | tf_op jit(solution)/shard_map/ppermute | solution.py:279
  11.5 1.9 %collective-permute-start.4 = (f32[80,128]{1,0:T(8,128)S(1)}, f32[80,128]{1,0:T(8,128)S(1)}, u32[]{:S(2)}, u32[]{:S(2)}) collective-permute-start(f32[80,128]{1,0:T(8,128)S(1)} %get-tuple-element.31), channel_id=1, source_target_pairs={{0,12},{4,8},{8,4},{12,0},{16,28},{20,24},{24,20},{28,16},{1,13},{... | collective-permute-start | bytes 122888 | tf_op jit(solution)/shard_map/ppermute | solution.py:279
  13.3 1.1 %collective-permute-start.5 = (f32[80,128]{1,0:T(8,128)S(1)}, f32[80,128]{1,0:T(8,128)S(1)}, u32[]{:S(2)}, u32[]{:S(2)}) collective-permute-start(f32[80,128]{1,0:T(8,128)S(1)} %get-tuple-element.32), channel_id=1, source_target_pairs={{0,8},{4,12},{8,0},{12,4},{16,24},{20,28},{24,16},{28,20},{1,9},{5... | collective-permute-start | bytes 122888 | tf_op jit(solution)/shard_map/ppermute | solution.py:279
  14.5 1.3 %collective-permute-done.1.refs_5_ = f32[80,128]{1,0:T(8,128)S(1)} collective-permute-done((f32[80,128]{1,0:T(8,128)S(1)}, f32[80,128]{1,0:T(8,128)S(1)}, u32[]{:S(2)}, u32[]{:S(2)}) %collective-permute-start.1) | collective-permute-done | bytes 40992 | tf_op jit(solution)/shard_map/ppermute | solution.py:279
  15.8 0.2 collective-permute-done.3.refs_7_
  16.0 1.2 %collective-permute-done.4.refs_8_ = f32[80,128]{1,0:T(8,128)S(1)} collective-permute-done((f32[80,128]{1,0:T(8,128)S(1)}, f32[80,128]{1,0:T(8,128)S(1)}, u32[]{:S(2)}, u32[]{:S(2)}) %collective-permute-start.4) | collective-permute-done | bytes 40992 | tf_op jit(solution)/shard_map/ppermute | solution.py:279
  17.2 0.2 collective-permute-done.5.refs_9_
  17.3 2.5 %collective-permute-done.6.refs_10_ = f32[80,128]{1,0:T(8,128)S(1)} collective-permute-done((f32[80,128]{1,0:T(8,128)S(1)}, f32[80,128]{1,0:T(8,128)S(1)}, u32[]{:S(2)}, u32[]{:S(2)}) %collective-permute-start.6) | collective-permute-done | bytes 40992 | tf_op jit(solution)/shard_map/ppermute | solution.py:279
  19.8 1.0 %owner.1 = (f32[256,128]{1,0:T(8,128)S(1)}, f32[72,128]{1,0:T(8,128)S(1)}, f32[72,128]{1,0:T(8,128)S(1)}, f32[72,128]{1,0:T(8,128)S(1)}, f32[72,128]{1,0:T(8,128...) custom-call(s32[1,64]{1,0:T(1,128)S(1)} %get-tuple-element.25.refs_0_, ...), custom_call_target="tpu_custom_call" | custom-call | tf_op jit(solution)/shard_map/owner/pallas_call | solution.py:333
  20.8 1.8 %collective-permute-start.7 = (f32[72,128]{1,0:T(8,128)S(1)}, f32[72,128]{1,0:T(8,128)S(1)}, u32[]{:S(2)}, u32[]{:S(2)}) collective-permute-start(f32[72,128]{1,0:T(8,128)S(1)} %get-tuple-element.37), channel_id=1, source_target_pairs={{0,28},{4,24},{8,20},{12,16},{16,12},{20,8},{24,4},{28,0},{1,29},{... | collective-permute-start | bytes 110600 | tf_op jit(solution)/shard_map/ppermute | solution.py:279
  22.6 0.2 collective-permute-start.8
  22.8 2.5 %collective-permute-start.9 = (f32[72,128]{1,0:T(8,128)S(1)}, f32[72,128]{1,0:T(8,128)S(1)}, u32[]{:S(2)}, u32[]{:S(2)}) collective-permute-start(f32[72,128]{1,0:T(8,128)S(1)} %get-tuple-element.39), channel_id=1, source_target_pairs={{0,24},{4,28},{8,16},{12,20},{16,8},{20,12},{24,0},{28,4},{1,25},{... | collective-permute-start | bytes 110600 | tf_op jit(solution)/shard_map/ppermute | solution.py:279
  25.3 2.4 %collective-permute-start.10 = (f32[72,128]{1,0:T(8,128)S(1)}, f32[72,128]{1,0:T(8,128)S(1)}, u32[]{:S(2)}, u32[]{:S(2)}) collective-permute-start(f32[72,128]{1,0:T(8,128)S(1)} %get-tuple-element.40), channel_id=1, source_target_pairs={{0,16},{4,20},{8,24},{12,28},{16,0},{20,4},{24,8},{28,12},{1,17},{... | collective-permute-start | bytes 110600 | tf_op jit(solution)/shard_map/ppermute | solution.py:279
  27.7 0.1 collective-permute-start.11
  27.8 0.2 collective-permute-done.7.refs_4_
  28.0 1.1 %collective-permute-start.12 = (f32[72,128]{1,0:T(8,128)S(1)}, f32[72,128]{1,0:T(8,128)S(1)}, u32[]{:S(2)}, u32[]{:S(2)}) collective-permute-start(f32[72,128]{1,0:T(8,128)S(1)} %get-tuple-element.42), channel_id=1, source_target_pairs={{0,8},{4,12},{8,0},{12,4},{16,24},{20,28},{24,16},{28,20},{1,9},{5... | collective-permute-start | bytes 110600 | tf_op jit(solution)/shard_map/ppermute | solution.py:279
  29.1 2.0 %collective-permute-start.13 = (f32[72,128]{1,0:T(8,128)S(1)}, f32[72,128]{1,0:T(8,128)S(1)}, u32[]{:S(2)}, u32[]{:S(2)}) collective-permute-start(f32[72,128]{1,0:T(8,128)S(1)} %get-tuple-element.43), channel_id=1, source_target_pairs={{0,4},{4,0},{8,12},{12,8},{16,20},{20,16},{24,28},{28,24},{1,5},{5... | collective-permute-start | bytes 110600 | tf_op jit(solution)/shard_map/ppermute | solution.py:279
  31.2 1.4 %collective-permute-done.11.refs_8_ = f32[72,128]{1,0:T(8,128)S(1)} collective-permute-done((f32[72,128]{1,0:T(8,128)S(1)}, f32[72,128]{1,0:T(8,128)S(1)}, u32[]{:S(2)}, u32[]{:S(2)}) %collective-permute-start.11) | collective-permute-done | bytes 36896 | tf_op jit(solution)/shard_map/ppermute | solution.py:279
  32.5 0.6 %collective-permute-done.13.refs_10_ = f32[72,128]{1,0:T(8,128)S(1)} collective-permute-done((f32[72,128]{1,0:T(8,128)S(1)}, f32[72,128]{1,0:T(8,128)S(1)}, u32[]{:S(2)}, u32[]{:S(2)}) %collective-permute-start.13) | collective-permute-done | bytes 36896 | tf_op jit(solution)/shard_map/ppermute | solution.py:279
  33.1 0.6 %gradient.1 = (f32[128,128]{1,0:T(8,128)S(1)}, f32[128,128]{1,0:T(8,128)S(1)}, f32[128,128]{1,0:T(8,128)S(1)}, f32[128,128]{1,0:T(8,128)S(1)}) custom-call(s32[8,128]{1,0:T(8,128)S(1)} %get-tuple-element.35.refs_0_, f32[8,2,48,256]{3,2,1,0:T(8,128)S(1)} %bitcast.10, f32[512,128]{1,0:T(8,128)S(1)} %copy-done.1, f32[72,128]{1,0:T(8,128)S(1)} %get-tuple-element.36.refs_3_, ...), custom_call_target="tpu_custom_call" | custom-call | tf_op jit(solution)/shard_map/gradient/pallas_call | solution.py:349
  33.7 0.1 collective-permute-start.14
  33.8 1.6 %collective-permute-start.15 = (f32[128,128]{1,0:T(8,128)S(1)}, f32[128,128]{1,0:T(8,128)S(1)}, u32[]{:S(2)}, u32[]{:S(2)}) collective-permute-start(f32[128,128]{1,0:T(8,128)S(1)} %get-tuple-element.46), channel_id=1, source_target_pairs={{0,2},{1,3},{2,0},{3,1},{4,6},{5,7},{6,4},{7,5},{8,10},{9,11},{10,... | collective-permute-start | bytes 196616 | tf_op jit(solution)/shard_map/ppermute | solution.py:361
  35.4 0.3 collective-permute-start.16
  35.7 0.7 %copy.9 = f32[1,1,256,128]{3,2,1,0:T(8,128)} copy(f32[1,1,256,128]{3,2,1,0:T(8,128)S(1)} %bitcast.8) | data formatting | bytes 262144
  36.3 2.0 %collective-permute-done.15 = f32[128,128]{1,0:T(8,128)S(1)} collective-permute-done((f32[128,128]{1,0:T(8,128)S(1)}, f32[128,128]{1,0:T(8,128)S(1)}, u32[]{:S(2)}, u32[]{:S(2)}) %collective-permute-start.15) | collective-permute-done | bytes 65568 | tf_op jit(solution)/shard_map/ppermute | solution.py:361
  38.3 1.1 %collective-permute-done.16 = f32[128,128]{1,0:T(8,128)S(1)} collective-permute-done((f32[128,128]{1,0:T(8,128)S(1)}, f32[128,128]{1,0:T(8,128)S(1)}, u32[]{:S(2)}, u32[]{:S(2)}) %collective-permute-start.16) | collective-permute-done | bytes 65568 | tf_op jit(solution)/shard_map/ppermute | solution.py:361
  39.4 0.6 %add_add_fusion = f32[128,128]{1,0:T(8,128)} fusion(f32[128,128]{1,0:T(8,128)S(1)} %collective-permute-done.16, f32[128,128]{1,0:T(8,128)S(1)} %collective-permute-done.15, f32[128,128]{1,0:T(8,128)S(1)} %get-tuple-element.44, f32[128,128]{1,0:T(8,128)S(1)} %collective-permute-done.14), kind=kLoop, calls=%fused_computation | loop fusion | flops 49152 | bytes 327680 | tf_op jit(solution)/shard_map/add | solution.py:361
  (15 shorter events, 0.0 us)
Async XLA Ops:
  0.6 19.2 %copy-start.2 = (f32[1,1,256,768]{3,2,1,0:T(8,128)S(1)}, f32[1,1,256,768]{3,2,1,0:T(8,128)}, u32[]{:S(2)}) copy-start(f32[1,1,256,768]{3,2,1,0:T(8,128)} %param.9) | copy-start | bytes 2359300
  0.6 19.2 %copy-start.3 = (f32[1,1,64,128]{3,2,1,0:T(8,128)S(1)}, f32[1,1,64,128]{3,2,1,0:T(8,128)}, u32[]{:S(2)}) copy-start(f32[1,1,64,128]{3,2,1,0:T(8,128)} %param.13) | copy-start | bytes 98308
  2.5 30.6 %copy-start = (f32[8,1,2,48,256]{4,3,2,1,0:T(8,128)S(1)}, f32[8,1,2,48,256]{4,3,2,1,0:T(8,128)}, u32[]{:S(2)}) copy-start(f32[8,1,2,48,256]{4,3,2,1,0:T(8,128)} %param.8) | copy-start | bytes 2359300
  2.5 10.8 %collective-permute-start = (f32[80,128]{1,0:T(8,128)S(1)}, f32[80,128]{1,0:T(8,128)S(1)}, u32[]{:S(2)}, u32[]{:S(2)}) collective-permute-start(f32[80,128]{1,0:T(8,128)S(1)} %get-tuple-element.27), channel_id=1, source_target_pairs={{0,28},{4,24},{8,20},{12,16},{16,12},{20,8},{24,4},{28,0},{1,29},{... | collective-permute-start | bytes 122888 | tf_op jit(solution)/shard_map/ppermute | solution.py:279
  8.6 7.2 %collective-permute-start.1 = (f32[80,128]{1,0:T(8,128)S(1)}, f32[80,128]{1,0:T(8,128)S(1)}, u32[]{:S(2)}, u32[]{:S(2)}) collective-permute-start(f32[80,128]{1,0:T(8,128)S(1)} %get-tuple-element.28), channel_id=1, source_target_pairs={{0,20},{4,16},{8,28},{12,24},{16,4},{20,0},{24,12},{28,8},{1,21},{... | collective-permute-start | bytes 122888 | tf_op jit(solution)/shard_map/ppermute | solution.py:279
  8.6 7.2 %collective-permute-start.2 = (f32[80,128]{1,0:T(8,128)S(1)}, f32[80,128]{1,0:T(8,128)S(1)}, u32[]{:S(2)}, u32[]{:S(2)}) collective-permute-start(f32[80,128]{1,0:T(8,128)S(1)} %get-tuple-element.29), channel_id=1, source_target_pairs={{0,24},{4,28},{8,16},{12,20},{16,8},{20,12},{24,0},{28,4},{1,25},{... | collective-permute-start | bytes 122888 | tf_op jit(solution)/shard_map/ppermute | solution.py:279
  10.5 5.6 %collective-permute-start.3 = (f32[80,128]{1,0:T(8,128)S(1)}, f32[80,128]{1,0:T(8,128)S(1)}, u32[]{:S(2)}, u32[]{:S(2)}) collective-permute-start(f32[80,128]{1,0:T(8,128)S(1)} %get-tuple-element.30), channel_id=1, source_target_pairs={{0,16},{4,20},{8,24},{12,28},{16,0},{20,4},{24,8},{28,12},{1,17},{... | collective-permute-start | bytes 122888 | tf_op jit(solution)/shard_map/ppermute | solution.py:279
  11.5 5.7 %collective-permute-start.4 = (f32[80,128]{1,0:T(8,128)S(1)}, f32[80,128]{1,0:T(8,128)S(1)}, u32[]{:S(2)}, u32[]{:S(2)}) collective-permute-start(f32[80,128]{1,0:T(8,128)S(1)} %get-tuple-element.31), channel_id=1, source_target_pairs={{0,12},{4,8},{8,4},{12,0},{16,28},{20,24},{24,20},{28,16},{1,13},{... | collective-permute-start | bytes 122888 | tf_op jit(solution)/shard_map/ppermute | solution.py:279
  13.3 4.0 %collective-permute-start.5 = (f32[80,128]{1,0:T(8,128)S(1)}, f32[80,128]{1,0:T(8,128)S(1)}, u32[]{:S(2)}, u32[]{:S(2)}) collective-permute-start(f32[80,128]{1,0:T(8,128)S(1)} %get-tuple-element.32), channel_id=1, source_target_pairs={{0,8},{4,12},{8,0},{12,4},{16,24},{20,28},{24,16},{28,20},{1,9},{5... | collective-permute-start | bytes 122888 | tf_op jit(solution)/shard_map/ppermute | solution.py:279
  15.8 4.0 %collective-permute-start.6 = (f32[80,128]{1,0:T(8,128)S(1)}, f32[80,128]{1,0:T(8,128)S(1)}, u32[]{:S(2)}, u32[]{:S(2)}) collective-permute-start(f32[80,128]{1,0:T(8,128)S(1)} %get-tuple-element.33), channel_id=1, source_target_pairs={{0,4},{4,0},{8,12},{12,8},{16,20},{20,16},{24,28},{28,24},{1,5},{5... | collective-permute-start | bytes 122888 | tf_op jit(solution)/shard_map/ppermute | solution.py:279
  19.8 13.3 %copy-start.1 = (f32[512,128]{1,0:T(8,128)S(1)}, f32[512,128]{1,0:T(8,128)}, u32[]{:S(2)}) copy-start(f32[512,128]{1,0:T(8,128)} %refs_2_.1) | copy-start | bytes 786436
  20.8 7.1 %collective-permute-start.7 = (f32[72,128]{1,0:T(8,128)S(1)}, f32[72,128]{1,0:T(8,128)S(1)}, u32[]{:S(2)}, u32[]{:S(2)}) collective-permute-start(f32[72,128]{1,0:T(8,128)S(1)} %get-tuple-element.37), channel_id=1, source_target_pairs={{0,28},{4,24},{8,20},{12,16},{16,12},{20,8},{24,4},{28,0},{1,29},{... | collective-permute-start | bytes 110600 | tf_op jit(solution)/shard_map/ppermute | solution.py:279
  22.6 6.5 %collective-permute-start.8 = (f32[72,128]{1,0:T(8,128)S(1)}, f32[72,128]{1,0:T(8,128)S(1)}, u32[]{:S(2)}, u32[]{:S(2)}) collective-permute-start(f32[72,128]{1,0:T(8,128)S(1)} %get-tuple-element.38), channel_id=1, source_target_pairs={{0,20},{4,16},{8,28},{12,24},{16,4},{20,0},{24,12},{28,8},{1,21},{... | collective-permute-start | bytes 110600 | tf_op jit(solution)/shard_map/ppermute | solution.py:279
  22.8 8.3 %collective-permute-start.9 = (f32[72,128]{1,0:T(8,128)S(1)}, f32[72,128]{1,0:T(8,128)S(1)}, u32[]{:S(2)}, u32[]{:S(2)}) collective-permute-start(f32[72,128]{1,0:T(8,128)S(1)} %get-tuple-element.39), channel_id=1, source_target_pairs={{0,24},{4,28},{8,16},{12,20},{16,8},{20,12},{24,0},{28,4},{1,25},{... | collective-permute-start | bytes 110600 | tf_op jit(solution)/shard_map/ppermute | solution.py:279
  25.3 5.9 %collective-permute-start.10 = (f32[72,128]{1,0:T(8,128)S(1)}, f32[72,128]{1,0:T(8,128)S(1)}, u32[]{:S(2)}, u32[]{:S(2)}) collective-permute-start(f32[72,128]{1,0:T(8,128)S(1)} %get-tuple-element.40), channel_id=1, source_target_pairs={{0,16},{4,20},{8,24},{12,28},{16,0},{20,4},{24,8},{28,12},{1,17},{... | collective-permute-start | bytes 110600 | tf_op jit(solution)/shard_map/ppermute | solution.py:279
  27.7 4.9 %collective-permute-start.11 = (f32[72,128]{1,0:T(8,128)S(1)}, f32[72,128]{1,0:T(8,128)S(1)}, u32[]{:S(2)}, u32[]{:S(2)}) collective-permute-start(f32[72,128]{1,0:T(8,128)S(1)} %get-tuple-element.41), channel_id=1, source_target_pairs={{0,12},{4,8},{8,4},{12,0},{16,28},{20,24},{24,20},{28,16},{1,13},{... | collective-permute-start | bytes 110600 | tf_op jit(solution)/shard_map/ppermute | solution.py:279
  28.0 4.5 %collective-permute-start.12 = (f32[72,128]{1,0:T(8,128)S(1)}, f32[72,128]{1,0:T(8,128)S(1)}, u32[]{:S(2)}, u32[]{:S(2)}) collective-permute-start(f32[72,128]{1,0:T(8,128)S(1)} %get-tuple-element.42), channel_id=1, source_target_pairs={{0,8},{4,12},{8,0},{12,4},{16,24},{20,28},{24,16},{28,20},{1,9},{5... | collective-permute-start | bytes 110600 | tf_op jit(solution)/shard_map/ppermute | solution.py:279
  29.1 4.0 %collective-permute-start.13 = (f32[72,128]{1,0:T(8,128)S(1)}, f32[72,128]{1,0:T(8,128)S(1)}, u32[]{:S(2)}, u32[]{:S(2)}) collective-permute-start(f32[72,128]{1,0:T(8,128)S(1)} %get-tuple-element.43), channel_id=1, source_target_pairs={{0,4},{4,0},{8,12},{12,8},{16,20},{20,16},{24,28},{28,24},{1,5},{5... | collective-permute-start | bytes 110600 | tf_op jit(solution)/shard_map/ppermute | solution.py:279
  33.7 2.6 %collective-permute-start.14 = (f32[128,128]{1,0:T(8,128)S(1)}, f32[128,128]{1,0:T(8,128)S(1)}, u32[]{:S(2)}, u32[]{:S(2)}) collective-permute-start(f32[128,128]{1,0:T(8,128)S(1)} %get-tuple-element.45), channel_id=1, source_target_pairs={{0,1},{1,0},{2,3},{3,2},{4,5},{5,4},{6,7},{7,6},{8,9},{9,8},{10,11... | collective-permute-start | bytes 196616 | tf_op jit(solution)/shard_map/ppermute | solution.py:361
  33.8 4.5 %collective-permute-start.15 = (f32[128,128]{1,0:T(8,128)S(1)}, f32[128,128]{1,0:T(8,128)S(1)}, u32[]{:S(2)}, u32[]{:S(2)}) collective-permute-start(f32[128,128]{1,0:T(8,128)S(1)} %get-tuple-element.46), channel_id=1, source_target_pairs={{0,2},{1,3},{2,0},{3,1},{4,6},{5,7},{6,4},{7,5},{8,10},{9,11},{10,... | collective-permute-start | bytes 196616 | tf_op jit(solution)/shard_map/ppermute | solution.py:361
  35.4 4.0 %collective-permute-start.16 = (f32[128,128]{1,0:T(8,128)S(1)}, f32[128,128]{1,0:T(8,128)S(1)}, u32[]{:S(2)}, u32[]{:S(2)}) collective-permute-start(f32[128,128]{1,0:T(8,128)S(1)} %get-tuple-element.47), channel_id=1, source_target_pairs={{0,3},{1,2},{2,1},{3,0},{4,7},{5,6},{6,5},{7,4},{8,11},{9,10},{10,... | collective-permute-start | bytes 196616 | tf_op jit(solution)/shard_map/ppermute | solution.py:361

commit v7 on v6

--- a/solution.py
+++ b/solution.py
@@ -292,7 +292,7 @@
     chunk = 768 if depth % 768 == 0 else depth
     direct = rows <= 8 and rows & (rows - 1) == 0 and rows > 1
     count = rows if direct else 1
-    far = [0] + sorted(range(1, count), key=lambda k: (-k.bit_length(), -(k & 1), -k))
+    far = [0] + sorted(range(1, count), key=lambda k: (-k.bit_length(), (k & 1) ^ (k.bit_length() == 2), k))
 
     def carried(size):
         shape = (size, width) if direct else (rows, size, width)

time: 40.2 us -> 39.4 us (0.980)
  waiting for transfers between devices: 10.6 us -> 9.02 us
  starting transfers between devices: 24 us -> 24.7 us
    ppermute x14, waiting for transfers between devices: 7.48 us -> 5.94 us  [exchange(): lax.ppermute(arrays[k], 'col', [(i, i ^ k) for i in range(count)])]
    ppermute x14, starting transfers between devices: 22 us -> 22.7 us  [exchange(): lax.ppermute(arrays[k], 'col', [(i, i ^ k) for i in range(count)])]
  transfers between devices with their start and end apart: 17 -> 17, of which waited for: 10 -> 8; matrix products, arithmetic and copies ran while one was open for 2% -> 2% of each run, Pallas kernels for 0% -> 0%
where the time goes in v7:
time: 39.4 us; the launch traced here: 39.2 us
  starting transfers between devices  24.7 us (63%)
  waiting for transfers between devices  9.02 us (23%)
  Pallas kernels  3.5 us (9%)
  between operations  0.71 us (2%)
  local copies, waits for them, and re-layouts  0.67 us (2%)
  other arithmetic  0.64 us (2%)
    ppermute x14, starting transfers between devices, exchange(): lax.ppermute(arrays[k], 'col', [(i, i ^ k) for i in range(count)])  22.7 us
    ppermute x14, waiting for transfers between devices, exchange(): lax.ppermute(arrays[k], 'col', [(i, i ^ k) for i in range(count)])  5.94 us
    ppermute x3, waiting for transfers between devices, on_device(): gradient = gradient + lax.ppermute(parts[step], 'row', pairs_of)  3.08 us
    ppermute x3, starting transfers between devices, on_device(): gradient = gradient + lax.ppermute(parts[step], 'row', pairs_of)  1.93 us
    pallas_call x1, Pallas kernels, on_device(): pl.pallas_call(functools.partial(blocks_kernel, group), out_shape=(*carri...  1.86 us
    pallas_call x1, Pallas kernels, on_device(): pl.pallas_call(sorted_refs(functools.partial(owner_kernel, chunk, rank_pa...  1.03 us
  transfers between devices with their start and end apart: 17, of which 8 were waited for; matrix products, arithmetic and copies ran while one was open for 2% of the time, Pallas kernels for 0%

profile of v7, /device:TPU:0, one launch (start us, length us, event | category | flops | bytes accessed | tf_op | source)
XLA Modules:
  0.0 39.2 jit_solution(9170884047403561181)
XLA Ops:
  0.7 1.9 %blocks.1 = (f32[80,128]{1,0:T(8,128)S(1)}, f32[80,128]{1,0:T(8,128)S(1)}, f32[80,128]{1,0:T(8,128)S(1)}, f32[80,128]{1,0:T(8,128)S(1)}, f32[80,128]{1,0:T(8,128...) custom-call(s32[1,8]{1,0:T(1,128)} %order_hbm.1, ...), custom_call_target="tpu_custom_call" | custom-call | tf_op jit(solution)/shard_map/blocks/pallas_call | solution.py:311
  2.5 0.0 copy-start
  2.5 4.1 %collective-permute-start = (f32[80,128]{1,0:T(8,128)S(1)}, f32[80,128]{1,0:T(8,128)S(1)}, u32[]{:S(2)}, u32[]{:S(2)}) collective-permute-start(f32[80,128]{1,0:T(8,128)S(1)} %get-tuple-element.27), channel_id=1, source_target_pairs={{0,16},{4,20},{8,24},{12,28},{16,0},{20,4},{24,8},{28,12},{1,17},{... | collective-permute-start | bytes 122888 | tf_op jit(solution)/shard_map/ppermute | solution.py:279
  6.6 1.4 %collective-permute-start.1 = (f32[80,128]{1,0:T(8,128)S(1)}, f32[80,128]{1,0:T(8,128)S(1)}, u32[]{:S(2)}, u32[]{:S(2)}) collective-permute-start(f32[80,128]{1,0:T(8,128)S(1)} %get-tuple-element.28), channel_id=1, source_target_pairs={{0,24},{4,28},{8,16},{12,20},{16,8},{20,12},{24,0},{28,4},{1,25},{... | collective-permute-start | bytes 122888 | tf_op jit(solution)/shard_map/ppermute | solution.py:279
  8.0 2.6 %collective-permute-start.2 = (f32[80,128]{1,0:T(8,128)S(1)}, f32[80,128]{1,0:T(8,128)S(1)}, u32[]{:S(2)}, u32[]{:S(2)}) collective-permute-start(f32[80,128]{1,0:T(8,128)S(1)} %get-tuple-element.29), channel_id=1, source_target_pairs={{0,20},{4,16},{8,28},{12,24},{16,4},{20,0},{24,12},{28,8},{1,21},{... | collective-permute-start | bytes 122888 | tf_op jit(solution)/shard_map/ppermute | solution.py:279
  10.6 0.8 %collective-permute-start.3 = (f32[80,128]{1,0:T(8,128)S(1)}, f32[80,128]{1,0:T(8,128)S(1)}, u32[]{:S(2)}, u32[]{:S(2)}) collective-permute-start(f32[80,128]{1,0:T(8,128)S(1)} %get-tuple-element.30), channel_id=1, source_target_pairs={{0,28},{4,24},{8,20},{12,16},{16,12},{20,8},{24,4},{28,0},{1,29},{... | collective-permute-start | bytes 122888 | tf_op jit(solution)/shard_map/ppermute | solution.py:279
  11.5 1.9 %collective-permute-start.4 = (f32[80,128]{1,0:T(8,128)S(1)}, f32[80,128]{1,0:T(8,128)S(1)}, u32[]{:S(2)}, u32[]{:S(2)}) collective-permute-start(f32[80,128]{1,0:T(8,128)S(1)} %get-tuple-element.31), channel_id=1, source_target_pairs={{0,12},{4,8},{8,4},{12,0},{16,28},{20,24},{24,20},{28,16},{1,13},{... | collective-permute-start | bytes 122888 | tf_op jit(solution)/shard_map/ppermute | solution.py:279
  13.3 1.1 %collective-permute-start.5 = (f32[80,128]{1,0:T(8,128)S(1)}, f32[80,128]{1,0:T(8,128)S(1)}, u32[]{:S(2)}, u32[]{:S(2)}) collective-permute-start(f32[80,128]{1,0:T(8,128)S(1)} %get-tuple-element.32), channel_id=1, source_target_pairs={{0,8},{4,12},{8,0},{12,4},{16,24},{20,28},{24,16},{28,20},{1,9},{5... | collective-permute-start | bytes 122888 | tf_op jit(solution)/shard_map/ppermute | solution.py:279
  14.5 0.0 collective-permute-done.1.refs_5_
  14.5 0.5 %collective-permute-start.6 = (f32[80,128]{1,0:T(8,128)S(1)}, f32[80,128]{1,0:T(8,128)S(1)}, u32[]{:S(2)}, u32[]{:S(2)}) collective-permute-start(f32[80,128]{1,0:T(8,128)S(1)} %get-tuple-element.33), channel_id=1, source_target_pairs={{0,4},{4,0},{8,12},{12,8},{16,20},{20,16},{24,28},{28,24},{1,5},{5... | collective-permute-start | bytes 122888 | tf_op jit(solution)/shard_map/ppermute | solution.py:279
  15.0 0.6 %collective-permute-done.2.refs_6_ = f32[80,128]{1,0:T(8,128)S(1)} collective-permute-done((f32[80,128]{1,0:T(8,128)S(1)}, f32[80,128]{1,0:T(8,128)S(1)}, u32[]{:S(2)}, u32[]{:S(2)}) %collective-permute-start.2) | collective-permute-done | bytes 40992 | tf_op jit(solution)/shard_map/ppermute | solution.py:279
  15.5 1.9 %collective-permute-done.3.refs_7_ = f32[80,128]{1,0:T(8,128)S(1)} collective-permute-done((f32[80,128]{1,0:T(8,128)S(1)}, f32[80,128]{1,0:T(8,128)S(1)}, u32[]{:S(2)}, u32[]{:S(2)}) %collective-permute-start.3) | collective-permute-done | bytes 40992 | tf_op jit(solution)/shard_map/ppermute | solution.py:279
  17.4 1.0 %collective-permute-done.6.refs_10_ = f32[80,128]{1,0:T(8,128)S(1)} collective-permute-done((f32[80,128]{1,0:T(8,128)S(1)}, f32[80,128]{1,0:T(8,128)S(1)}, u32[]{:S(2)}, u32[]{:S(2)}) %collective-permute-start.6) | collective-permute-done | bytes 40992 | tf_op jit(solution)/shard_map/ppermute | solution.py:279
  18.5 1.0 %owner.1 = (f32[256,128]{1,0:T(8,128)S(1)}, f32[72,128]{1,0:T(8,128)S(1)}, f32[72,128]{1,0:T(8,128)S(1)}, f32[72,128]{1,0:T(8,128)S(1)}, f32[72,128]{1,0:T(8,128...) custom-call(s32[1,64]{1,0:T(1,128)S(1)} %get-tuple-element.25.refs_0_, ...), custom_call_target="tpu_custom_call" | custom-call | tf_op jit(solution)/shard_map/owner/pallas_call | solution.py:333
  19.5 2.0 %collective-permute-start.7 = (f32[72,128]{1,0:T(8,128)S(1)}, f32[72,128]{1,0:T(8,128)S(1)}, u32[]{:S(2)}, u32[]{:S(2)}) collective-permute-start(f32[72,128]{1,0:T(8,128)S(1)} %get-tuple-element.37), channel_id=1, source_target_pairs={{0,16},{4,20},{8,24},{12,28},{16,0},{20,4},{24,8},{28,12},{1,17},{... | collective-permute-start | bytes 110600 | tf_op jit(solution)/shard_map/ppermute | solution.py:279
  21.5 1.3 %collective-permute-start.8 = (f32[72,128]{1,0:T(8,128)S(1)}, f32[72,128]{1,0:T(8,128)S(1)}, u32[]{:S(2)}, u32[]{:S(2)}) collective-permute-start(f32[72,128]{1,0:T(8,128)S(1)} %get-tuple-element.38), channel_id=1, source_target_pairs={{0,24},{4,28},{8,16},{12,20},{16,8},{20,12},{24,0},{28,4},{1,25},{... | collective-permute-start | bytes 110600 | tf_op jit(solution)/shard_map/ppermute | solution.py:279
  22.8 1.6 %collective-permute-start.9 = (f32[72,128]{1,0:T(8,128)S(1)}, f32[72,128]{1,0:T(8,128)S(1)}, u32[]{:S(2)}, u32[]{:S(2)}) collective-permute-start(f32[72,128]{1,0:T(8,128)S(1)} %get-tuple-element.39), channel_id=1, source_target_pairs={{0,20},{4,16},{8,28},{12,24},{16,4},{20,0},{24,12},{28,8},{1,21},{... | collective-permute-start | bytes 110600 | tf_op jit(solution)/shard_map/ppermute | solution.py:279
  24.5 1.9 %collective-permute-start.10 = (f32[72,128]{1,0:T(8,128)S(1)}, f32[72,128]{1,0:T(8,128)S(1)}, u32[]{:S(2)}, u32[]{:S(2)}) collective-permute-start(f32[72,128]{1,0:T(8,128)S(1)} %get-tuple-element.40), channel_id=1, source_target_pairs={{0,28},{4,24},{8,20},{12,16},{16,12},{20,8},{24,4},{28,0},{1,29},{... | collective-permute-start | bytes 110600 | tf_op jit(solution)/shard_map/ppermute | solution.py:279
  26.3 0.8 %collective-permute-start.11 = (f32[72,128]{1,0:T(8,128)S(1)}, f32[72,128]{1,0:T(8,128)S(1)}, u32[]{:S(2)}, u32[]{:S(2)}) collective-permute-start(f32[72,128]{1,0:T(8,128)S(1)} %get-tuple-element.41), channel_id=1, source_target_pairs={{0,12},{4,8},{8,4},{12,0},{16,28},{20,24},{24,20},{28,16},{1,13},{... | collective-permute-start | bytes 110600 | tf_op jit(solution)/shard_map/ppermute | solution.py:279
  27.2 1.1 %collective-permute-start.12 = (f32[72,128]{1,0:T(8,128)S(1)}, f32[72,128]{1,0:T(8,128)S(1)}, u32[]{:S(2)}, u32[]{:S(2)}) collective-permute-start(f32[72,128]{1,0:T(8,128)S(1)} %get-tuple-element.42), channel_id=1, source_target_pairs={{0,8},{4,12},{8,0},{12,4},{16,24},{20,28},{24,16},{28,20},{1,9},{5... | collective-permute-start | bytes 110600 | tf_op jit(solution)/shard_map/ppermute | solution.py:279
  28.3 1.5 %collective-permute-start.13 = (f32[72,128]{1,0:T(8,128)S(1)}, f32[72,128]{1,0:T(8,128)S(1)}, u32[]{:S(2)}, u32[]{:S(2)}) collective-permute-start(f32[72,128]{1,0:T(8,128)S(1)} %get-tuple-element.43), channel_id=1, source_target_pairs={{0,4},{4,0},{8,12},{12,8},{16,20},{20,16},{24,28},{28,24},{1,5},{5... | collective-permute-start | bytes 110600 | tf_op jit(solution)/shard_map/ppermute | solution.py:279
  29.8 1.3 %collective-permute-done.10.refs_7_ = f32[72,128]{1,0:T(8,128)S(1)} collective-permute-done((f32[72,128]{1,0:T(8,128)S(1)}, f32[72,128]{1,0:T(8,128)S(1)}, u32[]{:S(2)}, u32[]{:S(2)}) %collective-permute-start.10) | collective-permute-done | bytes 36896 | tf_op jit(solution)/shard_map/ppermute | solution.py:279
  31.1 0.4 collective-permute-done.11.refs_8_
  31.5 0.7 %collective-permute-done.13.refs_10_ = f32[72,128]{1,0:T(8,128)S(1)} collective-permute-done((f32[72,128]{1,0:T(8,128)S(1)}, f32[72,128]{1,0:T(8,128)S(1)}, u32[]{:S(2)}, u32[]{:S(2)}) %collective-permute-start.13) | collective-permute-done | bytes 36896 | tf_op jit(solution)/shard_map/ppermute | solution.py:279
  32.3 0.6 %gradient.1 = (f32[128,128]{1,0:T(8,128)S(1)}, f32[128,128]{1,0:T(8,128)S(1)}, f32[128,128]{1,0:T(8,128)S(1)}, f32[128,128]{1,0:T(8,128)S(1)}) custom-call(s32[8,128]{1,0:T(8,128)S(1)} %get-tuple-element.35.refs_0_, f32[8,2,48,256]{3,2,1,0:T(8,128)S(1)} %bitcast.10, f32[512,128]{1,0:T(8,128)S(1)} %copy-done.1, f32[72,128]{1,0:T(8,128)S(1)} %get-tuple-element.36.refs_3_, ...), custom_call_target="tpu_custom_call" | custom-call | tf_op jit(solution)/shard_map/gradient/pallas_call | solution.py:349
  32.9 0.1 collective-permute-start.14
  33.0 1.6 %collective-permute-start.15 = (f32[128,128]{1,0:T(8,128)S(1)}, f32[128,128]{1,0:T(8,128)S(1)}, u32[]{:S(2)}, u32[]{:S(2)}) collective-permute-start(f32[128,128]{1,0:T(8,128)S(1)} %get-tuple-element.46), channel_id=1, source_target_pairs={{0,2},{1,3},{2,0},{3,1},{4,6},{5,7},{6,4},{7,5},{8,10},{9,11},{10,... | collective-permute-start | bytes 196616 | tf_op jit(solution)/shard_map/ppermute | solution.py:361
  34.5 0.3 collective-permute-start.16
  34.8 0.7 %copy.9 = f32[1,1,256,128]{3,2,1,0:T(8,128)} copy(f32[1,1,256,128]{3,2,1,0:T(8,128)S(1)} %bitcast.8) | data formatting | bytes 262144
  35.5 2.0 %collective-permute-done.15 = f32[128,128]{1,0:T(8,128)S(1)} collective-permute-done((f32[128,128]{1,0:T(8,128)S(1)}, f32[128,128]{1,0:T(8,128)S(1)}, u32[]{:S(2)}, u32[]{:S(2)}) %collective-permute-start.15) | collective-permute-done | bytes 65568 | tf_op jit(solution)/shard_map/ppermute | solution.py:361
  37.5 1.1 %collective-permute-done.16 = f32[128,128]{1,0:T(8,128)S(1)} collective-permute-done((f32[128,128]{1,0:T(8,128)S(1)}, f32[128,128]{1,0:T(8,128)S(1)}, u32[]{:S(2)}, u32[]{:S(2)}) %collective-permute-start.16) | collective-permute-done | bytes 65568 | tf_op jit(solution)/shard_map/ppermute | solution.py:361
  38.6 0.6 %add_add_fusion = f32[128,128]{1,0:T(8,128)} fusion(f32[128,128]{1,0:T(8,128)S(1)} %collective-permute-done.16, f32[128,128]{1,0:T(8,128)S(1)} %collective-permute-done.15, f32[128,128]{1,0:T(8,128)S(1)} %get-tuple-element.44, f32[128,128]{1,0:T(8,128)S(1)} %collective-permute-done.14), kind=kLoop, calls=%fused_computation | loop fusion | flops 49152 | bytes 327680 | tf_op jit(solution)/shard_map/add | solution.py:361
  (15 shorter events, 0.0 us)
Async XLA Ops:
  0.6 17.8 %copy-start.2 = (f32[1,1,256,768]{3,2,1,0:T(8,128)S(1)}, f32[1,1,256,768]{3,2,1,0:T(8,128)}, u32[]{:S(2)}) copy-start(f32[1,1,256,768]{3,2,1,0:T(8,128)} %param.9) | copy-start | bytes 2359300
  0.6 17.8 %copy-start.3 = (f32[1,1,64,128]{3,2,1,0:T(8,128)S(1)}, f32[1,1,64,128]{3,2,1,0:T(8,128)}, u32[]{:S(2)}) copy-start(f32[1,1,64,128]{3,2,1,0:T(8,128)} %param.13) | copy-start | bytes 98308
  2.5 29.7 %copy-start = (f32[8,1,2,48,256]{4,3,2,1,0:T(8,128)S(1)}, f32[8,1,2,48,256]{4,3,2,1,0:T(8,128)}, u32[]{:S(2)}) copy-start(f32[8,1,2,48,256]{4,3,2,1,0:T(8,128)} %param.8) | copy-start | bytes 2359300
  2.5 10.8 %collective-permute-start = (f32[80,128]{1,0:T(8,128)S(1)}, f32[80,128]{1,0:T(8,128)S(1)}, u32[]{:S(2)}, u32[]{:S(2)}) collective-permute-start(f32[80,128]{1,0:T(8,128)S(1)} %get-tuple-element.27), channel_id=1, source_target_pairs={{0,16},{4,20},{8,24},{12,28},{16,0},{20,4},{24,8},{28,12},{1,17},{... | collective-permute-start | bytes 122888 | tf_op jit(solution)/shard_map/ppermute | solution.py:279
  6.6 7.8 %collective-permute-start.1 = (f32[80,128]{1,0:T(8,128)S(1)}, f32[80,128]{1,0:T(8,128)S(1)}, u32[]{:S(2)}, u32[]{:S(2)}) collective-permute-start(f32[80,128]{1,0:T(8,128)S(1)} %get-tuple-element.28), channel_id=1, source_target_pairs={{0,24},{4,28},{8,16},{12,20},{16,8},{20,12},{24,0},{28,4},{1,25},{... | collective-permute-start | bytes 122888 | tf_op jit(solution)/shard_map/ppermute | solution.py:279
  8.0 7.6 %collective-permute-start.2 = (f32[80,128]{1,0:T(8,128)S(1)}, f32[80,128]{1,0:T(8,128)S(1)}, u32[]{:S(2)}, u32[]{:S(2)}) collective-permute-start(f32[80,128]{1,0:T(8,128)S(1)} %get-tuple-element.29), channel_id=1, source_target_pairs={{0,20},{4,16},{8,28},{12,24},{16,4},{20,0},{24,12},{28,8},{1,21},{... | collective-permute-start | bytes 122888 | tf_op jit(solution)/shard_map/ppermute | solution.py:279
  10.6 6.8 %collective-permute-start.3 = (f32[80,128]{1,0:T(8,128)S(1)}, f32[80,128]{1,0:T(8,128)S(1)}, u32[]{:S(2)}, u32[]{:S(2)}) collective-permute-start(f32[80,128]{1,0:T(8,128)S(1)} %get-tuple-element.30), channel_id=1, source_target_pairs={{0,28},{4,24},{8,20},{12,16},{16,12},{20,8},{24,4},{28,0},{1,29},{... | collective-permute-start | bytes 122888 | tf_op jit(solution)/shard_map/ppermute | solution.py:279
  11.5 6.0 %collective-permute-start.4 = (f32[80,128]{1,0:T(8,128)S(1)}, f32[80,128]{1,0:T(8,128)S(1)}, u32[]{:S(2)}, u32[]{:S(2)}) collective-permute-start(f32[80,128]{1,0:T(8,128)S(1)} %get-tuple-element.31), channel_id=1, source_target_pairs={{0,12},{4,8},{8,4},{12,0},{16,28},{20,24},{24,20},{28,16},{1,13},{... | collective-permute-start | bytes 122888 | tf_op jit(solution)/shard_map/ppermute | solution.py:279
  13.3 4.1 %collective-permute-start.5 = (f32[80,128]{1,0:T(8,128)S(1)}, f32[80,128]{1,0:T(8,128)S(1)}, u32[]{:S(2)}, u32[]{:S(2)}) collective-permute-start(f32[80,128]{1,0:T(8,128)S(1)} %get-tuple-element.32), channel_id=1, source_target_pairs={{0,8},{4,12},{8,0},{12,4},{16,24},{20,28},{24,16},{28,20},{1,9},{5... | collective-permute-start | bytes 122888 | tf_op jit(solution)/shard_map/ppermute | solution.py:279
  14.5 4.0 %collective-permute-start.6 = (f32[80,128]{1,0:T(8,128)S(1)}, f32[80,128]{1,0:T(8,128)S(1)}, u32[]{:S(2)}, u32[]{:S(2)}) collective-permute-start(f32[80,128]{1,0:T(8,128)S(1)} %get-tuple-element.33), channel_id=1, source_target_pairs={{0,4},{4,0},{8,12},{12,8},{16,20},{20,16},{24,28},{28,24},{1,5},{5... | collective-permute-start | bytes 122888 | tf_op jit(solution)/shard_map/ppermute | solution.py:279
  18.5 13.8 %copy-start.1 = (f32[512,128]{1,0:T(8,128)S(1)}, f32[512,128]{1,0:T(8,128)}, u32[]{:S(2)}) copy-start(f32[512,128]{1,0:T(8,128)} %refs_2_.1) | copy-start | bytes 786436
  19.5 7.7 %collective-permute-start.7 = (f32[72,128]{1,0:T(8,128)S(1)}, f32[72,128]{1,0:T(8,128)S(1)}, u32[]{:S(2)}, u32[]{:S(2)}) collective-permute-start(f32[72,128]{1,0:T(8,128)S(1)} %get-tuple-element.37), channel_id=1, source_target_pairs={{0,16},{4,20},{8,24},{12,28},{16,0},{20,4},{24,8},{28,12},{1,17},{... | collective-permute-start | bytes 110600 | tf_op jit(solution)/shard_map/ppermute | solution.py:279
  21.5 6.8 %collective-permute-start.8 = (f32[72,128]{1,0:T(8,128)S(1)}, f32[72,128]{1,0:T(8,128)S(1)}, u32[]{:S(2)}, u32[]{:S(2)}) collective-permute-start(f32[72,128]{1,0:T(8,128)S(1)} %get-tuple-element.38), channel_id=1, source_target_pairs={{0,24},{4,28},{8,16},{12,20},{16,8},{20,12},{24,0},{28,4},{1,25},{... | collective-permute-start | bytes 110600 | tf_op jit(solution)/shard_map/ppermute | solution.py:279
  22.8 7.0 %collective-permute-start.9 = (f32[72,128]{1,0:T(8,128)S(1)}, f32[72,128]{1,0:T(8,128)S(1)}, u32[]{:S(2)}, u32[]{:S(2)}) collective-permute-start(f32[72,128]{1,0:T(8,128)S(1)} %get-tuple-element.39), channel_id=1, source_target_pairs={{0,20},{4,16},{8,28},{12,24},{16,4},{20,0},{24,12},{28,8},{1,21},{... | collective-permute-start | bytes 110600 | tf_op jit(solution)/shard_map/ppermute | solution.py:279
  24.5 6.7 %collective-permute-start.10 = (f32[72,128]{1,0:T(8,128)S(1)}, f32[72,128]{1,0:T(8,128)S(1)}, u32[]{:S(2)}, u32[]{:S(2)}) collective-permute-start(f32[72,128]{1,0:T(8,128)S(1)} %get-tuple-element.40), channel_id=1, source_target_pairs={{0,28},{4,24},{8,20},{12,16},{16,12},{20,8},{24,4},{28,0},{1,29},{... | collective-permute-start | bytes 110600 | tf_op jit(solution)/shard_map/ppermute | solution.py:279
  26.3 5.2 %collective-permute-start.11 = (f32[72,128]{1,0:T(8,128)S(1)}, f32[72,128]{1,0:T(8,128)S(1)}, u32[]{:S(2)}, u32[]{:S(2)}) collective-permute-start(f32[72,128]{1,0:T(8,128)S(1)} %get-tuple-element.41), channel_id=1, source_target_pairs={{0,12},{4,8},{8,4},{12,0},{16,28},{20,24},{24,20},{28,16},{1,13},{... | collective-permute-start | bytes 110600 | tf_op jit(solution)/shard_map/ppermute | solution.py:279
  27.2 4.4 %collective-permute-start.12 = (f32[72,128]{1,0:T(8,128)S(1)}, f32[72,128]{1,0:T(8,128)S(1)}, u32[]{:S(2)}, u32[]{:S(2)}) collective-permute-start(f32[72,128]{1,0:T(8,128)S(1)} %get-tuple-element.42), channel_id=1, source_target_pairs={{0,8},{4,12},{8,0},{12,4},{16,24},{20,28},{24,16},{28,20},{1,9},{5... | collective-permute-start | bytes 110600 | tf_op jit(solution)/shard_map/ppermute | solution.py:279
  28.3 4.0 %collective-permute-start.13 = (f32[72,128]{1,0:T(8,128)S(1)}, f32[72,128]{1,0:T(8,128)S(1)}, u32[]{:S(2)}, u32[]{:S(2)}) collective-permute-start(f32[72,128]{1,0:T(8,128)S(1)} %get-tuple-element.43), channel_id=1, source_target_pairs={{0,4},{4,0},{8,12},{12,8},{16,20},{20,16},{24,28},{28,24},{1,5},{5... | collective-permute-start | bytes 110600 | tf_op jit(solution)/shard_map/ppermute | solution.py:279
  32.9 2.6 %collective-permute-start.14 = (f32[128,128]{1,0:T(8,128)S(1)}, f32[128,128]{1,0:T(8,128)S(1)}, u32[]{:S(2)}, u32[]{:S(2)}) collective-permute-start(f32[128,128]{1,0:T(8,128)S(1)} %get-tuple-element.45), channel_id=1, source_target_pairs={{0,1},{1,0},{2,3},{3,2},{4,5},{5,4},{6,7},{7,6},{8,9},{9,8},{10,11... | collective-permute-start | bytes 196616 | tf_op jit(solution)/shard_map/ppermute | solution.py:361
  33.0 4.5 %collective-permute-start.15 = (f32[128,128]{1,0:T(8,128)S(1)}, f32[128,128]{1,0:T(8,128)S(1)}, u32[]{:S(2)}, u32[]{:S(2)}) collective-permute-start(f32[128,128]{1,0:T(8,128)S(1)} %get-tuple-element.46), channel_id=1, source_target_pairs={{0,2},{1,3},{2,0},{3,1},{4,6},{5,7},{6,4},{7,5},{8,10},{9,11},{10,... | collective-permute-start | bytes 196616 | tf_op jit(solution)/shard_map/ppermute | solution.py:361
  34.5 4.0 %collective-permute-start.16 = (f32[128,128]{1,0:T(8,128)S(1)}, f32[128,128]{1,0:T(8,128)S(1)}, u32[]{:S(2)}, u32[]{:S(2)}) collective-permute-start(f32[128,128]{1,0:T(8,128)S(1)} %get-tuple-element.47), channel_id=1, source_target_pairs={{0,3},{1,2},{2,1},{3,0},{4,7},{5,6},{6,5},{7,4},{8,11},{9,10},{10,... | collective-permute-start | bytes 196616 | tf_op jit(solution)/shard_map/ppermute | solution.py:361

commit v8 on v7

--- a/solution.py
+++ b/solution.py
@@ -141,7 +141,42 @@
         copy.wait()
 
 
+def unpack_into(stacked_ref, received_ref, rank_pad, at, pair):
+    size = packed_rows(rank_pad)
+    width = stacked_ref.shape[1]
+    rank_index = lax.broadcasted_iota(jnp.int32, (rank_pad, width), 0)
+    base = pair * (size + MARK)
+    cut = scalar(received_ref, base + size, 0).astype(jnp.int32)
+    both = received_ref[base : base + size, :]
+    left = pl.multiple_of(at, 8)
+    stacked_ref[pl.ds(left, rank_pad), :] = jnp.where(rank_index < cut, both[:rank_pad], 0.0)
+    second = pltpu.roll(both, size - cut, 0)[:rank_pad]
+    right = pl.multiple_of(left + rank_pad, 8)
+    stacked_ref[pl.ds(right, rank_pad), :] = jnp.where(rank_index < size - cut, second, 0.0)
+
+
+def half_product(rank_pad, flip, u_ref, received_refs, stacked_ref):
+    half = len(received_refs)
+    depth = u_ref.shape[1] // 2
+    each_rows = depth // half
+    me = lax.axis_index("col")
+    for k, received_ref in enumerate(received_refs):
+        for pair in range(each_rows // (2 * rank_pad)):
+            at = ((me ^ k) % half) * each_rows + pair * 2 * rank_pad
+            unpack_into(stacked_ref, received_ref, rank_pad, at, pair)
+    columns = pl.ds(pl.multiple_of(((me // half) ^ flip) * depth, depth), depth)
+    return product(u_ref[:, columns], stacked_ref[:depth, :])
+
+
+def owner_far_kernel(rank_pad, u_ref, *refs):
+    received_refs, (part_ref, stacked_ref) = refs[:-2], refs[-2:]
+    part_ref[...] = half_product(rank_pad, 1, u_ref, received_refs, stacked_ref)
+
+
 def owner_kernel(chunk, rank_pad, count, wells_ref, u_ref, observed_ref, *refs):
+    split_up = count > 1
+    if split_up:
+        far_part_ref, refs = refs[0], refs[1:]
     received_refs, field_ref, packed_refs, (stacked_ref, rows_ref) = (
         refs[:count],
         refs[count],
@@ -182,14 +217,18 @@
             here = slice(pair * size, (pair + 1) * size)
             block(packed_refs, k)[here, :] = jnp.where(packed_index < cut, first, second)
 
-    each(sources, unpack)
+    if not split_up:
+        each(sources, unpack)
     picked = jnp.where(lax.broadcasted_iota(jnp.int32, (cells, wells), 0) == wells_ref[...], 1.0, 0.0).astype(BF16)
     turned = (((0,), (0,)), ((), ()))
 
     def first(k):
         here = pl.ds(k * chunk, chunk)
         high, low = split(u_ref[:, here])
-        part = product_of(high, low, stacked_ref[here, :])
+        if split_up:
+            part = half_product(rank_pad, 0, u_ref, received_refs[: count // 2], stacked_ref) + far_part_ref[...]
+        else:
+            part = product_of(high, low, stacked_ref[here, :])
         own = lax.dot_general(picked, high, turned, preferred_element_type=F32).astype(BF16)
         rows_ref[0:wells, here] = own
         rows_ref[wells : 2 * wells, here] = own
@@ -224,6 +263,53 @@
     each(sources, pack)
 
 
+def gradient_part(plan_ref, v_ref, returned_refs, first, ordered_ref, chosen_ref):
+    _, local, rank_pad, cells = v_ref.shape
+    width = ordered_ref.shape[2]
+    packed = packed_rows(rank_pad)
+    rank_index = lax.broadcasted_iota(jnp.int32, (rank_pad, width), 0)
+    for i, returned_ref in enumerate(returned_refs):
+        q = scalar(plan_ref, first + i, 0)
+        here = slice(i * rank_pad, (i + 1) * rank_pad)
+        for pair in range(local // 2):
+            left, right = 2 * pair, 2 * pair + 1
+            cut = scalar(plan_ref, first + i, 1 + left)
+            both = returned_ref[pair * packed : (pair + 1) * packed, :]
+            ordered_ref[left, here, :] = jnp.where(rank_index < cut, both[:rank_pad], 0.0)
+            second = pltpu.roll(both, packed - cut, 0)[:rank_pad]
+            ordered_ref[right, here, :] = jnp.where(rank_index < scalar(plan_ref, first + i, 1 + right), second, 0.0)
+        for j in range(local):
+            chosen_ref[j, here, :] = v_ref[q, j]
+    return [product(chosen_ref[j], ordered_ref[j], (0, 0)) for j in range(local)]
+
+
+def gradient_far_kernel(plan_ref, v_ref, *refs):
+    returned_refs, (part_ref, ordered_ref, chosen_ref) = refs[:-3], refs[-3:]
+    cells = v_ref.shape[3]
+    for j, part in enumerate(gradient_part(plan_ref, v_ref, returned_refs, len(returned_refs), ordered_ref, chosen_ref)):
+        part_ref[j * cells : (j + 1) * cells, :] = part
+
+
+def gradient_near_kernel(axis, turn, half, plan_ref, v_ref, latent_ref, part_ref, *refs):
+    returned_refs, out_refs, (ordered_ref, chosen_ref, total_ref) = refs[:half], refs[half:-3], refs[-3:]
+    cells = v_ref.shape[3]
+    for j, part in enumerate(gradient_part(plan_ref, v_ref, returned_refs, 0, ordered_ref, chosen_ref)):
+        here = slice(j * cells, (j + 1) * cells)
+        total_ref[here, :] = part + part_ref[here, :]
+    hand_out(axis, turn, total_ref, latent_ref, out_refs)
+
+
+def hand_out(axis, turn, total_ref, latent_ref, out_refs):
+    me = lax.axis_index(axis)
+    size = out_refs[0].shape[0]
+    for step, out_ref in enumerate(out_refs):
+        there = pl.ds(pl.multiple_of(turn(me, step) * size, size), size)
+        if step == 0:
+            out_ref[...] = total_ref[there, :] + latent_ref[there, :]
+        else:
+            out_ref[...] = total_ref[there, :]
+
+
 def gradient_kernel(group, axis, turn, count, plan_ref, v_ref, latent_ref, *refs):
     returned_refs, out_refs, (ordered_ref, total_ref) = refs[:count], refs[count:-2], refs[-2:]
     rows, local, rank_pad, cells = v_ref.shape
@@ -262,14 +348,7 @@
                     total_ref[here, :] += part
 
     repeat(rows // group, some)
-    me = lax.axis_index(axis)
-    size = out_refs[0].shape[0]
-    for step, out_ref in enumerate(out_refs):
-        there = pl.ds(pl.multiple_of(turn(me, step) * size, size), size)
-        if step == 0:
-            out_ref[...] = total_ref[there, :] + latent_ref[there, :]
-        else:
-            out_ref[...] = total_ref[there, :]
+    hand_out(axis, turn, total_ref, latent_ref, out_refs)
 
 
 def exchange(arrays):
@@ -298,12 +377,11 @@
         shape = (size, width) if direct else (rows, size, width)
         return [jax.ShapeDtypeStruct(shape, F32)] * count
 
-    def sorted_refs(kernel, before, lists):
+    def put_back(kernel, before, handed):
         def run(*refs):
             refs = list(refs)
-            for start in (before + at for at in lists):
-                moved = refs[start : start + count]
-                refs[start : start + count] = [moved[far.index(k)] for k in range(count)]
+            moved = refs[before : before + len(handed)]
+            refs[before : before + len(handed)] = [moved[handed.index(k)] for k in range(len(handed))]
             kernel(*refs)
 
         return run
@@ -330,15 +408,32 @@
     )(stay(slot_row), stay(ranks[:, 0].T), stay(wells[0]), stay(latent), stay(v_rows))
     sent, (plan, wells_here) = outs[:count], outs[count:]
     received = exchange(sent)
+    half = count // 2
+    first_half = [k for k in far if k < half]
+    other_half = [k for k in far if k >= half]
+    extra = []
+    if direct:
+        far_part = pl.pallas_call(
+            put_back(functools.partial(owner_far_kernel, rank_pad), 1, [k - half for k in other_half]),
+            out_shape=jax.ShapeDtypeStruct((cells, width), F32),
+            in_specs=[VMEM] * (1 + half),
+            out_specs=VMEM,
+            scratch_shapes=[pltpu.VMEM((depth // 2, width), F32)],
+            compiler_params=params([u_owned, u_owned]),
+            cost_estimate=pl.CostEstimate(flops=3 * cells * depth * width, bytes_accessed=4 * cells * depth, transcendentals=0),
+            name="owner_far",
+        )(u_owned, *[received[k] for k in other_half])
+        extra = [far_part]
+    handed = other_half + first_half if direct else far
     field, *adjoint = pl.pallas_call(
-        sorted_refs(functools.partial(owner_kernel, chunk, rank_pad, count), 3, [0]),
+        put_back(functools.partial(owner_kernel, chunk, rank_pad, count), 3 + len(extra), handed),
         out_shape=(pltpu.VMEM((cells, width), F32), *carried(pairs * packed)),
-        in_specs=[VMEM] * (3 + count),
+        in_specs=[VMEM] * (3 + len(extra) + count),
         out_specs=(VMEM,) * (1 + count),
         scratch_shapes=[pltpu.VMEM((depth, width), F32), pltpu.VMEM((3 * well_count, depth), BF16)],
         compiler_params=params([u_owned, u_owned, observed_here]),
         name="owner",
-    )(wells_here, u_owned, observed_here, *[received[k] for k in far])
+    )(wells_here, u_owned, observed_here, *extra, *[received[k] for k in handed])
     returned = exchange(adjoint)
     paired = n_row & (n_row - 1) == 0
 
@@ -346,15 +441,38 @@
         return index ^ step if paired else lax.rem(index + step, n_row)
 
     size = local * cells // n_row
-    parts = pl.pallas_call(
-        sorted_refs(functools.partial(gradient_kernel, group, "row", turn, count), 3, [0]),
-        out_shape=[jax.ShapeDtypeStruct((size, width), F32)] * n_row,
-        in_specs=[VMEM] * (3 + count),
-        out_specs=[VMEM] * n_row,
-        scratch_shapes=[pltpu.VMEM((local, rows, rank_pad, width), F32), pltpu.VMEM((local * cells, width), F32)],
-        compiler_params=params([u_owned, v_rows, latent]),
-        name="gradient",
-    )(plan, v_rows, latent, *[returned[k] for k in far])
+    part_shape = [jax.ShapeDtypeStruct((size, width), F32)] * n_row
+    if direct:
+        halves = [pltpu.VMEM((local, half * rank_pad, width), F32), pltpu.VMEM((local, half * rank_pad, cells), F32)]
+        far_part = pl.pallas_call(
+            put_back(gradient_far_kernel, 2, [k - half for k in other_half]),
+            out_shape=jax.ShapeDtypeStruct((local * cells, width), F32),
+            in_specs=[VMEM] * (2 + half),
+            out_specs=VMEM,
+            scratch_shapes=halves,
+            compiler_params=params([u_owned, v_rows, latent]),
+            cost_estimate=pl.CostEstimate(flops=3 * cells * depth * width, bytes_accessed=4 * cells * depth, transcendentals=0),
+            name="gradient_far",
+        )(plan, v_rows, *[returned[k] for k in other_half])
+        parts = pl.pallas_call(
+            put_back(functools.partial(gradient_near_kernel, "row", turn, half), 4, first_half),
+            out_shape=part_shape,
+            in_specs=[VMEM] * (4 + half),
+            out_specs=[VMEM] * n_row,
+            scratch_shapes=[*halves, pltpu.VMEM((local * cells, width), F32)],
+            compiler_params=params([u_owned, v_rows, latent]),
+            name="gradient",
+        )(plan, v_rows, latent, far_part, *[returned[k] for k in first_half])
+    else:
+        parts = pl.pallas_call(
+            functools.partial(gradient_kernel, group, "row", turn, count),
+            out_shape=part_shape,
+            in_specs=[VMEM] * (3 + count),
+            out_specs=[VMEM] * n_row,
+            scratch_shapes=[pltpu.VMEM((local, rows, rank_pad, width), F32), pltpu.VMEM((local * cells, width), F32)],
+            compiler_params=params([u_owned, v_rows, latent]),
+            name="gradient",
+        )(plan, v_rows, latent, *returned)
     gradient = parts[0]
     for step in range(1, n_row):
         pairs_of = [(i, i ^ step if paired else (i + step) % n_row) for i in range(n_row)]

time: 39.4 us -> 39.1 us (level)
  waiting for transfers between devices: 9.02 us -> 8.14 us
  Pallas kernels: 3.5 us -> 4.09 us
    ppermute x14, waiting for transfers between devices: 5.94 us -> 5.05 us  [exchange(): lax.ppermute(arrays[k], 'col', [(i, i ^ k) for i in range(count)])]
    pallas_call x2 -> x4, Pallas kernels: 1.65 us -> 2.24 us  [the longest x1 0.91 us: on_device(): pl.pallas_call(put_back(functools.partial(owner_kernel, chunk, rank_pad,...]
  transfers between devices with their start and end apart: 17 -> 17, of which waited for: 8 -> 7; matrix products, arithmetic and copies ran while one was open for 2% -> 2% of each run, Pallas kernels for 0% -> 2%
where the time goes in v8:
time: 39.1 us; the launch traced here: 39 us
  starting transfers between devices  24.7 us (63%)
  waiting for transfers between devices  8.14 us (21%)
  Pallas kernels  4.09 us (10%)
  between operations  0.74 us (2%)
  local copies, waits for them, and re-layouts  0.67 us (2%)
  other arithmetic  0.64 us (2%)
    ppermute x14, starting transfers between devices, exchange(): lax.ppermute(arrays[k], 'col', [(i, i ^ k) for i in range(count)])  22.7 us
    ppermute x14, waiting for transfers between devices, exchange(): lax.ppermute(arrays[k], 'col', [(i, i ^ k) for i in range(count)])  5.05 us
    ppermute x3, waiting for transfers between devices, on_device(): gradient = gradient + lax.ppermute(parts[step], 'row', pairs_of)  3.09 us
    ppermute x3, starting transfers between devices, on_device(): gradient = gradient + lax.ppermute(parts[step], 'row', pairs_of)  1.93 us
    pallas_call x1, Pallas kernels, on_device(): pl.pallas_call(functools.partial(blocks_kernel, group), out_shape=(*carri...  1.86 us
    pallas_call x1, Pallas kernels, on_device(): pl.pallas_call(put_back(functools.partial(owner_kernel, chunk, rank_pad,...  0.91 us
  transfers between devices with their start and end apart: 17, of which 7 were waited for; matrix products, arithmetic and copies ran while one was open for 2% of the time, Pallas kernels for 2%

profile of v8, /device:TPU:0, one launch (start us, length us, event | category | flops | bytes accessed | tf_op | source)
XLA Modules:
  0.0 39.0 jit_solution(12840884179780388368)
XLA Ops:
  0.6 1.9 %blocks.1 = (f32[80,128]{1,0:T(8,128)S(1)}, f32[80,128]{1,0:T(8,128)S(1)}, f32[80,128]{1,0:T(8,128)S(1)}, f32[80,128]{1,0:T(8,128)S(1)}, f32[80,128]{1,0:T(8,128...) custom-call(s32[1,8]{1,0:T(1,128)} %order_hbm.1, ...), custom_call_target="tpu_custom_call" | custom-call | tf_op jit(solution)/shard_map/blocks/pallas_call | solution.py:389
  2.5 4.1 %collective-permute-start = (f32[80,128]{1,0:T(8,128)S(1)}, f32[80,128]{1,0:T(8,128)S(1)}, u32[]{:S(2)}, u32[]{:S(2)}) collective-permute-start(f32[80,128]{1,0:T(8,128)S(1)} %get-tuple-element.26), channel_id=1, source_target_pairs={{0,16},{4,20},{8,24},{12,28},{16,0},{20,4},{24,8},{28,12},{1,17},{... | collective-permute-start | bytes 122888 | tf_op jit(solution)/shard_map/ppermute | solution.py:358
  6.6 1.4 %collective-permute-start.1 = (f32[80,128]{1,0:T(8,128)S(1)}, f32[80,128]{1,0:T(8,128)S(1)}, u32[]{:S(2)}, u32[]{:S(2)}) collective-permute-start(f32[80,128]{1,0:T(8,128)S(1)} %get-tuple-element.27), channel_id=1, source_target_pairs={{0,24},{4,28},{8,16},{12,20},{16,8},{20,12},{24,0},{28,4},{1,25},{... | collective-permute-start | bytes 122888 | tf_op jit(solution)/shard_map/ppermute | solution.py:358
  8.0 2.6 %collective-permute-start.2 = (f32[80,128]{1,0:T(8,128)S(1)}, f32[80,128]{1,0:T(8,128)S(1)}, u32[]{:S(2)}, u32[]{:S(2)}) collective-permute-start(f32[80,128]{1,0:T(8,128)S(1)} %get-tuple-element.28), channel_id=1, source_target_pairs={{0,20},{4,16},{8,28},{12,24},{16,4},{20,0},{24,12},{28,8},{1,21},{... | collective-permute-start | bytes 122888 | tf_op jit(solution)/shard_map/ppermute | solution.py:358
  10.6 0.8 %collective-permute-start.3 = (f32[80,128]{1,0:T(8,128)S(1)}, f32[80,128]{1,0:T(8,128)S(1)}, u32[]{:S(2)}, u32[]{:S(2)}) collective-permute-start(f32[80,128]{1,0:T(8,128)S(1)} %get-tuple-element.29), channel_id=1, source_target_pairs={{0,28},{4,24},{8,20},{12,16},{16,12},{20,8},{24,4},{28,0},{1,29},{... | collective-permute-start | bytes 122888 | tf_op jit(solution)/shard_map/ppermute | solution.py:358
  11.4 1.9 %collective-permute-start.4 = (f32[80,128]{1,0:T(8,128)S(1)}, f32[80,128]{1,0:T(8,128)S(1)}, u32[]{:S(2)}, u32[]{:S(2)}) collective-permute-start(f32[80,128]{1,0:T(8,128)S(1)} %get-tuple-element.31), channel_id=1, source_target_pairs={{0,12},{4,8},{8,4},{12,0},{16,28},{20,24},{24,20},{28,16},{1,13},{... | collective-permute-start | bytes 122888 | tf_op jit(solution)/shard_map/ppermute | solution.py:358
  13.3 1.1 %collective-permute-start.5 = (f32[80,128]{1,0:T(8,128)S(1)}, f32[80,128]{1,0:T(8,128)S(1)}, u32[]{:S(2)}, u32[]{:S(2)}) collective-permute-start(f32[80,128]{1,0:T(8,128)S(1)} %get-tuple-element.32), channel_id=1, source_target_pairs={{0,8},{4,12},{8,0},{12,4},{16,24},{20,28},{24,16},{28,20},{1,9},{5... | collective-permute-start | bytes 122888 | tf_op jit(solution)/shard_map/ppermute | solution.py:358
  14.4 0.5 %collective-permute-start.6 = (f32[80,128]{1,0:T(8,128)S(1)}, f32[80,128]{1,0:T(8,128)S(1)}, u32[]{:S(2)}, u32[]{:S(2)}) collective-permute-start(f32[80,128]{1,0:T(8,128)S(1)} %get-tuple-element.33), channel_id=1, source_target_pairs={{0,4},{4,0},{8,12},{12,8},{16,20},{20,16},{24,28},{28,24},{1,5},{5... | collective-permute-start | bytes 122888 | tf_op jit(solution)/shard_map/ppermute | solution.py:358
  14.9 0.6 %collective-permute-done.2.refs_3_.refs_6_ = f32[80,128]{1,0:T(8,128)S(1)} collective-permute-done((f32[80,128]{1,0:T(8,128)S(1)}, f32[80,128]{1,0:T(8,128)S(1)}, u32[]{:S(2)}, u32[]{:S(2)}) %collective-permute-start.2) | collective-permute-done | bytes 40992 | tf_op jit(solution)/shard_map/ppermute | solution.py:358
  15.5 1.9 %collective-permute-done.3.refs_4_.refs_7_ = f32[80,128]{1,0:T(8,128)S(1)} collective-permute-done((f32[80,128]{1,0:T(8,128)S(1)}, f32[80,128]{1,0:T(8,128)S(1)}, u32[]{:S(2)}, u32[]{:S(2)}) %collective-permute-start.3) | collective-permute-done | bytes 40992 | tf_op jit(solution)/shard_map/ppermute | solution.py:358
  17.4 0.4 owner_far.1.refs_3_
  17.8 0.0 copy-start
  17.8 0.6 %collective-permute-done.6.refs_11_ = f32[80,128]{1,0:T(8,128)S(1)} collective-permute-done((f32[80,128]{1,0:T(8,128)S(1)}, f32[80,128]{1,0:T(8,128)S(1)}, u32[]{:S(2)}, u32[]{:S(2)}) %collective-permute-start.6) | collective-permute-done | bytes 40992 | tf_op jit(solution)/shard_map/ppermute | solution.py:358
  18.4 0.9 %owner.1 = (f32[256,128]{1,0:T(8,128)S(1)}, f32[72,128]{1,0:T(8,128)S(1)}, f32[72,128]{1,0:T(8,128)S(1)}, f32[72,128]{1,0:T(8,128)S(1)}, f32[72,128]{1,0:T(8,128...) custom-call(s32[1,64]{1,0:T(1,128)S(1)} %get-tuple-element.25.refs_0_, ...), custom_call_target="tpu_custom_call" | custom-call | tf_op jit(solution)/shard_map/owner/pallas_call | solution.py:428
  19.4 2.0 %collective-permute-start.7 = (f32[72,128]{1,0:T(8,128)S(1)}, f32[72,128]{1,0:T(8,128)S(1)}, u32[]{:S(2)}, u32[]{:S(2)}) collective-permute-start(f32[72,128]{1,0:T(8,128)S(1)} %get-tuple-element.36), channel_id=1, source_target_pairs={{0,16},{4,20},{8,24},{12,28},{16,0},{20,4},{24,8},{28,12},{1,17},{... | collective-permute-start | bytes 110600 | tf_op jit(solution)/shard_map/ppermute | solution.py:358
  21.3 1.4 %collective-permute-start.8 = (f32[72,128]{1,0:T(8,128)S(1)}, f32[72,128]{1,0:T(8,128)S(1)}, u32[]{:S(2)}, u32[]{:S(2)}) collective-permute-start(f32[72,128]{1,0:T(8,128)S(1)} %get-tuple-element.37), channel_id=1, source_target_pairs={{0,24},{4,28},{8,16},{12,20},{16,8},{20,12},{24,0},{28,4},{1,25},{... | collective-permute-start | bytes 110600 | tf_op jit(solution)/shard_map/ppermute | solution.py:358
  22.7 1.6 %collective-permute-start.9 = (f32[72,128]{1,0:T(8,128)S(1)}, f32[72,128]{1,0:T(8,128)S(1)}, u32[]{:S(2)}, u32[]{:S(2)}) collective-permute-start(f32[72,128]{1,0:T(8,128)S(1)} %get-tuple-element.38), channel_id=1, source_target_pairs={{0,20},{4,16},{8,28},{12,24},{16,4},{20,0},{24,12},{28,8},{1,21},{... | collective-permute-start | bytes 110600 | tf_op jit(solution)/shard_map/ppermute | solution.py:358
  24.3 1.9 %collective-permute-start.10 = (f32[72,128]{1,0:T(8,128)S(1)}, f32[72,128]{1,0:T(8,128)S(1)}, u32[]{:S(2)}, u32[]{:S(2)}) collective-permute-start(f32[72,128]{1,0:T(8,128)S(1)} %get-tuple-element.39), channel_id=1, source_target_pairs={{0,28},{4,24},{8,20},{12,16},{16,12},{20,8},{24,4},{28,0},{1,29},{... | collective-permute-start | bytes 110600 | tf_op jit(solution)/shard_map/ppermute | solution.py:358
  26.2 0.8 %collective-permute-start.11 = (f32[72,128]{1,0:T(8,128)S(1)}, f32[72,128]{1,0:T(8,128)S(1)}, u32[]{:S(2)}, u32[]{:S(2)}) collective-permute-start(f32[72,128]{1,0:T(8,128)S(1)} %get-tuple-element.41), channel_id=1, source_target_pairs={{0,12},{4,8},{8,4},{12,0},{16,28},{20,24},{24,20},{28,16},{1,13},{... | collective-permute-start | bytes 110600 | tf_op jit(solution)/shard_map/ppermute | solution.py:358
  27.0 1.1 %collective-permute-start.12 = (f32[72,128]{1,0:T(8,128)S(1)}, f32[72,128]{1,0:T(8,128)S(1)}, u32[]{:S(2)}, u32[]{:S(2)}) collective-permute-start(f32[72,128]{1,0:T(8,128)S(1)} %get-tuple-element.42), channel_id=1, source_target_pairs={{0,8},{4,12},{8,0},{12,4},{16,24},{20,28},{24,16},{28,20},{1,9},{5... | collective-permute-start | bytes 110600 | tf_op jit(solution)/shard_map/ppermute | solution.py:358
  28.2 1.5 %collective-permute-start.13 = (f32[72,128]{1,0:T(8,128)S(1)}, f32[72,128]{1,0:T(8,128)S(1)}, u32[]{:S(2)}, u32[]{:S(2)}) collective-permute-start(f32[72,128]{1,0:T(8,128)S(1)} %get-tuple-element.43), channel_id=1, source_target_pairs={{0,4},{4,0},{8,12},{12,8},{16,20},{20,16},{24,28},{28,24},{1,5},{5... | collective-permute-start | bytes 110600 | tf_op jit(solution)/shard_map/ppermute | solution.py:358
  29.7 1.3 %collective-permute-done.10.refs_5_ = f32[72,128]{1,0:T(8,128)S(1)} collective-permute-done((f32[72,128]{1,0:T(8,128)S(1)}, f32[72,128]{1,0:T(8,128)S(1)}, u32[]{:S(2)}, u32[]{:S(2)}) %collective-permute-start.10) | collective-permute-done | bytes 36896 | tf_op jit(solution)/shard_map/ppermute | solution.py:358
  31.0 0.5 %gradient_far.1.refs_3_ = f32[512,128]{1,0:T(8,128)S(1)} custom-call(s32[8,128]{1,0:T(8,128)S(1)} %get-tuple-element.35.refs_0_, f32[8,2,48,256]{3,2,1,0:T(8,128)S(1)} %bitcast.10, f32[72,128]{1,0:T(8,128)S(1)} %collective-permute-done.7.refs_2_, f32[72,128]{1,0:T(8,128)S(1)} %collective-permute-done.8.refs_3_, ...), custom_call_target="tpu_custom_call" | custom-call | flops 75497472 | bytes 786432 | tf_op jit(solution)/shard_map/gradient_far/pallas_call | solution.py:447
  31.5 0.6 %collective-permute-done.13.refs_7_ = f32[72,128]{1,0:T(8,128)S(1)} collective-permute-done((f32[72,128]{1,0:T(8,128)S(1)}, f32[72,128]{1,0:T(8,128)S(1)}, u32[]{:S(2)}, u32[]{:S(2)}) %collective-permute-start.13) | collective-permute-done | bytes 36896 | tf_op jit(solution)/shard_map/ppermute | solution.py:358
  32.1 0.5 %gradient.1 = (f32[128,128]{1,0:T(8,128)S(1)}, f32[128,128]{1,0:T(8,128)S(1)}, f32[128,128]{1,0:T(8,128)S(1)}, f32[128,128]{1,0:T(8,128)S(1)}) custom-call(s32[8,128]{1,0:T(8,128)S(1)} %get-tuple-element.35.refs_0_, f32[8,2,48,256]{3,2,1,0:T(8,128)S(1)} %bitcast.11, f32[512,128]{1,0:T(8,128)S(1)} %copy-done.2, f32[512,128]{1,0:T(8,128)S(1)} %gradient_far.1.refs_3_, ...), custom_call_target="tpu_custom_call" | custom-call | tf_op jit(solution)/shard_map/gradient/pallas_call | solution.py:457
  32.6 0.1 collective-permute-start.14
  32.7 1.6 %collective-permute-start.15 = (f32[128,128]{1,0:T(8,128)S(1)}, f32[128,128]{1,0:T(8,128)S(1)}, u32[]{:S(2)}, u32[]{:S(2)}) collective-permute-start(f32[128,128]{1,0:T(8,128)S(1)} %get-tuple-element.46), channel_id=1, source_target_pairs={{0,2},{1,3},{2,0},{3,1},{4,6},{5,7},{6,4},{7,5},{8,10},{9,11},{10,... | collective-permute-start | bytes 196616 | tf_op jit(solution)/shard_map/ppermute | solution.py:479
  34.3 0.3 collective-permute-start.16
  34.6 0.7 %copy.9 = f32[1,1,256,128]{3,2,1,0:T(8,128)} copy(f32[1,1,256,128]{3,2,1,0:T(8,128)S(1)} %bitcast.8) | data formatting | bytes 262144
  35.2 2.0 %collective-permute-done.15 = f32[128,128]{1,0:T(8,128)S(1)} collective-permute-done((f32[128,128]{1,0:T(8,128)S(1)}, f32[128,128]{1,0:T(8,128)S(1)}, u32[]{:S(2)}, u32[]{:S(2)}) %collective-permute-start.15) | collective-permute-done | bytes 65568 | tf_op jit(solution)/shard_map/ppermute | solution.py:479
  37.2 1.1 %collective-permute-done.16 = f32[128,128]{1,0:T(8,128)S(1)} collective-permute-done((f32[128,128]{1,0:T(8,128)S(1)}, f32[128,128]{1,0:T(8,128)S(1)}, u32[]{:S(2)}, u32[]{:S(2)}) %collective-permute-start.16) | collective-permute-done | bytes 65568 | tf_op jit(solution)/shard_map/ppermute | solution.py:479
  38.3 0.6 %add_add_fusion = f32[128,128]{1,0:T(8,128)} fusion(f32[128,128]{1,0:T(8,128)S(1)} %collective-permute-done.16, f32[128,128]{1,0:T(8,128)S(1)} %collective-permute-done.15, f32[128,128]{1,0:T(8,128)S(1)} %get-tuple-element.44, f32[128,128]{1,0:T(8,128)S(1)} %collective-permute-done.14), kind=kLoop, calls=%fused_computation | loop fusion | flops 49152 | bytes 327680 | tf_op jit(solution)/shard_map/add | solution.py:479
  (17 shorter events, 0.0 us)
Async XLA Ops:
  0.6 16.8 %copy-start.1 = (f32[1,1,256,768]{3,2,1,0:T(8,128)S(1)}, f32[1,1,256,768]{3,2,1,0:T(8,128)}, u32[]{:S(2)}) copy-start(f32[1,1,256,768]{3,2,1,0:T(8,128)} %param.9) | copy-start | bytes 2359300
  2.5 10.8 %collective-permute-start = (f32[80,128]{1,0:T(8,128)S(1)}, f32[80,128]{1,0:T(8,128)S(1)}, u32[]{:S(2)}, u32[]{:S(2)}) collective-permute-start(f32[80,128]{1,0:T(8,128)S(1)} %get-tuple-element.26), channel_id=1, source_target_pairs={{0,16},{4,20},{8,24},{12,28},{16,0},{20,4},{24,8},{28,12},{1,17},{... | collective-permute-start | bytes 122888 | tf_op jit(solution)/shard_map/ppermute | solution.py:358
  6.6 7.8 %collective-permute-start.1 = (f32[80,128]{1,0:T(8,128)S(1)}, f32[80,128]{1,0:T(8,128)S(1)}, u32[]{:S(2)}, u32[]{:S(2)}) collective-permute-start(f32[80,128]{1,0:T(8,128)S(1)} %get-tuple-element.27), channel_id=1, source_target_pairs={{0,24},{4,28},{8,16},{12,20},{16,8},{20,12},{24,0},{28,4},{1,25},{... | collective-permute-start | bytes 122888 | tf_op jit(solution)/shard_map/ppermute | solution.py:358
  8.0 7.6 %collective-permute-start.2 = (f32[80,128]{1,0:T(8,128)S(1)}, f32[80,128]{1,0:T(8,128)S(1)}, u32[]{:S(2)}, u32[]{:S(2)}) collective-permute-start(f32[80,128]{1,0:T(8,128)S(1)} %get-tuple-element.28), channel_id=1, source_target_pairs={{0,20},{4,16},{8,28},{12,24},{16,4},{20,0},{24,12},{28,8},{1,21},{... | collective-permute-start | bytes 122888 | tf_op jit(solution)/shard_map/ppermute | solution.py:358
  10.6 6.8 %collective-permute-start.3 = (f32[80,128]{1,0:T(8,128)S(1)}, f32[80,128]{1,0:T(8,128)S(1)}, u32[]{:S(2)}, u32[]{:S(2)}) collective-permute-start(f32[80,128]{1,0:T(8,128)S(1)} %get-tuple-element.29), channel_id=1, source_target_pairs={{0,28},{4,24},{8,20},{12,16},{16,12},{20,8},{24,4},{28,0},{1,29},{... | collective-permute-start | bytes 122888 | tf_op jit(solution)/shard_map/ppermute | solution.py:358
  11.4 6.4 %collective-permute-start.4 = (f32[80,128]{1,0:T(8,128)S(1)}, f32[80,128]{1,0:T(8,128)S(1)}, u32[]{:S(2)}, u32[]{:S(2)}) collective-permute-start(f32[80,128]{1,0:T(8,128)S(1)} %get-tuple-element.31), channel_id=1, source_target_pairs={{0,12},{4,8},{8,4},{12,0},{16,28},{20,24},{24,20},{28,16},{1,13},{... | collective-permute-start | bytes 122888 | tf_op jit(solution)/shard_map/ppermute | solution.py:358
  13.3 4.5 %collective-permute-start.5 = (f32[80,128]{1,0:T(8,128)S(1)}, f32[80,128]{1,0:T(8,128)S(1)}, u32[]{:S(2)}, u32[]{:S(2)}) collective-permute-start(f32[80,128]{1,0:T(8,128)S(1)} %get-tuple-element.32), channel_id=1, source_target_pairs={{0,8},{4,12},{8,0},{12,4},{16,24},{20,28},{24,16},{28,20},{1,9},{5... | collective-permute-start | bytes 122888 | tf_op jit(solution)/shard_map/ppermute | solution.py:358
  14.4 4.0 %collective-permute-start.6 = (f32[80,128]{1,0:T(8,128)S(1)}, f32[80,128]{1,0:T(8,128)S(1)}, u32[]{:S(2)}, u32[]{:S(2)}) collective-permute-start(f32[80,128]{1,0:T(8,128)S(1)} %get-tuple-element.33), channel_id=1, source_target_pairs={{0,4},{4,0},{8,12},{12,8},{16,20},{20,16},{24,28},{28,24},{1,5},{5... | collective-permute-start | bytes 122888 | tf_op jit(solution)/shard_map/ppermute | solution.py:358
  17.4 1.0 %copy-start.3 = (f32[1,1,64,128]{3,2,1,0:T(8,128)S(1)}, f32[1,1,64,128]{3,2,1,0:T(8,128)}, u32[]{:S(2)}) copy-start(f32[1,1,64,128]{3,2,1,0:T(8,128)} %param.13) | copy-start | bytes 98308
  17.8 13.2 %copy-start = (f32[8,1,2,48,256]{4,3,2,1,0:T(8,128)S(1)}, f32[8,1,2,48,256]{4,3,2,1,0:T(8,128)}, u32[]{:S(2)}) copy-start(f32[8,1,2,48,256]{4,3,2,1,0:T(8,128)} %param.8) | copy-start | bytes 2359300
  19.4 7.7 %collective-permute-start.7 = (f32[72,128]{1,0:T(8,128)S(1)}, f32[72,128]{1,0:T(8,128)S(1)}, u32[]{:S(2)}, u32[]{:S(2)}) collective-permute-start(f32[72,128]{1,0:T(8,128)S(1)} %get-tuple-element.36), channel_id=1, source_target_pairs={{0,16},{4,20},{8,24},{12,28},{16,0},{20,4},{24,8},{28,12},{1,17},{... | collective-permute-start | bytes 110600 | tf_op jit(solution)/shard_map/ppermute | solution.py:358
  21.3 6.8 %collective-permute-start.8 = (f32[72,128]{1,0:T(8,128)S(1)}, f32[72,128]{1,0:T(8,128)S(1)}, u32[]{:S(2)}, u32[]{:S(2)}) collective-permute-start(f32[72,128]{1,0:T(8,128)S(1)} %get-tuple-element.37), channel_id=1, source_target_pairs={{0,24},{4,28},{8,16},{12,20},{16,8},{20,12},{24,0},{28,4},{1,25},{... | collective-permute-start | bytes 110600 | tf_op jit(solution)/shard_map/ppermute | solution.py:358
  22.7 7.0 %collective-permute-start.9 = (f32[72,128]{1,0:T(8,128)S(1)}, f32[72,128]{1,0:T(8,128)S(1)}, u32[]{:S(2)}, u32[]{:S(2)}) collective-permute-start(f32[72,128]{1,0:T(8,128)S(1)} %get-tuple-element.38), channel_id=1, source_target_pairs={{0,20},{4,16},{8,28},{12,24},{16,4},{20,0},{24,12},{28,8},{1,21},{... | collective-permute-start | bytes 110600 | tf_op jit(solution)/shard_map/ppermute | solution.py:358
  24.3 6.7 %collective-permute-start.10 = (f32[72,128]{1,0:T(8,128)S(1)}, f32[72,128]{1,0:T(8,128)S(1)}, u32[]{:S(2)}, u32[]{:S(2)}) collective-permute-start(f32[72,128]{1,0:T(8,128)S(1)} %get-tuple-element.39), channel_id=1, source_target_pairs={{0,28},{4,24},{8,20},{12,16},{16,12},{20,8},{24,4},{28,0},{1,29},{... | collective-permute-start | bytes 110600 | tf_op jit(solution)/shard_map/ppermute | solution.py:358
  26.2 5.3 %collective-permute-start.11 = (f32[72,128]{1,0:T(8,128)S(1)}, f32[72,128]{1,0:T(8,128)S(1)}, u32[]{:S(2)}, u32[]{:S(2)}) collective-permute-start(f32[72,128]{1,0:T(8,128)S(1)} %get-tuple-element.41), channel_id=1, source_target_pairs={{0,12},{4,8},{8,4},{12,0},{16,28},{20,24},{24,20},{28,16},{1,13},{... | collective-permute-start | bytes 110600 | tf_op jit(solution)/shard_map/ppermute | solution.py:358
  27.0 4.5 %collective-permute-start.12 = (f32[72,128]{1,0:T(8,128)S(1)}, f32[72,128]{1,0:T(8,128)S(1)}, u32[]{:S(2)}, u32[]{:S(2)}) collective-permute-start(f32[72,128]{1,0:T(8,128)S(1)} %get-tuple-element.42), channel_id=1, source_target_pairs={{0,8},{4,12},{8,0},{12,4},{16,24},{20,28},{24,16},{28,20},{1,9},{5... | collective-permute-start | bytes 110600 | tf_op jit(solution)/shard_map/ppermute | solution.py:358
  28.2 4.0 %collective-permute-start.13 = (f32[72,128]{1,0:T(8,128)S(1)}, f32[72,128]{1,0:T(8,128)S(1)}, u32[]{:S(2)}, u32[]{:S(2)}) collective-permute-start(f32[72,128]{1,0:T(8,128)S(1)} %get-tuple-element.43), channel_id=1, source_target_pairs={{0,4},{4,0},{8,12},{12,8},{16,20},{20,16},{24,28},{28,24},{1,5},{5... | collective-permute-start | bytes 110600 | tf_op jit(solution)/shard_map/ppermute | solution.py:358
  31.0 1.1 %copy-start.2 = (f32[512,128]{1,0:T(8,128)S(1)}, f32[512,128]{1,0:T(8,128)}, u32[]{:S(2)}) copy-start(f32[512,128]{1,0:T(8,128)} %refs_2_.1) | copy-start | bytes 786436
  32.6 2.6 %collective-permute-start.14 = (f32[128,128]{1,0:T(8,128)S(1)}, f32[128,128]{1,0:T(8,128)S(1)}, u32[]{:S(2)}, u32[]{:S(2)}) collective-permute-start(f32[128,128]{1,0:T(8,128)S(1)} %get-tuple-element.45), channel_id=1, source_target_pairs={{0,1},{1,0},{2,3},{3,2},{4,5},{5,4},{6,7},{7,6},{8,9},{9,8},{10,11... | collective-permute-start | bytes 196616 | tf_op jit(solution)/shard_map/ppermute | solution.py:479
  32.7 4.5 %collective-permute-start.15 = (f32[128,128]{1,0:T(8,128)S(1)}, f32[128,128]{1,0:T(8,128)S(1)}, u32[]{:S(2)}, u32[]{:S(2)}) collective-permute-start(f32[128,128]{1,0:T(8,128)S(1)} %get-tuple-element.46), channel_id=1, source_target_pairs={{0,2},{1,3},{2,0},{3,1},{4,6},{5,7},{6,4},{7,5},{8,10},{9,11},{10,... | collective-permute-start | bytes 196616 | tf_op jit(solution)/shard_map/ppermute | solution.py:479
  34.3 4.0 %collective-permute-start.16 = (f32[128,128]{1,0:T(8,128)S(1)}, f32[128,128]{1,0:T(8,128)S(1)}, u32[]{:S(2)}, u32[]{:S(2)}) collective-permute-start(f32[128,128]{1,0:T(8,128)S(1)} %get-tuple-element.47), channel_id=1, source_target_pairs={{0,3},{1,2},{2,1},{3,0},{4,7},{5,6},{6,5},{7,4},{8,11},{9,10},{10,... | collective-permute-start | bytes 196616 | tf_op jit(solution)/shard_map/ppermute | solution.py:479

commit v9 on v8

--- a/solution.py
+++ b/solution.py
@@ -473,10 +473,20 @@
             compiler_params=params([u_owned, v_rows, latent]),
             name="gradient",
         )(plan, v_rows, latent, *returned)
-    gradient = parts[0]
-    for step in range(1, n_row):
-        pairs_of = [(i, i ^ step if paired else (i + step) % n_row) for i in range(n_row)]
-        gradient = gradient + lax.ppermute(parts[step], "row", pairs_of)
+    parts = list(parts)
+    if paired:
+        bit = 1
+        while bit < n_row:
+            pairs_of = [(i, i ^ bit) for i in range(n_row)]
+            kept = [k for k in range(0, n_row, bit) if not k & bit]
+            for k in reversed(kept):
+                parts[k] = parts[k] + lax.ppermute(parts[k | bit], "row", pairs_of)
+            bit *= 2
+        gradient = parts[0]
+    else:
+        gradient = parts[0]
+        for step in range(1, n_row):
+            gradient = gradient + lax.ppermute(parts[step], "row", [(i, (i + step) % n_row) for i in range(n_row)])
     return field[None, None], gradient
 
 

time: 39.1 us -> 39.1 us (level)
  no operation moved by 1% of the time
where the time goes in v9:
time: 39.1 us; the launch traced here: 38.9 us
  starting transfers between devices  24.9 us (64%)
  waiting for transfers between devices  7.91 us (20%)
  Pallas kernels  4.09 us (10%)
  between operations  0.74 us (2%)
  local copies, waits for them, and re-layouts  0.67 us (2%)
  other arithmetic  0.65 us (2%)
    ppermute x14, starting transfers between devices, exchange(): lax.ppermute(arrays[k], 'col', [(i, i ^ k) for i in range(count)])  22.7 us
    ppermute x14, waiting for transfers between devices, exchange(): lax.ppermute(arrays[k], 'col', [(i, i ^ k) for i in range(count)])  5.05 us
    ppermute x3, waiting for transfers between devices, on_device(): parts[k] = parts[k] + lax.ppermute(parts[k | bit], 'row', pairs_of)  2.86 us
    ppermute x3, starting transfers between devices, on_device(): parts[k] = parts[k] + lax.ppermute(parts[k | bit], 'row', pairs_of)  2.13 us
    pallas_call x1, Pallas kernels, on_device(): pl.pallas_call(functools.partial(blocks_kernel, group), out_shape=(*carri...  1.86 us
    pallas_call x1, Pallas kernels, on_device(): pl.pallas_call(put_back(functools.partial(owner_kernel, chunk, rank_pad,...  0.91 us
  transfers between devices with their start and end apart: 17, of which 7 were waited for; matrix products, arithmetic and copies ran while one was open for 2% of the time, Pallas kernels for 2%

profile of v9, /device:TPU:0, one launch (start us, length us, event | category | flops | bytes accessed | tf_op | source)
XLA Modules:
  0.0 38.9 jit_solution(18247512400310651837)
XLA Ops:
  0.6 1.9 %blocks.1 = (f32[80,128]{1,0:T(8,128)S(1)}, f32[80,128]{1,0:T(8,128)S(1)}, f32[80,128]{1,0:T(8,128)S(1)}, f32[80,128]{1,0:T(8,128)S(1)}, f32[80,128]{1,0:T(8,128...) custom-call(s32[1,8]{1,0:T(1,128)} %order_hbm.1, ...), custom_call_target="tpu_custom_call" | custom-call | tf_op jit(solution)/shard_map/blocks/pallas_call | solution.py:389
  2.5 4.1 %collective-permute-start = (f32[80,128]{1,0:T(8,128)S(1)}, f32[80,128]{1,0:T(8,128)S(1)}, u32[]{:S(2)}, u32[]{:S(2)}) collective-permute-start(f32[80,128]{1,0:T(8,128)S(1)} %get-tuple-element.26), channel_id=1, source_target_pairs={{0,16},{4,20},{8,24},{12,28},{16,0},{20,4},{24,8},{28,12},{1,17},{... | collective-permute-start | bytes 122888 | tf_op jit(solution)/shard_map/ppermute | solution.py:358
  6.6 1.4 %collective-permute-start.1 = (f32[80,128]{1,0:T(8,128)S(1)}, f32[80,128]{1,0:T(8,128)S(1)}, u32[]{:S(2)}, u32[]{:S(2)}) collective-permute-start(f32[80,128]{1,0:T(8,128)S(1)} %get-tuple-element.27), channel_id=1, source_target_pairs={{0,24},{4,28},{8,16},{12,20},{16,8},{20,12},{24,0},{28,4},{1,25},{... | collective-permute-start | bytes 122888 | tf_op jit(solution)/shard_map/ppermute | solution.py:358
  8.0 2.6 %collective-permute-start.2 = (f32[80,128]{1,0:T(8,128)S(1)}, f32[80,128]{1,0:T(8,128)S(1)}, u32[]{:S(2)}, u32[]{:S(2)}) collective-permute-start(f32[80,128]{1,0:T(8,128)S(1)} %get-tuple-element.28), channel_id=1, source_target_pairs={{0,20},{4,16},{8,28},{12,24},{16,4},{20,0},{24,12},{28,8},{1,21},{... | collective-permute-start | bytes 122888 | tf_op jit(solution)/shard_map/ppermute | solution.py:358
  10.6 0.8 %collective-permute-start.3 = (f32[80,128]{1,0:T(8,128)S(1)}, f32[80,128]{1,0:T(8,128)S(1)}, u32[]{:S(2)}, u32[]{:S(2)}) collective-permute-start(f32[80,128]{1,0:T(8,128)S(1)} %get-tuple-element.29), channel_id=1, source_target_pairs={{0,28},{4,24},{8,20},{12,16},{16,12},{20,8},{24,4},{28,0},{1,29},{... | collective-permute-start | bytes 122888 | tf_op jit(solution)/shard_map/ppermute | solution.py:358
  11.4 1.9 %collective-permute-start.4 = (f32[80,128]{1,0:T(8,128)S(1)}, f32[80,128]{1,0:T(8,128)S(1)}, u32[]{:S(2)}, u32[]{:S(2)}) collective-permute-start(f32[80,128]{1,0:T(8,128)S(1)} %get-tuple-element.31), channel_id=1, source_target_pairs={{0,12},{4,8},{8,4},{12,0},{16,28},{20,24},{24,20},{28,16},{1,13},{... | collective-permute-start | bytes 122888 | tf_op jit(solution)/shard_map/ppermute | solution.py:358
  13.3 1.1 %collective-permute-start.5 = (f32[80,128]{1,0:T(8,128)S(1)}, f32[80,128]{1,0:T(8,128)S(1)}, u32[]{:S(2)}, u32[]{:S(2)}) collective-permute-start(f32[80,128]{1,0:T(8,128)S(1)} %get-tuple-element.32), channel_id=1, source_target_pairs={{0,8},{4,12},{8,0},{12,4},{16,24},{20,28},{24,16},{28,20},{1,9},{5... | collective-permute-start | bytes 122888 | tf_op jit(solution)/shard_map/ppermute | solution.py:358
  14.4 0.5 %collective-permute-start.6 = (f32[80,128]{1,0:T(8,128)S(1)}, f32[80,128]{1,0:T(8,128)S(1)}, u32[]{:S(2)}, u32[]{:S(2)}) collective-permute-start(f32[80,128]{1,0:T(8,128)S(1)} %get-tuple-element.33), channel_id=1, source_target_pairs={{0,4},{4,0},{8,12},{12,8},{16,20},{20,16},{24,28},{28,24},{1,5},{5... | collective-permute-start | bytes 122888 | tf_op jit(solution)/shard_map/ppermute | solution.py:358
  14.9 0.6 %collective-permute-done.2.refs_3_.refs_6_ = f32[80,128]{1,0:T(8,128)S(1)} collective-permute-done((f32[80,128]{1,0:T(8,128)S(1)}, f32[80,128]{1,0:T(8,128)S(1)}, u32[]{:S(2)}, u32[]{:S(2)}) %collective-permute-start.2) | collective-permute-done | bytes 40992 | tf_op jit(solution)/shard_map/ppermute | solution.py:358
  15.5 1.9 %collective-permute-done.3.refs_4_.refs_7_ = f32[80,128]{1,0:T(8,128)S(1)} collective-permute-done((f32[80,128]{1,0:T(8,128)S(1)}, f32[80,128]{1,0:T(8,128)S(1)}, u32[]{:S(2)}, u32[]{:S(2)}) %collective-permute-start.3) | collective-permute-done | bytes 40992 | tf_op jit(solution)/shard_map/ppermute | solution.py:358
  17.4 0.4 owner_far.1.refs_3_
  17.8 0.0 copy-start
  17.8 0.6 %collective-permute-done.6.refs_11_ = f32[80,128]{1,0:T(8,128)S(1)} collective-permute-done((f32[80,128]{1,0:T(8,128)S(1)}, f32[80,128]{1,0:T(8,128)S(1)}, u32[]{:S(2)}, u32[]{:S(2)}) %collective-permute-start.6) | collective-permute-done | bytes 40992 | tf_op jit(solution)/shard_map/ppermute | solution.py:358
  18.4 0.9 %owner.1 = (f32[256,128]{1,0:T(8,128)S(1)}, f32[72,128]{1,0:T(8,128)S(1)}, f32[72,128]{1,0:T(8,128)S(1)}, f32[72,128]{1,0:T(8,128)S(1)}, f32[72,128]{1,0:T(8,128...) custom-call(s32[1,64]{1,0:T(1,128)S(1)} %get-tuple-element.25.refs_0_, ...), custom_call_target="tpu_custom_call" | custom-call | tf_op jit(solution)/shard_map/owner/pallas_call | solution.py:428
  19.4 2.0 %collective-permute-start.7 = (f32[72,128]{1,0:T(8,128)S(1)}, f32[72,128]{1,0:T(8,128)S(1)}, u32[]{:S(2)}, u32[]{:S(2)}) collective-permute-start(f32[72,128]{1,0:T(8,128)S(1)} %get-tuple-element.36), channel_id=1, source_target_pairs={{0,16},{4,20},{8,24},{12,28},{16,0},{20,4},{24,8},{28,12},{1,17},{... | collective-permute-start | bytes 110600 | tf_op jit(solution)/shard_map/ppermute | solution.py:358
  21.3 1.4 %collective-permute-start.8 = (f32[72,128]{1,0:T(8,128)S(1)}, f32[72,128]{1,0:T(8,128)S(1)}, u32[]{:S(2)}, u32[]{:S(2)}) collective-permute-start(f32[72,128]{1,0:T(8,128)S(1)} %get-tuple-element.37), channel_id=1, source_target_pairs={{0,24},{4,28},{8,16},{12,20},{16,8},{20,12},{24,0},{28,4},{1,25},{... | collective-permute-start | bytes 110600 | tf_op jit(solution)/shard_map/ppermute | solution.py:358
  22.7 1.6 %collective-permute-start.9 = (f32[72,128]{1,0:T(8,128)S(1)}, f32[72,128]{1,0:T(8,128)S(1)}, u32[]{:S(2)}, u32[]{:S(2)}) collective-permute-start(f32[72,128]{1,0:T(8,128)S(1)} %get-tuple-element.38), channel_id=1, source_target_pairs={{0,20},{4,16},{8,28},{12,24},{16,4},{20,0},{24,12},{28,8},{1,21},{... | collective-permute-start | bytes 110600 | tf_op jit(solution)/shard_map/ppermute | solution.py:358
  24.3 1.9 %collective-permute-start.10 = (f32[72,128]{1,0:T(8,128)S(1)}, f32[72,128]{1,0:T(8,128)S(1)}, u32[]{:S(2)}, u32[]{:S(2)}) collective-permute-start(f32[72,128]{1,0:T(8,128)S(1)} %get-tuple-element.39), channel_id=1, source_target_pairs={{0,28},{4,24},{8,20},{12,16},{16,12},{20,8},{24,4},{28,0},{1,29},{... | collective-permute-start | bytes 110600 | tf_op jit(solution)/shard_map/ppermute | solution.py:358
  26.2 0.8 %collective-permute-start.11 = (f32[72,128]{1,0:T(8,128)S(1)}, f32[72,128]{1,0:T(8,128)S(1)}, u32[]{:S(2)}, u32[]{:S(2)}) collective-permute-start(f32[72,128]{1,0:T(8,128)S(1)} %get-tuple-element.41), channel_id=1, source_target_pairs={{0,12},{4,8},{8,4},{12,0},{16,28},{20,24},{24,20},{28,16},{1,13},{... | collective-permute-start | bytes 110600 | tf_op jit(solution)/shard_map/ppermute | solution.py:358
  27.0 1.1 %collective-permute-start.12 = (f32[72,128]{1,0:T(8,128)S(1)}, f32[72,128]{1,0:T(8,128)S(1)}, u32[]{:S(2)}, u32[]{:S(2)}) collective-permute-start(f32[72,128]{1,0:T(8,128)S(1)} %get-tuple-element.42), channel_id=1, source_target_pairs={{0,8},{4,12},{8,0},{12,4},{16,24},{20,28},{24,16},{28,20},{1,9},{5... | collective-permute-start | bytes 110600 | tf_op jit(solution)/shard_map/ppermute | solution.py:358
  28.2 1.5 %collective-permute-start.13 = (f32[72,128]{1,0:T(8,128)S(1)}, f32[72,128]{1,0:T(8,128)S(1)}, u32[]{:S(2)}, u32[]{:S(2)}) collective-permute-start(f32[72,128]{1,0:T(8,128)S(1)} %get-tuple-element.43), channel_id=1, source_target_pairs={{0,4},{4,0},{8,12},{12,8},{16,20},{20,16},{24,28},{28,24},{1,5},{5... | collective-permute-start | bytes 110600 | tf_op jit(solution)/shard_map/ppermute | solution.py:358
  29.7 1.3 %collective-permute-done.10.refs_5_ = f32[72,128]{1,0:T(8,128)S(1)} collective-permute-done((f32[72,128]{1,0:T(8,128)S(1)}, f32[72,128]{1,0:T(8,128)S(1)}, u32[]{:S(2)}, u32[]{:S(2)}) %collective-permute-start.10) | collective-permute-done | bytes 36896 | tf_op jit(solution)/shard_map/ppermute | solution.py:358
  31.0 0.5 %gradient_far.1.refs_3_ = f32[512,128]{1,0:T(8,128)S(1)} custom-call(s32[8,128]{1,0:T(8,128)S(1)} %get-tuple-element.35.refs_0_, f32[8,2,48,256]{3,2,1,0:T(8,128)S(1)} %bitcast.10, f32[72,128]{1,0:T(8,128)S(1)} %collective-permute-done.7.refs_2_, f32[72,128]{1,0:T(8,128)S(1)} %collective-permute-done.8.refs_3_, ...), custom_call_target="tpu_custom_call" | custom-call | flops 75497472 | bytes 786432 | tf_op jit(solution)/shard_map/gradient_far/pallas_call | solution.py:447
  31.5 0.6 %collective-permute-done.13.refs_7_ = f32[72,128]{1,0:T(8,128)S(1)} collective-permute-done((f32[72,128]{1,0:T(8,128)S(1)}, f32[72,128]{1,0:T(8,128)S(1)}, u32[]{:S(2)}, u32[]{:S(2)}) %collective-permute-start.13) | collective-permute-done | bytes 36896 | tf_op jit(solution)/shard_map/ppermute | solution.py:358
  32.1 0.5 %gradient.1 = (f32[128,128]{1,0:T(8,128)S(1)}, f32[128,128]{1,0:T(8,128)S(1)}, f32[128,128]{1,0:T(8,128)S(1)}, f32[128,128]{1,0:T(8,128)S(1)}) custom-call(s32[8,128]{1,0:T(8,128)S(1)} %get-tuple-element.35.refs_0_, f32[8,2,48,256]{3,2,1,0:T(8,128)S(1)} %bitcast.11, f32[512,128]{1,0:T(8,128)S(1)} %copy-done.2, f32[512,128]{1,0:T(8,128)S(1)} %gradient_far.1.refs_3_, ...), custom_call_target="tpu_custom_call" | custom-call | tf_op jit(solution)/shard_map/gradient/pallas_call | solution.py:457
  32.6 0.1 collective-permute-start.15
  32.7 0.5 %collective-permute-start.14 = (f32[128,128]{1,0:T(8,128)S(1)}, f32[128,128]{1,0:T(8,128)S(1)}, u32[]{:S(2)}, u32[]{:S(2)}) collective-permute-start(f32[128,128]{1,0:T(8,128)S(1)} %get-tuple-element.45), channel_id=1, source_target_pairs={{0,1},{1,0},{2,3},{3,2},{4,5},{5,4},{6,7},{7,6},{8,9},{9,8},{10,11... | collective-permute-start | bytes 196616 | tf_op jit(solution)/shard_map/ppermute | solution.py:483
  33.2 0.7 %collective-permute-done.15 = f32[128,128]{1,0:T(8,128)S(1)} collective-permute-done((f32[128,128]{1,0:T(8,128)S(1)}, f32[128,128]{1,0:T(8,128)S(1)}, u32[]{:S(2)}, u32[]{:S(2)}) %collective-permute-start.15) | collective-permute-done | bytes 65568 | tf_op jit(solution)/shard_map/ppermute | solution.py:483
  34.0 1.6 %collective-permute-start.16 = (f32[128,128]{1,0:T(8,128)S(1)}, f32[128,128]{1,0:T(8,128)S(1)}, u32[]{:S(2)}, u32[]{:S(2)}) collective-permute-start(f32[128,128]{1,0:T(8,128)S(1)} %add.10), channel_id=1, source_target_pairs={{0,2},{1,3},{2,0},{3,1},{4,6},{5,7},{6,4},{7,5},{8,10},{9,11},{10,... | collective-permute-start | bytes 196616 | tf_op jit(solution)/shard_map/ppermute | solution.py:483
  35.5 0.7 %copy.9 = f32[1,1,256,128]{3,2,1,0:T(8,128)} copy(f32[1,1,256,128]{3,2,1,0:T(8,128)S(1)} %bitcast.8) | data formatting | bytes 262144
  36.2 2.1 %collective-permute-done.16 = f32[128,128]{1,0:T(8,128)S(1)} collective-permute-done((f32[128,128]{1,0:T(8,128)S(1)}, f32[128,128]{1,0:T(8,128)S(1)}, u32[]{:S(2)}, u32[]{:S(2)}) %collective-permute-start.16) | collective-permute-done | bytes 65568 | tf_op jit(solution)/shard_map/ppermute | solution.py:483
  38.3 0.6 %add_add_fusion = f32[128,128]{1,0:T(8,128)} fusion(f32[128,128]{1,0:T(8,128)S(1)} %collective-permute-done.16, f32[128,128]{1,0:T(8,128)S(1)} %get-tuple-element.44, f32[128,128]{1,0:T(8,128)S(1)} %collective-permute-done.14), kind=kLoop, calls=%fused_computation | loop fusion | flops 32768 | bytes 262144 | tf_op jit(solution)/shard_map/add | solution.py:483
  (18 shorter events, 0.0 us)
Async XLA Ops:
  0.6 16.8 %copy-start.1 = (f32[1,1,256,768]{3,2,1,0:T(8,128)S(1)}, f32[1,1,256,768]{3,2,1,0:T(8,128)}, u32[]{:S(2)}) copy-start(f32[1,1,256,768]{3,2,1,0:T(8,128)} %param.9) | copy-start | bytes 2359300
  2.5 10.8 %collective-permute-start = (f32[80,128]{1,0:T(8,128)S(1)}, f32[80,128]{1,0:T(8,128)S(1)}, u32[]{:S(2)}, u32[]{:S(2)}) collective-permute-start(f32[80,128]{1,0:T(8,128)S(1)} %get-tuple-element.26), channel_id=1, source_target_pairs={{0,16},{4,20},{8,24},{12,28},{16,0},{20,4},{24,8},{28,12},{1,17},{... | collective-permute-start | bytes 122888 | tf_op jit(solution)/shard_map/ppermute | solution.py:358
  6.6 7.8 %collective-permute-start.1 = (f32[80,128]{1,0:T(8,128)S(1)}, f32[80,128]{1,0:T(8,128)S(1)}, u32[]{:S(2)}, u32[]{:S(2)}) collective-permute-start(f32[80,128]{1,0:T(8,128)S(1)} %get-tuple-element.27), channel_id=1, source_target_pairs={{0,24},{4,28},{8,16},{12,20},{16,8},{20,12},{24,0},{28,4},{1,25},{... | collective-permute-start | bytes 122888 | tf_op jit(solution)/shard_map/ppermute | solution.py:358
  8.0 7.6 %collective-permute-start.2 = (f32[80,128]{1,0:T(8,128)S(1)}, f32[80,128]{1,0:T(8,128)S(1)}, u32[]{:S(2)}, u32[]{:S(2)}) collective-permute-start(f32[80,128]{1,0:T(8,128)S(1)} %get-tuple-element.28), channel_id=1, source_target_pairs={{0,20},{4,16},{8,28},{12,24},{16,4},{20,0},{24,12},{28,8},{1,21},{... | collective-permute-start | bytes 122888 | tf_op jit(solution)/shard_map/ppermute | solution.py:358
  10.6 6.8 %collective-permute-start.3 = (f32[80,128]{1,0:T(8,128)S(1)}, f32[80,128]{1,0:T(8,128)S(1)}, u32[]{:S(2)}, u32[]{:S(2)}) collective-permute-start(f32[80,128]{1,0:T(8,128)S(1)} %get-tuple-element.29), channel_id=1, source_target_pairs={{0,28},{4,24},{8,20},{12,16},{16,12},{20,8},{24,4},{28,0},{1,29},{... | collective-permute-start | bytes 122888 | tf_op jit(solution)/shard_map/ppermute | solution.py:358
  11.4 6.4 %collective-permute-start.4 = (f32[80,128]{1,0:T(8,128)S(1)}, f32[80,128]{1,0:T(8,128)S(1)}, u32[]{:S(2)}, u32[]{:S(2)}) collective-permute-start(f32[80,128]{1,0:T(8,128)S(1)} %get-tuple-element.31), channel_id=1, source_target_pairs={{0,12},{4,8},{8,4},{12,0},{16,28},{20,24},{24,20},{28,16},{1,13},{... | collective-permute-start | bytes 122888 | tf_op jit(solution)/shard_map/ppermute | solution.py:358
  13.3 4.5 %collective-permute-start.5 = (f32[80,128]{1,0:T(8,128)S(1)}, f32[80,128]{1,0:T(8,128)S(1)}, u32[]{:S(2)}, u32[]{:S(2)}) collective-permute-start(f32[80,128]{1,0:T(8,128)S(1)} %get-tuple-element.32), channel_id=1, source_target_pairs={{0,8},{4,12},{8,0},{12,4},{16,24},{20,28},{24,16},{28,20},{1,9},{5... | collective-permute-start | bytes 122888 | tf_op jit(solution)/shard_map/ppermute | solution.py:358
  14.4 4.0 %collective-permute-start.6 = (f32[80,128]{1,0:T(8,128)S(1)}, f32[80,128]{1,0:T(8,128)S(1)}, u32[]{:S(2)}, u32[]{:S(2)}) collective-permute-start(f32[80,128]{1,0:T(8,128)S(1)} %get-tuple-element.33), channel_id=1, source_target_pairs={{0,4},{4,0},{8,12},{12,8},{16,20},{20,16},{24,28},{28,24},{1,5},{5... | collective-permute-start | bytes 122888 | tf_op jit(solution)/shard_map/ppermute | solution.py:358
  17.4 1.0 %copy-start.3 = (f32[1,1,64,128]{3,2,1,0:T(8,128)S(1)}, f32[1,1,64,128]{3,2,1,0:T(8,128)}, u32[]{:S(2)}) copy-start(f32[1,1,64,128]{3,2,1,0:T(8,128)} %param.13) | copy-start | bytes 98308
  17.8 13.2 %copy-start = (f32[8,1,2,48,256]{4,3,2,1,0:T(8,128)S(1)}, f32[8,1,2,48,256]{4,3,2,1,0:T(8,128)}, u32[]{:S(2)}) copy-start(f32[8,1,2,48,256]{4,3,2,1,0:T(8,128)} %param.8) | copy-start | bytes 2359300
  19.4 7.7 %collective-permute-start.7 = (f32[72,128]{1,0:T(8,128)S(1)}, f32[72,128]{1,0:T(8,128)S(1)}, u32[]{:S(2)}, u32[]{:S(2)}) collective-permute-start(f32[72,128]{1,0:T(8,128)S(1)} %get-tuple-element.36), channel_id=1, source_target_pairs={{0,16},{4,20},{8,24},{12,28},{16,0},{20,4},{24,8},{28,12},{1,17},{... | collective-permute-start | bytes 110600 | tf_op jit(solution)/shard_map/ppermute | solution.py:358
  21.3 6.8 %collective-permute-start.8 = (f32[72,128]{1,0:T(8,128)S(1)}, f32[72,128]{1,0:T(8,128)S(1)}, u32[]{:S(2)}, u32[]{:S(2)}) collective-permute-start(f32[72,128]{1,0:T(8,128)S(1)} %get-tuple-element.37), channel_id=1, source_target_pairs={{0,24},{4,28},{8,16},{12,20},{16,8},{20,12},{24,0},{28,4},{1,25},{... | collective-permute-start | bytes 110600 | tf_op jit(solution)/shard_map/ppermute | solution.py:358
  22.7 7.0 %collective-permute-start.9 = (f32[72,128]{1,0:T(8,128)S(1)}, f32[72,128]{1,0:T(8,128)S(1)}, u32[]{:S(2)}, u32[]{:S(2)}) collective-permute-start(f32[72,128]{1,0:T(8,128)S(1)} %get-tuple-element.38), channel_id=1, source_target_pairs={{0,20},{4,16},{8,28},{12,24},{16,4},{20,0},{24,12},{28,8},{1,21},{... | collective-permute-start | bytes 110600 | tf_op jit(solution)/shard_map/ppermute | solution.py:358
  24.3 6.7 %collective-permute-start.10 = (f32[72,128]{1,0:T(8,128)S(1)}, f32[72,128]{1,0:T(8,128)S(1)}, u32[]{:S(2)}, u32[]{:S(2)}) collective-permute-start(f32[72,128]{1,0:T(8,128)S(1)} %get-tuple-element.39), channel_id=1, source_target_pairs={{0,28},{4,24},{8,20},{12,16},{16,12},{20,8},{24,4},{28,0},{1,29},{... | collective-permute-start | bytes 110600 | tf_op jit(solution)/shard_map/ppermute | solution.py:358
  26.2 5.3 %collective-permute-start.11 = (f32[72,128]{1,0:T(8,128)S(1)}, f32[72,128]{1,0:T(8,128)S(1)}, u32[]{:S(2)}, u32[]{:S(2)}) collective-permute-start(f32[72,128]{1,0:T(8,128)S(1)} %get-tuple-element.41), channel_id=1, source_target_pairs={{0,12},{4,8},{8,4},{12,0},{16,28},{20,24},{24,20},{28,16},{1,13},{... | collective-permute-start | bytes 110600 | tf_op jit(solution)/shard_map/ppermute | solution.py:358
  27.0 4.5 %collective-permute-start.12 = (f32[72,128]{1,0:T(8,128)S(1)}, f32[72,128]{1,0:T(8,128)S(1)}, u32[]{:S(2)}, u32[]{:S(2)}) collective-permute-start(f32[72,128]{1,0:T(8,128)S(1)} %get-tuple-element.42), channel_id=1, source_target_pairs={{0,8},{4,12},{8,0},{12,4},{16,24},{20,28},{24,16},{28,20},{1,9},{5... | collective-permute-start | bytes 110600 | tf_op jit(solution)/shard_map/ppermute | solution.py:358
  28.2 4.0 %collective-permute-start.13 = (f32[72,128]{1,0:T(8,128)S(1)}, f32[72,128]{1,0:T(8,128)S(1)}, u32[]{:S(2)}, u32[]{:S(2)}) collective-permute-start(f32[72,128]{1,0:T(8,128)S(1)} %get-tuple-element.43), channel_id=1, source_target_pairs={{0,4},{4,0},{8,12},{12,8},{16,20},{20,16},{24,28},{28,24},{1,5},{5... | collective-permute-start | bytes 110600 | tf_op jit(solution)/shard_map/ppermute | solution.py:358
  31.0 1.1 %copy-start.2 = (f32[512,128]{1,0:T(8,128)S(1)}, f32[512,128]{1,0:T(8,128)}, u32[]{:S(2)}) copy-start(f32[512,128]{1,0:T(8,128)} %refs_2_.1) | copy-start | bytes 786436
  32.6 1.3 %collective-permute-start.15 = (f32[128,128]{1,0:T(8,128)S(1)}, f32[128,128]{1,0:T(8,128)S(1)}, u32[]{:S(2)}, u32[]{:S(2)}) collective-permute-start(f32[128,128]{1,0:T(8,128)S(1)} %get-tuple-element.47), channel_id=1, source_target_pairs={{0,1},{1,0},{2,3},{3,2},{4,5},{5,4},{6,7},{7,6},{8,9},{9,8},{10,11... | collective-permute-start | bytes 196616 | tf_op jit(solution)/shard_map/ppermute | solution.py:483
  32.7 3.5 %collective-permute-start.14 = (f32[128,128]{1,0:T(8,128)S(1)}, f32[128,128]{1,0:T(8,128)S(1)}, u32[]{:S(2)}, u32[]{:S(2)}) collective-permute-start(f32[128,128]{1,0:T(8,128)S(1)} %get-tuple-element.45), channel_id=1, source_target_pairs={{0,1},{1,0},{2,3},{3,2},{4,5},{5,4},{6,7},{7,6},{8,9},{9,8},{10,11... | collective-permute-start | bytes 196616 | tf_op jit(solution)/shard_map/ppermute | solution.py:483
  34.0 4.3 %collective-permute-start.16 = (f32[128,128]{1,0:T(8,128)S(1)}, f32[128,128]{1,0:T(8,128)S(1)}, u32[]{:S(2)}, u32[]{:S(2)}) collective-permute-start(f32[128,128]{1,0:T(8,128)S(1)} %add.10), channel_id=1, source_target_pairs={{0,2},{1,3},{2,0},{3,1},{4,6},{5,7},{6,4},{7,5},{8,10},{9,11},{10,... | collective-permute-start | bytes 196616 | tf_op jit(solution)/shard_map/ppermute | solution.py:483
